TPU v7x, 32 devices: a whole 2x2x4 slice. The times are simulated.
32 devices in a mesh: track: 8 (over z, x), tm: 4 (over y, core).
Axes of the slice: x: 2, y: 2, z: 4, core: 2. Of those that a mesh axis runs over, the one named last changes fastest.
Arguments:
- positions: float32 [3, 8, 3072], P(None, 'tm', 'track'), may hold values from -6 to 6
- embeddings: float32 [8, 128, 3072], P('tm', None, 'track'), may hold values from -6 to 6
- visible: int32 [8, 3072], P('tm', 'track'), may hold values 0 or 1
Outputs:
- grad_positions: float32 [3, 8, 3072], P(None, 'tm', 'track')
- grad_embeddings: float32 [8, 128, 3072], P('tm', None, 'track')
- mean_loss: float32 [], replicated
All inputs are finite; a program needn't handle non-finite values. No bound on the sum of `visible` on one device may be relied on, other than what follows from the above.
Results may differ from a plain program's by a relative error of at most 0.00014.
Values sent between devices are 32-bit elements; how exact they have to be, the bound alone decides.
No kernel may reach another device: no remote copies, remote signals or barrier semaphores. Data moves between devices by JAX's collectives and lax.ppermute only.
A program may use at most 128 MiB of HBM per device.

v0:
```python
import math

import jax
import jax.numpy as jnp
from jax import lax
from jax.sharding import PartitionSpec as P

rigidity = 4.0
highest = lax.Precision.HIGHEST


def shifted(array, axis, by):
    size = lax.axis_size(axis)
    pairs = [(i, i + by) for i in range(size) if 0 <= i + by < size]
    return lax.ppermute(array, axis, pairs)


def shifted_2(value, axis, steps):
    count = lax.axis_size(axis)
    pairs = [(source, (source + steps) % count) for source in range(count)]
    return lax.ppermute(value, axis, pairs)


def tile_terms(pos_a, mask_a, emb_a, pos_b, mask_b, emb_b, weight_scale):
    inv_root = 1.0 / math.sqrt(emb_a.shape[1])
    offset = pos_a[:, :, :, None] - pos_b[:, :, None, :]
    distance = jnp.sqrt(jnp.sum(offset * offset, axis=0) + 1.0)
    change = distance[1:] - distance[:-1]
    both_seen = mask_a[:, :, None] * mask_b[:, None, :]
    seen_pair = both_seen[1:] * both_seen[:-1]
    logits = jnp.einsum("fei,fej->fij", emb_a, emb_b, precision=highest) * inv_root
    affinity = jax.nn.sigmoid(logits)
    squared = seen_pair * change * change
    energy = jnp.sum(affinity * squared)
    grad_change = 2.0 * weight_scale * affinity * seen_pair * change
    padding = jnp.zeros_like(grad_change[:1])
    grad_dist = jnp.concatenate([padding, grad_change], 0) - jnp.concatenate(
        [grad_change, padding], 0
    )
    scaled = (grad_dist / distance)[None] * offset
    grad_pos_a = jnp.sum(scaled, axis=3)
    grad_pos_b = -jnp.sum(scaled, axis=2)
    grad_logit = weight_scale * squared * affinity * (1.0 - affinity) * inv_root
    grad_emb_a = jnp.einsum("fij,fej->fei", grad_logit, emb_b, precision=highest)
    grad_emb_b = jnp.einsum("fij,fei->fej", grad_logit, emb_a, precision=highest)
    return (energy, grad_pos_a, grad_emb_a, grad_pos_b, grad_emb_b)


def on_device(positions, embeddings, visible):
    frames_local = embeddings.shape[0]
    block_width = embeddings.shape[2]
    tracks = block_width * lax.axis_size("track")
    frames = frames_local * lax.axis_size("tm")
    weight_scale = rigidity / math.sqrt(tracks)
    seen_mask = visible.astype(jnp.float32)
    next_pos, next_mask = shifted((positions[:, :1], seen_mask[:1]), "tm", -1)
    pos_ext = jnp.concatenate([positions, next_pos], 1)
    mask_ext = jnp.concatenate([seen_mask, next_mask], 0)
    packed = jnp.concatenate([pos_ext, mask_ext[None]], 0)

    def own_tile(others_packed, others_emb):
        return tile_terms(
            pos_ext,
            mask_ext,
            embeddings,
            others_packed[:3],
            others_packed[3],
            others_emb,
            weight_scale,
        )

    midway = lax.axis_size("track") // 2
    energy, grad_pos, grad_emb, unused_pos, unused_emb = own_tile(packed, embeddings)
    energy_sum = 0.5 * energy
    visiting = (packed, embeddings)
    for offset_step in range(1, midway + 1):
        visiting = shifted_2((visiting[0], visiting[1]), "track", 1)
        energy, grad_pos_a, grad_emb_a, grad_pos_b, grad_emb_b = own_tile(visiting[0], visiting[1])
        grad_pos = grad_pos + grad_pos_a
        grad_emb = grad_emb + grad_emb_a
        if offset_step < midway:
            energy_sum = energy_sum + energy
            returned = shifted_2((grad_pos_b, grad_emb_b), "track", -offset_step)
            grad_pos = grad_pos + returned[0]
            grad_emb = grad_emb + returned[1]
        else:
            energy_sum = energy_sum + 0.5 * energy
    incoming = shifted(grad_pos[:, -1:], "tm", 1)
    grad_positions = grad_pos[:, :-1]
    grad_positions = jnp.concatenate([grad_positions[:, :1] + incoming, grad_positions[:, 1:]], 1)
    total = lax.psum(energy_sum, ("track", "tm"))
    mean_loss = total / (tracks * (tracks - 1) / 2.0 * (frames - 1))
    return (grad_positions, grad_emb, mean_loss)


def solution(mesh):
    in_specs = (P(None, "tm", "track"), P("tm", None, "track"), P("tm", "track"))
    out_specs = (P(None, "tm", "track"), P("tm", None, "track"), P())
    return jax.shard_map(
        on_device, mesh=mesh, in_specs=in_specs, out_specs=out_specs, check_vma=False
    )
```

profile of v0, /device:TPU:1, one launch (start us, length us, event | category | flops | bytes accessed | tf_op | source)
XLA Modules:
  0.0 206.6 jit_solution(9600125651648879)
XLA Ops:
  1.3 2.0 collective-permute-start
  4.0 1.9 collective-permute-start.1
  5.9 2.7 %collective-permute-start.2 = (f32[2,128,384]{2,1,0:T(8,128)}, f32[2,128,384]{2,1,0:T(8,128)}, u32[]{:S(2)}, u32[]{:S(2)}) collective-permute-start(f32[2,128,384]{2,1,0:T(8,128)} %param.4), channel_id=1, source_target_pairs={{0,4},{4,8},{8,12},{12,16},{16,20},{20,24},{24,28},{28,0},{1,5},{5... | collective-permute-start | bytes 1179656 | tf_op jit(solution)/shard_map/ppermute | solution.py:21
  8.6 1.1 collective-permute-done.1
  10.5 2.3 %collective-permute-start.3 = (f32[4,3,384]{2,1,0:T(4,128)S(1)}, f32[4,3,384]{2,1,0:T(4,128)S(1)}, u32[]{:S(2)}, u32[]{:S(2)}) collective-permute-start(f32[4,3,384]{2,1,0:T(4,128)S(1)} %pad_maximum_fusion), channel_id=1, source_target_pairs={{0,4},{4,8},{8,12},{12,16},{16,20},{20,24},{24,28},{28,0},{1,5},{5... | collective-permute-start | bytes 55304 | tf_op jit(solution)/shard_map/ppermute | solution.py:21
  13.5 7.3 %collective-permute-done.3 = f32[4,3,384]{2,1,0:T(4,128)S(1)} collective-permute-done((f32[4,3,384]{2,1,0:T(4,128)S(1)}, f32[4,3,384]{2,1,0:T(4,128)S(1)}, u32[]{:S(2)}, u32[]{:S(2)}) %collective-permute-start.3) | collective-permute-done | bytes 18464 | tf_op jit(solution)/shard_map/ppermute | solution.py:21
  20.7 1.5 fusion.6
  22.8 1.7 add_sqrt_fusion.3
  24.4 5.8 %collective-permute-done.6 = f32[4,3,384]{2,1,0:T(4,128)S(1)} collective-permute-done((f32[4,3,384]{2,1,0:T(4,128)S(1)}, f32[4,3,384]{2,1,0:T(4,128)S(1)}, u32[]{:S(2)}, u32[]{:S(2)}) %collective-permute-start.6) | collective-permute-done | bytes 18464 | tf_op jit(solution)/shard_map/ppermute | solution.py:21
  30.9 4.8 %collective-permute-done.9 = f32[4,3,384]{2,1,0:T(4,128)S(1)} collective-permute-done((f32[4,3,384]{2,1,0:T(4,128)S(1)}, f32[4,3,384]{2,1,0:T(4,128)S(1)}, u32[]{:S(2)}, u32[]{:S(2)}) %collective-permute-start.9) | collective-permute-done | bytes 18464 | tf_op jit(solution)/shard_map/ppermute | solution.py:21
  36.2 4.8 %collective-permute-done.12 = f32[4,3,384]{2,1,0:T(4,128)S(1)} collective-permute-done((f32[4,3,384]{2,1,0:T(4,128)S(1)}, f32[4,3,384]{2,1,0:T(4,128)S(1)}, u32[]{:S(2)}, u32[]{:S(2)}) %collective-permute-start.12) | collective-permute-done | bytes 18464 | tf_op jit(solution)/shard_map/ppermute | solution.py:21
  41.6 3.6 %broadcast_multiply_fusion.1 = (f32[3,384,384]{2,1,0:T(8,128)}, f32[3,384,384]{2,1,0:T(8,128)}, f32[3,384,384]{2,1,0:T(8,128)}, f32[3,384,384]{2,1,0:T(8,128)S(1)}, f32[3,384,384]{2,1,0:T(8,128)}) fusion(f32[3,384]{1,0:T(4,128)S(1)} %slice_bitcast_fusion.1, f32[3,384]{1,0:T(4,128)S(1)} %get-tuple-element.44, f32[3,384]{1,0:T(4,128)S(1)} %slice_bitcast_fusion, ...), kind=kLoop, calls=%fused_computation.112 | loop fusion | flops 2211840 | bytes 8870400 | tf_op jit(solution)/shard_map/mul | solution.py:29
  45.2 3.3 %multiply_reduce_fusion.4 = (f32[]{:T(128)}, f32[2,384,384]{2,1,0:T(8,128)}, f32[2,384,384]{2,1,0:T(8,128)S(1)}) fusion(f32[3,384,384]{2,1,0:T(8,128)S(1)} %get-tuple-element.42, f32[3,384,384]{2,1,0:T(8,128)S(1)} %add_sqrt_fusion.4, f32[2,128,384]{2,1,0:T(8,128)S(1)} %copy-done.2), kind=kOutput, calls=%fused_computation.91 | convolution fusion | flops 456818688 | bytes 7864324 | tf_op jit(solution)/shard_map/fei,fej->fij/dot_general | solution.py:31
  48.5 2.3 %fusion.45 = f32[2,384,128]{2,1,0:T(8,128)} fusion(f32[2,128,384]{2,1,0:T(8,128)S(1)} %copy-done.2, f32[2,384,384]{2,1,0:T(8,128)S(1)} %get-tuple-element.46, f32[3,384,384]{2,1,0:T(8,128)S(1)} %get-tuple-element.42, f32[3,384,384]{2,1,0:T(8,128)S(1)} %add_sqrt_fusion.4), kind=kOutput, calls=%fused_computation.100 | convolution fusion | flops 455639040 | bytes 6684672 | tf_op jit(solution)/shard_map/fij,fej->fei/dot_general | solution.py:44
  52.2 2.4 %subtract_divide_fusion.4 = f32[3,384,384]{2,1,0:T(8,128)S(1)} fusion(f32[2,384,384]{2,1,0:T(8,128)} %get-tuple-element.36, f32[3,384,384]{2,1,0:T(8,128)S(1)} %get-tuple-element.19), kind=kLoop, calls=%fused_computation.31 | loop fusion | flops 1327104 | bytes 4718592 | tf_op jit(solution)/shard_map/div | solution.py:40
  55.0 3.5 %multiply_reduce_fusion.3 = (f32[]{:T(128)}, f32[2,384,384]{2,1,0:T(8,128)S(1)}, f32[2,384,384]{2,1,0:T(8,128)S(1)}) fusion(f32[3,384,384]{2,1,0:T(8,128)S(1)} %copy-done.21, f32[3,384,384]{2,1,0:T(8,128)S(1)} %copy-done.17, f32[2,128,384]{2,1,0:T(8,128)S(1)} %copy-done.3, f32[2,128,384]{2,1,0:T(8,128)} %collective-permute-done.2), kind=kOutput, calls=%fused_computation.90 | convolution fusion | flops 458293248 | bytes 7864324 | tf_op jit(solution)/shard_map/fei,fej->fij/dot_general | solution.py:31
  59.6 2.9 %convolution_bitcast_fusion.5 = f32[2,128,384]{1,2,0:T(8,128)} fusion(f32[2,384,384]{2,1,0:T(8,128)S(1)} %get-tuple-element.33, f32[2,128,384]{2,1,0:T(8,128)S(1)} %copy-done.3), kind=kOutput, calls=%fused_computation.68 | convolution fusion | flops 452984832 | bytes 1966080 | tf_op jit(solution)/shard_map/fij,fei->fej/dot_general | solution.py:45
  62.5 4.5 %fusion.1 = (f32[3,3,384]{2,1,0:T(4,128)}, f32[3,3,384]{2,1,0:T(4,128)S(1)}, f32[3,384,384]{2,1,0:T(8,128)S(1)}, f32[3,384,384]{2,1,0:T(8,128)S(1)}, f32[3,384,384]{2,1,0:T(8,128)S(1)}, /*index=5*/f32[3,3,384]{2,1,0:T(4,128)}) fusion(f32[3,384,384]{2,1,0:T(8,128)S(1)} %subtract_divide_fusion.3, f32[3,3,384]{2,1,0:T(4,128)S(1)} %copy-done.35, ...), kind=kLoop, calls=%fused_computation.11 | loop fusion | flops 19896192 | bytes 8957952 | tf_op jit(solution)/shard_map/reduce_sum | solution.py:41
  67.7 1.7 add_sqrt_fusion
  69.4 1.5 collective-permute-start.5
  70.8 1.7 add_sqrt_fusion.2
  73.2 1.7 add_sqrt_fusion.1
  74.9 5.3 %collective-permute-done.5 = f32[2,128,384]{2,1,0:T(8,128)} collective-permute-done((f32[2,128,384]{2,1,0:T(8,128)}, f32[2,128,384]{2,1,0:T(8,128)}, u32[]{:S(2)}, u32[]{:S(2)}) %collective-permute-start.5) | collective-permute-done | bytes 393248 | tf_op jit(solution)/shard_map/ppermute | solution.py:21
  80.2 5.2 %multiply_reduce_fusion.2 = (f32[]{:T(128)}, f32[2,384,384]{2,1,0:T(8,128)S(1)}, f32[2,384,384]{2,1,0:T(8,128)}) fusion(f32[3,384,384]{2,1,0:T(8,128)} %get-tuple-element.41, f32[3,384,384]{2,1,0:T(8,128)S(1)} %copy-done.19, f32[2,128,384]{2,1,0:T(8,128)S(1)} %copy-done.4, f32[2,128,384]{2,1,0:T(8,128)} %collective-permute-done.5), kind=kOutput, calls=%fused_computation.89 | convolution fusion | flops 458293248 | bytes 7864324 | tf_op jit(solution)/shard_map/fei,fej->fij/dot_general | solution.py:31
  85.5 2.9 %convolution_bitcast_fusion.3 = f32[2,128,384]{1,2,0:T(8,128)} fusion(f32[2,384,384]{2,1,0:T(8,128)S(1)} %get-tuple-element.30, f32[2,128,384]{2,1,0:T(8,128)S(1)} %copy-done.4), kind=kOutput, calls=%fused_computation.66 | convolution fusion | flops 452984832 | bytes 1966080 | tf_op jit(solution)/shard_map/fij,fei->fej/dot_general | solution.py:45
  88.3 3.2 %collective-permute-start.15 = (f32[2,128,384]{1,2,0:T(8,128)}, f32[2,128,384]{1,2,0:T(8,128)}, u32[]{:S(2)}, u32[]{:S(2)}) collective-permute-start(f32[2,128,384]{1,2,0:T(8,128)} %convolution_bitcast_fusion.3), channel_id=1, source_target_pairs={{0,24},{4,28},{8,0},{12,4},{16,8},{20,12},{24,16},{28,20},{1,25},{... | collective-permute-start | bytes 1179656 | tf_op jit(solution)/shard_map/ppermute | solution.py:21
  91.6 2.2 %collective-permute-start.8 = (f32[2,128,384]{2,1,0:T(8,128)}, f32[2,128,384]{2,1,0:T(8,128)}, u32[]{:S(2)}, u32[]{:S(2)}) collective-permute-start(f32[2,128,384]{2,1,0:T(8,128)} %collective-permute-done.5), channel_id=1, source_target_pairs={{0,4},{4,8},{8,12},{12,16},{16,20},{20,24},{24,28},{28,0},{1,5},{5... | collective-permute-start | bytes 1179656 | tf_op jit(solution)/shard_map/ppermute | solution.py:21
  93.8 3.0 %fusion.39 = f32[2,128,384]{1,2,0:T(8,128)} fusion(f32[2,128,384]{1,2,0:T(8,128)} %collective-permute-done.14, f32[2,384,128]{2,1,0:T(8,128)S(1)} %copy-done.22, f32[2,384,384]{2,1,0:T(8,128)S(1)} %copy-done.14, f32[2,128,384]{2,1,0:T(8,128)} %collective-permute-done.2), kind=kOutput, calls=%fused_computation.76 | convolution fusion | flops 453181440 | bytes 2752512 | tf_op jit(solution)/shard_map/fij,fej->fei/dot_general | solution.py:44
  97.5 4.2 %subtract_divide_fusion.2 = f32[3,384,384]{2,1,0:T(8,128)} fusion(f32[2,384,384]{2,1,0:T(8,128)} %get-tuple-element.31, f32[3,384,384]{2,1,0:T(8,128)} %copy-done), kind=kLoop, calls=%fused_computation.27 | loop fusion | flops 1327104 | bytes 4718592 | tf_op jit(solution)/shard_map/div | solution.py:40
  101.7 9.6 %collective-permute-done.8 = f32[2,128,384]{2,1,0:T(8,128)} collective-permute-done((f32[2,128,384]{2,1,0:T(8,128)}, f32[2,128,384]{2,1,0:T(8,128)}, u32[]{:S(2)}, u32[]{:S(2)}) %collective-permute-start.8) | collective-permute-done | bytes 393248 | tf_op jit(solution)/shard_map/ppermute | solution.py:21
  111.3 4.5 %multiply_reduce_fusion.1 = (f32[]{:T(128)}, f32[2,384,384]{2,1,0:T(8,128)S(1)}, f32[2,384,384]{2,1,0:T(8,128)}) fusion(f32[3,384,384]{2,1,0:T(8,128)S(1)} %copy-done.20, f32[3,384,384]{2,1,0:T(8,128)S(1)} %copy-done.18, f32[2,128,384]{2,1,0:T(8,128)S(1)} %copy-done.5, f32[2,128,384]{2,1,0:T(8,128)} %collective-permute-done.8), kind=kOutput, calls=%fused_computation.88 | convolution fusion | flops 458293248 | bytes 7864324 | tf_op jit(solution)/shard_map/fei,fej->fij/dot_general | solution.py:31
  115.8 2.9 %convolution_bitcast_fusion.1 = f32[2,128,384]{1,2,0:T(8,128)} fusion(f32[2,384,384]{2,1,0:T(8,128)S(1)} %get-tuple-element.27, f32[2,128,384]{2,1,0:T(8,128)S(1)} %copy-done.5), kind=kOutput, calls=%fused_computation.64 | convolution fusion | flops 452984832 | bytes 1966080 | tf_op jit(solution)/shard_map/fij,fei->fej/dot_general | solution.py:45
  118.7 1.3 collective-permute-start.11
  120.0 3.0 %fusion.34 = f32[2,128,384]{1,2,0:T(8,128)} fusion(f32[2,128,384]{1,2,0:T(8,128)} %collective-permute-done.15, f32[2,128,384]{1,2,0:T(8,128)S(1)} %copy-done.24, f32[2,384,384]{2,1,0:T(8,128)S(1)} %copy-done.16, f32[2,128,384]{2,1,0:T(8,128)} %collective-permute-done.5), kind=kOutput, calls=%fused_computation.70 | convolution fusion | flops 453181440 | bytes 2752512 | tf_op jit(solution)/shard_map/fij,fej->fei/dot_general | solution.py:44
  123.7 2.4 %subtract_divide_fusion.1 = f32[3,384,384]{2,1,0:T(8,128)S(1)} fusion(f32[2,384,384]{2,1,0:T(8,128)} %get-tuple-element.28, f32[3,384,384]{2,1,0:T(8,128)S(1)} %get-tuple-element.16), kind=kLoop, calls=%fused_computation.25 | loop fusion | flops 1327104 | bytes 4718592 | tf_op jit(solution)/shard_map/div | solution.py:40
  126.1 7.2 %collective-permute-done.11 = f32[2,128,384]{2,1,0:T(8,128)} collective-permute-done((f32[2,128,384]{2,1,0:T(8,128)}, f32[2,128,384]{2,1,0:T(8,128)}, u32[]{:S(2)}, u32[]{:S(2)}) %collective-permute-start.11) | collective-permute-done | bytes 393248 | tf_op jit(solution)/shard_map/ppermute | solution.py:21
  133.4 4.3 %multiply_reduce_fusion = (f32[]{:T(128)}, f32[2,384,384]{2,1,0:T(8,128)S(1)}, f32[2,384,384]{2,1,0:T(8,128)}) fusion(f32[3,384,384]{2,1,0:T(8,128)S(1)} %copy-done.9, f32[3,384,384]{2,1,0:T(8,128)S(1)} %copy-done.7, f32[2,128,384]{2,1,0:T(8,128)S(1)} %copy-done.6, f32[2,128,384]{2,1,0:T(8,128)} %collective-permute-done.11), kind=kOutput, calls=%fused_computation.87 | convolution fusion | flops 456818688 | bytes 7864324 | tf_op jit(solution)/shard_map/fei,fej->fij/dot_general | solution.py:31
  138.3 0.8 copy-done.1
  139.2 3.3 %fusion.3 = (f32[3,3,384]{2,1,0:T(4,128)}, f32[3,3,384]{2,1,0:T(4,128)S(1)}, f32[3,3,384]{2,1,0:T(4,128)}, f32[3,3,384]{2,1,0:T(4,128)S(1)}, f32[3,3,384]{2,1,0:T(4,128)}) fusion(f32[3,384,384]{2,1,0:T(8,128)S(1)} %copy-done.1, f32[3,3,384]{2,1,0:T(4,128)S(1)} %copy-done.29, f32[3,3,384]{2,1,0:T(4,128)S(1)} %copy-done.27, f32[3,3,384]{2,1,0:T(4,128)S(1)} %copy-done.33, ...), kind=kLoop, calls=%fused_computation.13 | loop fusion | flops 14580864 | bytes 5432832 | tf_op jit(solution)/shard_map/reduce_sum | solution.py:41
  143.8 7.0 %collective-permute-start.10 = (f32[3,3,384]{2,1,0:T(4,128)}, f32[3,3,384]{2,1,0:T(4,128)}, u32[]{:S(2)}, u32[]{:S(2)}) collective-permute-start(f32[3,3,384]{2,1,0:T(4,128)} %neg.30), channel_id=1, source_target_pairs={{0,20},{4,24},{8,28},{12,0},{16,4},{20,8},{24,12},{28,16},{1,21},{... | collective-permute-start | bytes 41480 | tf_op jit(solution)/shard_map/ppermute | solution.py:21
  150.8 0.9 collective-permute-start.7
  151.7 3.1 %fusion.36 = f32[2,128,384]{1,2,0:T(8,128)} fusion(f32[2,128,384]{1,2,0:T(8,128)} %collective-permute-done.16, f32[2,128,384]{1,2,0:T(8,128)S(1)} %copy-done.23, f32[2,384,384]{2,1,0:T(8,128)S(1)} %copy-done.12, f32[2,128,384]{2,1,0:T(8,128)} %collective-permute-done.8), kind=kOutput, calls=%fused_computation.72 | convolution fusion | flops 453181440 | bytes 2752512 | tf_op jit(solution)/shard_map/fij,fej->fei/dot_general | solution.py:44
  155.5 0.9 add_add_fusion
  156.9 2.4 %collective-permute-start.13 = (f32[3,1,384]{2,1,0:T(1,128)S(1)}, f32[3,1,384]{2,1,0:T(1,128)S(1)}, u32[]{:S(2)}, u32[]{:S(2)}) collective-permute-start(f32[3,1,384]{2,1,0:T(1,128)S(1)} %slice.165), channel_id=1, source_target_pairs={{0,1},{1,2},{2,3},{4,5},{5,6},{6,7},{8,9},{9,10},{10,11},{12,13},{... | collective-permute-start | bytes 13832 | tf_op jit(solution)/shard_map/ppermute | solution.py:15
  159.3 3.7 %fusion.37 = f32[2,128,384]{1,2,0:T(8,128)} fusion(f32[2,128,384]{1,2,0:T(8,128)} %fusion.36, f32[2,128,384]{2,1,0:T(8,128)} %collective-permute-done.11, f32[2,384,384]{2,1,0:T(8,128)} %get-tuple-element.47, f32[3,384,384]{2,1,0:T(8,128)S(1)} %copy-done.10, f32[3,384,384]{2,1,0:T(8,128)S(1)} %copy-done.8), kind=kOutput, calls=%fused_computation.73 | convolution fusion | flops 455737344 | bytes 7077888 | tf_op jit(solution)/shard_map/fij,fej->fei/dot_general | solution.py:44
  163.0 38.4 %psum.7 = f32[]{:T(128)} all-reduce(f32[]{:T(128)S(6)} %add.141), channel_id=1, replica_groups=mesh['track'=8,'tm'=4] {'track','tm'}, use_global_device_ids=true, to_apply=%region_18.0 | all-reduce | flops 1 | bytes 8 | tf_op jit(solution)/shard_map/psum | solution.py:91
  201.4 1.9 copy.23
  204.0 0.8 slice_add_fusion
  (112 shorter events, 11.2 us)
Async XLA Ops:
  1.3 7.3 %collective-permute-start = (f32[1,384]{1,0:T(1,128)S(1)}, f32[1,384]{1,0:T(1,128)S(1)}, u32[]{:S(2)}, u32[]{:S(2)}) collective-permute-start(f32[1,384]{1,0:T(1,128)S(1)} %slice.135), channel_id=1, source_target_pairs={{1,0},{2,1},{3,2},{5,4},{6,5},{7,6},{9,8},{10,9},{11,10},{13,12},{... | collective-permute-start | bytes 4616 | tf_op jit(solution)/shard_map/ppermute | solution.py:15
  4.0 5.8 %collective-permute-start.1 = (f32[3,1,384]{2,1,0:T(1,128)S(1)}, f32[3,1,384]{2,1,0:T(1,128)S(1)}, u32[]{:S(2)}, u32[]{:S(2)}) collective-permute-start(f32[3,1,384]{2,1,0:T(1,128)S(1)} %slice.105), channel_id=1, source_target_pairs={{1,0},{2,1},{3,2},{5,4},{6,5},{7,6},{9,8},{10,9},{11,10},{13,12},{... | collective-permute-start | bytes 13832 | tf_op jit(solution)/shard_map/ppermute | solution.py:15
  5.9 48.7 %collective-permute-start.2 = (f32[2,128,384]{2,1,0:T(8,128)}, f32[2,128,384]{2,1,0:T(8,128)}, u32[]{:S(2)}, u32[]{:S(2)}) collective-permute-start(f32[2,128,384]{2,1,0:T(8,128)} %param.4), channel_id=1, source_target_pairs={{0,4},{4,8},{8,12},{12,16},{16,20},{20,24},{24,28},{28,0},{1,5},{5... | collective-permute-start | bytes 1179656 | tf_op jit(solution)/shard_map/ppermute | solution.py:21
  10.5 10.2 %collective-permute-start.3 = (f32[4,3,384]{2,1,0:T(4,128)S(1)}, f32[4,3,384]{2,1,0:T(4,128)S(1)}, u32[]{:S(2)}, u32[]{:S(2)}) collective-permute-start(f32[4,3,384]{2,1,0:T(4,128)S(1)} %pad_maximum_fusion), channel_id=1, source_target_pairs={{0,4},{4,8},{8,12},{12,16},{16,20},{20,24},{24,28},{28,0},{1,5},{5... | collective-permute-start | bytes 55304 | tf_op jit(solution)/shard_map/ppermute | solution.py:21
  13.5 8.8 %copy-start.25 = (f32[3,3,384]{2,1,0:T(4,128)}, f32[3,3,384]{2,1,0:T(4,128)S(1)}, u32[]{:S(2)}) copy-start(f32[3,3,384]{2,1,0:T(4,128)S(1)} %pad_maximum_fusion.1) | copy-start | bytes 41476
  20.7 1.6 copy-start.34
  24.4 5.9 %collective-permute-start.6 = (f32[4,3,384]{2,1,0:T(4,128)S(1)}, f32[4,3,384]{2,1,0:T(4,128)S(1)}, u32[]{:S(2)}, u32[]{:S(2)}) collective-permute-start(f32[4,3,384]{2,1,0:T(4,128)S(1)} %collective-permute-done.3), channel_id=1, source_target_pairs={{0,4},{4,8},{8,12},{12,16},{16,20},{20,24},{24,28},{28,0},{1,5},{5... | collective-permute-start | bytes 55304 | tf_op jit(solution)/shard_map/ppermute | solution.py:21
  30.3 5.4 %collective-permute-start.9 = (f32[4,3,384]{2,1,0:T(4,128)S(1)}, f32[4,3,384]{2,1,0:T(4,128)S(1)}, u32[]{:S(2)}, u32[]{:S(2)}) collective-permute-start(f32[4,3,384]{2,1,0:T(4,128)S(1)} %collective-permute-done.6), channel_id=1, source_target_pairs={{0,4},{4,8},{8,12},{12,16},{16,20},{20,24},{24,28},{28,0},{1,5},{5... | collective-permute-start | bytes 55304 | tf_op jit(solution)/shard_map/ppermute | solution.py:21
  35.6 5.4 %collective-permute-start.12 = (f32[4,3,384]{2,1,0:T(4,128)S(1)}, f32[4,3,384]{2,1,0:T(4,128)S(1)}, u32[]{:S(2)}, u32[]{:S(2)}) collective-permute-start(f32[4,3,384]{2,1,0:T(4,128)S(1)} %collective-permute-done.9), channel_id=1, source_target_pairs={{0,4},{4,8},{8,12},{12,16},{16,20},{20,24},{24,28},{28,0},{1,5},{5... | collective-permute-start | bytes 55304 | tf_op jit(solution)/shard_map/ppermute | solution.py:21
  41.6 3.6 %copy-start.2 = (f32[2,128,384]{2,1,0:T(8,128)S(1)}, f32[2,128,384]{2,1,0:T(8,128)}, u32[]{:S(2)}) copy-start(f32[2,128,384]{2,1,0:T(8,128)} %param.4) | copy-start | bytes 1179652
  52.2 10.3 %copy-start.32 = (f32[3,3,384]{2,1,0:T(4,128)}, f32[3,3,384]{2,1,0:T(4,128)S(1)}, u32[]{:S(2)}) copy-start(f32[3,3,384]{2,1,0:T(4,128)S(1)} %slice.161) | copy-start | bytes 41476
  52.2 2.4 %copy-start.3 = (f32[2,128,384]{2,1,0:T(8,128)S(1)}, f32[2,128,384]{2,1,0:T(8,128)}, u32[]{:S(2)}) copy-start(f32[2,128,384]{2,1,0:T(8,128)} %param.4) | copy-start | bytes 1179652
  52.2 2.4 %copy-start.17 = (f32[3,384,384]{2,1,0:T(8,128)S(1)}, f32[3,384,384]{2,1,0:T(8,128)}, u32[]{:S(2)}) copy-start(f32[3,384,384]{2,1,0:T(8,128)} %add_sqrt_fusion.3) | copy-start | bytes 5308420
  52.2 2.9 %copy-start.21 = (f32[3,384,384]{2,1,0:T(8,128)S(1)}, f32[3,384,384]{2,1,0:T(8,128)}, u32[]{:S(2)}) copy-start(f32[3,384,384]{2,1,0:T(8,128)} %get-tuple-element.43) | copy-start | bytes 5308420
  59.2 3.3 %copy-start.26 = (f32[3,3,384]{2,1,0:T(4,128)S(1)}, f32[3,3,384]{2,1,0:T(4,128)}, u32[]{:S(2)}) copy-start(f32[3,3,384]{2,1,0:T(4,128)} %copy-done.25) | copy-start | bytes 41476
  59.2 3.3 %copy-start.28 = (f32[3,3,384]{2,1,0:T(4,128)S(1)}, f32[3,3,384]{2,1,0:T(4,128)}, u32[]{:S(2)}) copy-start(f32[3,3,384]{2,1,0:T(4,128)} %slice.149) | copy-start | bytes 41476
  59.2 3.3 %copy-start.30 = (f32[3,3,384]{2,1,0:T(4,128)S(1)}, f32[3,3,384]{2,1,0:T(4,128)}, u32[]{:S(2)}) copy-start(f32[3,3,384]{2,1,0:T(4,128)} %slice.155) | copy-start | bytes 41476
  59.2 3.3 %copy-start.35 = (f32[3,3,384]{2,1,0:T(4,128)S(1)}, f32[3,3,384]{2,1,0:T(4,128)}, u32[]{:S(2)}) copy-start(f32[3,3,384]{2,1,0:T(4,128)} %copy-done.34) | copy-start | bytes 41476
  62.5 31.3 %collective-permute-start.14 = (f32[2,128,384]{1,2,0:T(8,128)}, f32[2,128,384]{1,2,0:T(8,128)}, u32[]{:S(2)}, u32[]{:S(2)}) collective-permute-start(f32[2,128,384]{1,2,0:T(8,128)} %convolution_bitcast_fusion.5), channel_id=1, source_target_pairs={{0,28},{4,0},{8,4},{12,8},{16,12},{20,16},{24,20},{28,24},{1,29},{... | collective-permute-start | bytes 1179656 | tf_op jit(solution)/shard_map/ppermute | solution.py:21
  67.1 3.8 %copy-start = (f32[3,384,384]{2,1,0:T(8,128)}, f32[3,384,384]{2,1,0:T(8,128)S(1)}, u32[]{:S(2)}) copy-start(f32[3,384,384]{2,1,0:T(8,128)S(1)} %get-tuple-element.15) | copy-start | bytes 5308420
  67.7 87.7 %collective-permute-start.4 = (f32[3,3,384]{2,1,0:T(4,128)}, f32[3,3,384]{2,1,0:T(4,128)}, u32[]{:S(2)}, u32[]{:S(2)}) collective-permute-start(f32[3,3,384]{2,1,0:T(4,128)} %neg.26), channel_id=1, source_target_pairs={{0,28},{4,0},{8,4},{12,8},{16,12},{20,16},{24,20},{28,24},{1,29},{... | collective-permute-start | bytes 41480 | tf_op jit(solution)/shard_map/ppermute | solution.py:21
  69.4 10.9 %collective-permute-start.5 = (f32[2,128,384]{2,1,0:T(8,128)}, f32[2,128,384]{2,1,0:T(8,128)}, u32[]{:S(2)}, u32[]{:S(2)}) collective-permute-start(f32[2,128,384]{2,1,0:T(8,128)} %collective-permute-done.2), channel_id=1, source_target_pairs={{0,4},{4,8},{8,12},{12,16},{16,20},{20,24},{24,28},{28,0},{1,5},{5... | collective-permute-start | bytes 1179656 | tf_op jit(solution)/shard_map/ppermute | solution.py:21
  73.2 7.1 %copy-start.4 = (f32[2,128,384]{2,1,0:T(8,128)S(1)}, f32[2,128,384]{2,1,0:T(8,128)}, u32[]{:S(2)}) copy-start(f32[2,128,384]{2,1,0:T(8,128)} %param.4) | copy-start | bytes 1179652
  73.2 7.1 %copy-start.19 = (f32[3,384,384]{2,1,0:T(8,128)S(1)}, f32[3,384,384]{2,1,0:T(8,128)}, u32[]{:S(2)}) copy-start(f32[3,384,384]{2,1,0:T(8,128)} %add_sqrt_fusion.2) | copy-start | bytes 5308420
  85.5 11.3 %copy-start.15 = (f32[2,384,384]{2,1,0:T(8,128)}, f32[2,384,384]{2,1,0:T(8,128)S(1)}, u32[]{:S(2)}) copy-start(f32[2,384,384]{2,1,0:T(8,128)S(1)} %get-tuple-element.30) | copy-start | bytes 3538948
  85.5 8.3 %copy-start.14 = (f32[2,384,384]{2,1,0:T(8,128)S(1)}, f32[2,384,384]{2,1,0:T(8,128)}, u32[]{:S(2)}) copy-start(f32[2,384,384]{2,1,0:T(8,128)} %copy-done.13) | copy-start | bytes 3538948
  85.5 8.3 %copy-start.22 = (f32[2,384,128]{2,1,0:T(8,128)S(1)}, f32[2,384,128]{2,1,0:T(8,128)}, u32[]{:S(2)}) copy-start(f32[2,384,128]{2,1,0:T(8,128)} %fusion.45) | copy-start | bytes 1179652
  88.3 31.7 %collective-permute-start.15 = (f32[2,128,384]{1,2,0:T(8,128)}, f32[2,128,384]{1,2,0:T(8,128)}, u32[]{:S(2)}, u32[]{:S(2)}) collective-permute-start(f32[2,128,384]{1,2,0:T(8,128)} %convolution_bitcast_fusion.3), channel_id=1, source_target_pairs={{0,24},{4,28},{8,0},{12,4},{16,8},{20,12},{24,16},{28,20},{1,25},{... | collective-permute-start | bytes 1179656 | tf_op jit(solution)/shard_map/ppermute | solution.py:21
  91.6 19.7 %collective-permute-start.8 = (f32[2,128,384]{2,1,0:T(8,128)}, f32[2,128,384]{2,1,0:T(8,128)}, u32[]{:S(2)}, u32[]{:S(2)}) collective-permute-start(f32[2,128,384]{2,1,0:T(8,128)} %collective-permute-done.5), channel_id=1, source_target_pairs={{0,4},{4,8},{8,12},{12,16},{16,20},{20,24},{24,28},{28,0},{1,5},{5... | collective-permute-start | bytes 1179656 | tf_op jit(solution)/shard_map/ppermute | solution.py:21
  97.5 13.8 %copy-start.5 = (f32[2,128,384]{2,1,0:T(8,128)S(1)}, f32[2,128,384]{2,1,0:T(8,128)}, u32[]{:S(2)}) copy-start(f32[2,128,384]{2,1,0:T(8,128)} %param.4) | copy-start | bytes 1179652
  97.5 13.8 %copy-start.18 = (f32[3,384,384]{2,1,0:T(8,128)S(1)}, f32[3,384,384]{2,1,0:T(8,128)}, u32[]{:S(2)}) copy-start(f32[3,384,384]{2,1,0:T(8,128)} %add_sqrt_fusion.1) | copy-start | bytes 5308420
  97.5 13.8 %copy-start.20 = (f32[3,384,384]{2,1,0:T(8,128)S(1)}, f32[3,384,384]{2,1,0:T(8,128)}, u32[]{:S(2)}) copy-start(f32[3,384,384]{2,1,0:T(8,128)} %get-tuple-element.39) | copy-start | bytes 5308420
  115.8 7.2 %copy-start.11 = (f32[2,384,384]{2,1,0:T(8,128)}, f32[2,384,384]{2,1,0:T(8,128)S(1)}, u32[]{:S(2)}) copy-start(f32[2,384,384]{2,1,0:T(8,128)S(1)} %get-tuple-element.27) | copy-start | bytes 3538948
  115.8 4.2 %copy-start.16 = (f32[2,384,384]{2,1,0:T(8,128)S(1)}, f32[2,384,384]{2,1,0:T(8,128)}, u32[]{:S(2)}) copy-start(f32[2,384,384]{2,1,0:T(8,128)} %copy-done.15) | copy-start | bytes 3538948
  115.8 4.2 %copy-start.24 = (f32[2,128,384]{1,2,0:T(8,128)S(1)}, f32[2,128,384]{1,2,0:T(8,128)}, u32[]{:S(2)}) copy-start(f32[2,128,384]{1,2,0:T(8,128)} %fusion.39) | copy-start | bytes 1179652
  118.7 33.0 %collective-permute-start.16 = (f32[2,128,384]{1,2,0:T(8,128)}, f32[2,128,384]{1,2,0:T(8,128)}, u32[]{:S(2)}, u32[]{:S(2)}) collective-permute-start(f32[2,128,384]{1,2,0:T(8,128)} %convolution_bitcast_fusion.1), channel_id=1, source_target_pairs={{0,20},{4,24},{8,28},{12,0},{16,4},{20,8},{24,12},{28,16},{1,21},{... | collective-permute-start | bytes 1179656 | tf_op jit(solution)/shard_map/ppermute | solution.py:21
  118.7 14.7 %collective-permute-start.11 = (f32[2,128,384]{2,1,0:T(8,128)}, f32[2,128,384]{2,1,0:T(8,128)}, u32[]{:S(2)}, u32[]{:S(2)}) collective-permute-start(f32[2,128,384]{2,1,0:T(8,128)} %collective-permute-done.8), channel_id=1, source_target_pairs={{0,4},{4,8},{8,12},{12,16},{16,20},{20,24},{24,28},{28,0},{1,5},{5... | collective-permute-start | bytes 1179656 | tf_op jit(solution)/shard_map/ppermute | solution.py:21
  123.7 9.7 %copy-start.6 = (f32[2,128,384]{2,1,0:T(8,128)S(1)}, f32[2,128,384]{2,1,0:T(8,128)}, u32[]{:S(2)}) copy-start(f32[2,128,384]{2,1,0:T(8,128)} %param.4) | copy-start | bytes 1179652
  123.7 9.7 %copy-start.7 = (f32[3,384,384]{2,1,0:T(8,128)S(1)}, f32[3,384,384]{2,1,0:T(8,128)}, u32[]{:S(2)}) copy-start(f32[3,384,384]{2,1,0:T(8,128)} %add_sqrt_fusion) | copy-start | bytes 5308420
  123.7 9.6 %copy-start.9 = (f32[3,384,384]{2,1,0:T(8,128)S(1)}, f32[3,384,384]{2,1,0:T(8,128)}, u32[]{:S(2)}) copy-start(f32[3,384,384]{2,1,0:T(8,128)} %get-tuple-element.40) | copy-start | bytes 5308420
  137.7 1.5 copy-start.33
  139.2 12.5 %copy-start.12 = (f32[2,384,384]{2,1,0:T(8,128)S(1)}, f32[2,384,384]{2,1,0:T(8,128)}, u32[]{:S(2)}) copy-start(f32[2,384,384]{2,1,0:T(8,128)} %copy-done.11) | copy-start | bytes 3538948
  139.2 12.5 %copy-start.23 = (f32[2,128,384]{1,2,0:T(8,128)S(1)}, f32[2,128,384]{1,2,0:T(8,128)}, u32[]{:S(2)}) copy-start(f32[2,128,384]{1,2,0:T(8,128)} %fusion.34) | copy-start | bytes 1179652
  139.2 20.1 %copy-start.10 = (f32[3,384,384]{2,1,0:T(8,128)S(1)}, f32[3,384,384]{2,1,0:T(8,128)}, u32[]{:S(2)}) copy-start(f32[3,384,384]{2,1,0:T(8,128)} %get-tuple-element.40) | copy-start | bytes 5308420
  143.8 15.5 %copy-start.8 = (f32[3,384,384]{2,1,0:T(8,128)S(1)}, f32[3,384,384]{2,1,0:T(8,128)}, u32[]{:S(2)}) copy-start(f32[3,384,384]{2,1,0:T(8,128)} %add_sqrt_fusion) | copy-start | bytes 5308420
  143.8 11.7 %collective-permute-start.10 = (f32[3,3,384]{2,1,0:T(4,128)}, f32[3,3,384]{2,1,0:T(4,128)}, u32[]{:S(2)}, u32[]{:S(2)}) collective-permute-start(f32[3,3,384]{2,1,0:T(4,128)} %neg.30), channel_id=1, source_target_pairs={{0,20},{4,24},{8,28},{12,0},{16,4},{20,8},{24,12},{28,16},{1,21},{... | collective-permute-start | bytes 41480 | tf_op jit(solution)/shard_map/ppermute | solution.py:21
  150.8 4.7 %collective-permute-start.7 = (f32[3,3,384]{2,1,0:T(4,128)}, f32[3,3,384]{2,1,0:T(4,128)}, u32[]{:S(2)}, u32[]{:S(2)}) collective-permute-start(f32[3,3,384]{2,1,0:T(4,128)} %neg.28), channel_id=1, source_target_pairs={{0,24},{4,28},{8,0},{12,4},{16,8},{20,12},{24,16},{28,20},{1,25},{... | collective-permute-start | bytes 41480 | tf_op jit(solution)/shard_map/ppermute | solution.py:21
  156.9 47.1 %collective-permute-start.13 = (f32[3,1,384]{2,1,0:T(1,128)S(1)}, f32[3,1,384]{2,1,0:T(1,128)S(1)}, u32[]{:S(2)}, u32[]{:S(2)}) collective-permute-start(f32[3,1,384]{2,1,0:T(1,128)S(1)} %slice.165), channel_id=1, source_target_pairs={{0,1},{1,2},{2,3},{4,5},{5,6},{6,7},{8,9},{9,10},{10,11},{12,13},{... | collective-permute-start | bytes 13832 | tf_op jit(solution)/shard_map/ppermute | solution.py:15
  (7 other events, 8.2 us)
where the time goes:
time: 209 us; the launch traced here: 207 us
  waiting for transfers between devices  45.9 us (22%)
  matrix products  44.6 us (21%)
  blocking collectives  38.4 us (18%)
  other arithmetic  36.7 us (18%)
  starting transfers between devices  27.3 us (13%)
  local copies, waits for them, and re-layouts  7.58 us (4%)
  between operations  6.08 us (3%)
    ppermute x14, waiting for transfers between devices, shifted_2(): return lax.ppermute(value, axis, pairs)  44.8 us
    psum x1, blocking collectives, on_device(): total = lax.psum(energy_sum, ('track', 'tm'))  38.4 us
    ppermute x14, starting transfers between devices, shifted_2(): return lax.ppermute(value, axis, pairs)  21.1 us
    dot_general x5, matrix products, tile_terms(): jnp.einsum('fei,fej->fij', emb_a, emb_b, precision=highest) * inv_root  20.9 us
    dot_general x5, matrix products, tile_terms(): jnp.einsum('fij,fej->fei', grad_logit, emb_b, precision=highest)  15.1 us
    div x5, other arithmetic, tile_terms(): scaled = (grad_dist / distance)[None] * offset  10.2 us
    dot_general x3, matrix products, tile_terms(): jnp.einsum('fij,fei->fej', grad_logit, emb_a, precision=highest)  8.58 us
    reduce_sum x2, other arithmetic, tile_terms(): grad_pos_a = jnp.sum(scaled, axis=3)  7.88 us
  transfers between devices with their start and end apart: 17, of which 8 were waited for; matrix products, arithmetic and copies ran while one was open for 37% of the time, Pallas kernels for 0%

commit v1 on v0

v1 whole, which is shorter than its diff:
```python
import functools
import math

import jax
import jax.numpy as jnp
from jax import lax
from jax.experimental import pallas as pl
from jax.experimental.pallas import tpu as pltpu
from jax.sharding import PartitionSpec as P

f32 = jnp.float32
bf16 = jnp.bfloat16
rigidity = 4.0
AXES = ("track", "tm")
COMPS = 7


def split(values):
    high = values.astype(bf16)
    return high, (values - high.astype(f32)).astype(bf16)


def pair_kernel(own_n, col_n, chunk, strip, rows, final, weight_scale, *refs):
    refs = list(refs)

    def take(count):
        taken = refs[:count]
        del refs[:count]
        return taken

    own_emb, own_pts, col_emb, col_pts = take(own_n), take(own_n), take(col_n), take(col_n)
    prev = take(2) if final[0] else None
    outs = take(own_n + 1 if final[1] else 2)
    weights, lhs, emb_split, points, logits, g_high, g_low, sums, own, grad = refs
    emb, width = own_emb[0].shape
    own_size, col_size = width * own_n, width * col_n
    inv_root = 1.0 / math.sqrt(emb)
    for a in range(own_n):
        at = slice(a * width, (a + 1) * width)
        high, low = split(own_emb[a][...] * (0.5 * inv_root))
        weights[0:emb, at] = high
        weights[emb : 2 * emb, at] = low
        weights[2 * emb : 3 * emb, at] = high
        own[:, at] = own_pts[a][...]
    for b in range(col_n):
        at = slice(b * width, (b + 1) * width)
        values = col_emb[b][...]
        high, low = split(values)
        emb_split[0:emb, at] = high
        emb_split[emb : 2 * emb, at] = low
        high, low = split(values.T)
        lhs[at, 0:emb] = high
        lhs[at, emb : 2 * emb] = high
        lhs[at, 2 * emb : 3 * emb] = low
        flipped = col_pts[b][...].T
        for c in range(COMPS):
            points[c, at, :] = jnp.broadcast_to(flipped[:, c : c + 1], (width, 128))
    sums[...] = jnp.zeros_like(sums)
    if prev is None:
        grad[...] = jnp.zeros_like(grad)
    else:
        grad[...] = prev[0][...]

    def fold(values):
        return values.reshape(rows // 8, 8, strip).sum(0)

    def step(n, carry):
        first = pl.multiple_of(n * chunk, chunk)
        logits[...] = jnp.dot(lhs[pl.ds(first, chunk), :], weights[...], preferred_element_type=f32)
        for i in range(0, own_size, strip):
            at = slice(i, i + strip)
            mine = [jnp.broadcast_to(own[c : c + 1, at], (rows, strip)) for c in range(6)]
            total = [sums[k, :, at] for k in range(COMPS)]
            for b in range(0, chunk, rows):
                theirs = [
                    jnp.concatenate([points[c, pl.ds(first + b, rows), :]] * (strip // 128), 1)
                    for c in range(COMPS)
                ]
                off = [mine[c] - theirs[c] for c in range(6)]
                sq0 = off[0] * off[0] + off[1] * off[1] + off[2] * off[2] + 1.0
                sq1 = off[3] * off[3] + off[4] * off[4] + off[5] * off[5] + 1.0
                inv0 = lax.rsqrt(sq0)
                inv1 = lax.rsqrt(sq1)
                change = sq1 * inv1 - sq0 * inv0
                tanh = jnp.tanh(logits[b : b + rows, at])
                pull = (change + change * tanh) * theirs[6]
                energy = pull * change
                high, low = split(energy - energy * tanh)
                g_high[b : b + rows, at] = high
                g_low[b : b + rows, at] = low
                w0 = pull * inv0
                w1 = pull * inv1
                for c in range(3):
                    total[c] = total[c] + fold(w0 * off[c])
                    total[3 + c] = total[3 + c] + fold(w1 * off[3 + c])
                total[6] = total[6] + fold(energy)
            for k in range(COMPS):
                sums[k, :, at] = total[k]
        both = jnp.dot(emb_split[:, pl.ds(first, chunk)], g_high[...], preferred_element_type=f32)
        rest = jnp.dot(emb_split[0:emb, pl.ds(first, chunk)], g_low[...], preferred_element_type=f32)
        grad[...] += both[:emb] + both[emb:] + rest
        return carry

    lax.fori_loop(0, col_size // chunk, step, 0)
    if not final[1]:
        outs[0][...] = grad[...]
        for k in range(COMPS):
            row = jnp.sum(sums[k], axis=0, keepdims=True)
            outs[1][k : k + 1, :] = row if prev is None else row + prev[1][k : k + 1, :]
        outs[1][COMPS:8, :] = jnp.zeros((8 - COMPS, own_size), f32)
        return
    seen = own[6:7, :] * weight_scale
    scale = seen * (0.25 * inv_root)
    lines = []
    for k in range(COMPS):
        row = jnp.sum(sums[k], axis=0, keepdims=True)
        lines.append(row if prev is None else row + prev[1][k : k + 1, :])
    for a in range(own_n):
        at = slice(a * width, (a + 1) * width)
        outs[a][0:emb, :] = grad[:, at] * scale[:, at]
        for c in range(3):
            outs[a][emb + c : emb + c + 1, :] = -lines[c][:, at] * seen[:, at]
            outs[a][emb + 3 + c : emb + 4 + c, :] = lines[3 + c][:, at] * seen[:, at]
        outs[a][emb + 6 : emb + 8, :] = jnp.zeros((2, width), f32)
    loss = jnp.sum(lines[6] * own[6:7, :], axis=1, keepdims=True)
    outs[own_n][...] = jnp.broadcast_to(loss, outs[own_n].shape)


def pair_terms(own_emb, own_pts, col_emb, col_pts, prev, last, peers, weight_scale):
    own_n, col_n = len(own_emb), len(col_emb)
    emb, width = own_emb[0].shape
    own_size, col_size = width * own_n, width * col_n
    chunk = strip = 256
    if col_size % chunk or own_size % strip:
        chunk = strip = 128
    if last:
        out_shape = [jax.ShapeDtypeStruct((emb + 8, width), f32)] * own_n
        out_shape.append(jax.ShapeDtypeStruct((peers, 128), f32))
    else:
        out_shape = [
            jax.ShapeDtypeStruct((emb, own_size), f32),
            jax.ShapeDtypeStruct((8, own_size), f32),
        ]
    extra = [] if prev is None else list(prev)
    pairs = own_size * col_size
    return pl.pallas_call(
        functools.partial(
            pair_kernel, own_n, col_n, chunk, strip, 32, (prev is not None, last), weight_scale
        ),
        out_shape=out_shape,
        scratch_shapes=[
            pltpu.VMEM((3 * emb, own_size), bf16),
            pltpu.VMEM((col_size, 3 * emb), bf16),
            pltpu.VMEM((2 * emb, col_size), bf16),
            pltpu.VMEM((COMPS, col_size, 128), f32),
            pltpu.VMEM((chunk, own_size), f32),
            pltpu.VMEM((chunk, own_size), bf16),
            pltpu.VMEM((chunk, own_size), bf16),
            pltpu.VMEM((COMPS, 8, own_size), f32),
            pltpu.VMEM((8, own_size), f32),
            pltpu.VMEM((emb, own_size), f32),
        ],
        compiler_params=pltpu.CompilerParams(vmem_limit_bytes=40 * 2**20),
        cost_estimate=pl.CostEstimate(
            flops=pairs * 12 * emb, bytes_accessed=pairs * 4, transcendentals=3 * pairs
        ),
    )(*own_emb, *own_pts, *col_emb, *col_pts, *extra)


def pick(options, index):
    chosen = options[0]
    for n in range(1, len(options)):
        chosen = jnp.where(index == n, options[n], chosen)
    return chosen


def on_device(positions, embeddings, visible):
    frames_local, emb, width = embeddings.shape
    track_n, tm_n = lax.axis_size("track"), lax.axis_size("tm")
    tracks, frames = width * track_n, frames_local * tm_n
    weight_scale = rigidity / math.sqrt(tracks)
    team = 2 * frames_local
    teams = track_n // team

    def homes():
        for track in range(track_n):
            for tm in range(tm_n):
                yield track, tm

    def worker(track, tm, turn, shift):
        crew, member = divmod(track, team)
        frame = (turn + member) % frames_local
        core = tm % 2
        to_track = (crew + shift) % teams * team + core * frames_local + frame
        return to_track * tm_n + (tm - core + member // frames_local), frame

    def outward(turn, shift):
        return [(t * tm_n + m, worker(t, m, turn, shift)[0]) for t, m in homes()]

    def inward(turn):
        return [(worker(t, m, turn, 0)[0], t * tm_n + m) for t, m in homes()]

    def inward_next(turn):
        pairs = []
        for t, m in homes():
            at, frame = worker(t, m, turn, 0)
            if frame == frames_local - 1 and m + 1 < tm_n:
                pairs.append((at, t * tm_n + m + 1))
        return pairs

    swap = [(t * tm_n + m, t * tm_n + (m ^ 1)) for t, m in homes()]
    member = lax.rem(lax.axis_index("track"), team)
    turns = range(frames_local)

    frame_of = [lax.rem(member + turn, frames_local) for turn in turns]
    sent = [pick([embeddings[k] for k in turns], frame_of[turn]) for turn in turns]
    arrived = [
        [lax.ppermute(sent[turn], AXES, outward(turn, shift)) for turn in turns]
        for shift in range(teams)
    ]

    seen = visible.astype(f32)
    rows = jnp.concatenate([positions, seen[None]], 0)
    following = lax.ppermute(rows[:, 0], "tm", [(i, i - 1) for i in range(1, tm_n)])
    rows = jnp.concatenate([rows, following[:, None]], 1)
    points = []
    for k in turns:
        points.append(
            jnp.concatenate(
                [
                    rows[:3, k],
                    rows[:3, k + 1],
                    rows[3:, k] * rows[3:, k + 1],
                    jnp.zeros((1, width), f32),
                ],
                0,
            )
        )
    sent_pts = [pick(points, frame_of[turn]) for turn in turns]
    arrived_pts = [
        [lax.ppermute(sent_pts[turn], AXES, outward(turn, shift)) for turn in turns]
        for shift in range(teams)
    ]
    beside = [[lax.ppermute(v, AXES, swap) for v in group] for group in arrived]
    beside_pts = [[lax.ppermute(v, AXES, swap) for v in group] for group in arrived_pts]

    own_emb, own_pts = arrived[0], arrived_pts[0]
    stages = [(arrived[0] + beside[0], arrived_pts[0] + beside_pts[0])]
    for shift in range(1, teams):
        for turn in turns:
            stages.append(
                (
                    [arrived[shift][turn], beside[shift][turn]],
                    [arrived_pts[shift][turn], beside_pts[shift][turn]],
                )
            )
    totals = None
    for n, (col_emb, col_pts) in enumerate(stages):
        totals = pair_terms(
            own_emb,
            own_pts,
            col_emb,
            col_pts,
            totals,
            n == len(stages) - 1,
            track_n * tm_n,
            weight_scale,
        )

    back = [lax.ppermute(totals[turn], AXES, inward(turn)) for turn in turns]
    late = [lax.ppermute(totals[turn][emb:], AXES, inward_next(turn)) for turn in turns]
    shares = lax.all_to_all(totals[frames_local], AXES, 0, 0, tiled=True)
    total = jnp.sum(shares[:, :1]) * 0.25
    mean_loss = total / (tracks * (tracks - 1) / 2.0 * (frames - 1))

    of_frame = [
        pick(back, lax.rem(k - member + team * frames_local, frames_local)) for k in turns
    ]
    grad_emb = jnp.stack([v[:emb] for v in of_frame])
    from_before = sum(v[3:6] for v in late)
    grad_pos = []
    for k in turns:
        extra = from_before if k == 0 else of_frame[k - 1][emb + 3 : emb + 6]
        grad_pos.append(of_frame[k][emb : emb + 3] + extra)
    return (jnp.stack(grad_pos, 1), grad_emb, mean_loss)


def solution(mesh):
    in_specs = (P(None, "tm", "track"), P("tm", None, "track"), P("tm", "track"))
    out_specs = (P(None, "tm", "track"), P("tm", None, "track"), P())
    return jax.shard_map(
        on_device, mesh=mesh, in_specs=in_specs, out_specs=out_specs, check_vma=False
    )
```

time: 209 us -> 85.8 us (0.41)
  matrix products: 44.6 us -> 0 us
  blocking collectives: 38.4 us -> 0 us
  other arithmetic: 36.7 us -> 2.57 us
  Pallas kernels: 0 us -> 25.1 us
  waiting for transfers between devices: 45.9 us -> 24.6 us
  local copies, waits for them, and re-layouts: 7.58 us -> 0.73 us
  between operations: 6.08 us -> 2.69 us
    dot_general x13 -> x0, matrix products: 44.6 us -> none  [the longest x5 20.9 us: tile_terms(): jnp.einsum('fei,fej->fij', emb_a, emb_b, precision=highest) * inv_root]
    psum x1 -> x0, blocking collectives: 38.4 us -> none  [on_device(): total = lax.psum(energy_sum, ('track', 'tm'))]
    ppermute x17 -> x21, waiting for transfers between devices: 45.9 us -> 19.9 us  [the longest x4 13.7 us: on_device(): lax.ppermute(sent_pts[turn], AXES, outward(turn, shift))]
    pallas_call x0 -> x3, Pallas kernels: none -> 25.1 us  [pair_terms(): pl.pallas_call(functools.partial(pair_kernel, own_n, col_n, chunk, strip,...]
    div x5 -> x0, other arithmetic: 10.2 us -> none  [tile_terms(): scaled = (grad_dist / distance)[None] * offset]
    reduce_sum x3 -> x1, other arithmetic: 9.42 us -> 0.6 us  [on_device(): total = jnp.sum(shares[:, :1]) * 0.25]
    sqrt x5 -> x0, other arithmetic: 7.15 us -> none  [tile_terms(): distance = jnp.sqrt(jnp.sum(offset * offset, axis=0) + 1.0)]
    all_to_all x0 -> x1, waiting for transfers between devices: none -> 4.69 us  [on_device(): shares = lax.all_to_all(totals[frames_local], AXES, 0, 0, tiled=True)]
  transfers between devices with their start and end apart: 17 -> 22, of which waited for: 8 -> 9; matrix products, arithmetic and copies ran while one was open for 37% -> 1% of each run, Pallas kernels for 0% -> 21%
where the time goes in v1:
time: 85.8 us; the launch traced here: 85 us
  starting transfers between devices  29.2 us (34%)
  Pallas kernels  25.1 us (29%)
  waiting for transfers between devices  24.6 us (29%)
  between operations  2.69 us (3%)
  other arithmetic  2.57 us (3%)
    pallas_call x3, Pallas kernels, pair_terms(): pl.pallas_call(functools.partial(pair_kernel, own_n, col_n, chunk, strip,...  25.1 us
    ppermute x4, waiting for transfers between devices, on_device(): lax.ppermute(sent_pts[turn], AXES, outward(turn, shift))  13.7 us
    ppermute x4, starting transfers between devices, on_device(): lax.ppermute(sent[turn], AXES, outward(turn, shift))  9.42 us
    ppermute x4, starting transfers between devices, on_device(): lax.ppermute(sent_pts[turn], AXES, outward(turn, shift))  8.35 us
    all_to_all x1, waiting for transfers between devices, on_device(): shares = lax.all_to_all(totals[frames_local], AXES, 0, 0, tiled=True)  4.69 us
    ppermute x2, starting transfers between devices, on_device(): back = [lax.ppermute(totals[turn], AXES, inward(turn)) for turn in turns]  3.74 us
    ppermute x1, waiting for transfers between devices, on_device(): lax.ppermute(rows[:, 0], 'tm', [(i, i - 1) for i in range(1, tm_n)])  3.23 us
    all_to_all x1, starting transfers between devices, on_device(): shares = lax.all_to_all(totals[frames_local], AXES, 0, 0, tiled=True)  2.94 us
  transfers between devices with their start and end apart: 22, of which 9 were waited for; matrix products, arithmetic and copies ran while one was open for 1% of the time, Pallas kernels for 21%

profile of v1, /device:TPU:1, one launch (start us, length us, event | category | flops | bytes accessed | tf_op | source)
XLA Modules:
  0.0 85.0 jit_solution(10282663792323693733)
XLA Ops:
  0.7 1.1 %select_bitcast_fusion = (f32[128,384]{1,0:T(8,128)S(1)}, f32[128,384]{1,0:T(8,128)S(1)}) fusion(f32[2,128,384]{2,1,0:T(8,128)} %param.4, pred[]{:T(512)S(6)} %eq.16, pred[]{:T(512)S(6)} %eq.15), kind=kLoop, calls=%fused_computation.3 | loop fusion | flops 98304 | bytes 786434 | tf_op jit(solution)/shard_map/jit(_where)/select_n | solution.py:173
  1.7 4.6 %collective-permute-start = (f32[128,384]{1,0:T(8,128)S(1)}, f32[128,384]{1,0:T(8,128)S(1)}, u32[]{:S(2)}, u32[]{:S(2)}) collective-permute-start(f32[128,384]{1,0:T(8,128)S(1)} %get-tuple-element.26), channel_id=1, source_target_pairs={{0,0},{1,8},{2,2},{3,10},{4,4},{5,12},{6,6},{7,14},{8,1},{9,9},{10... | collective-permute-start | bytes 589832 | tf_op jit(solution)/shard_map/ppermute | solution.py:218
  6.3 2.1 %collective-permute-start.9 = (f32[128,384]{1,0:T(8,128)S(1)}, f32[128,384]{1,0:T(8,128)S(1)}, u32[]{:S(2)}, u32[]{:S(2)}) collective-permute-start(f32[128,384]{1,0:T(8,128)S(1)} %get-tuple-element.26), channel_id=1, source_target_pairs={{0,16},{1,24},{2,18},{3,26},{4,20},{5,28},{6,22},{7,30},{8,17},{9,... | collective-permute-start | bytes 589832 | tf_op jit(solution)/shard_map/ppermute | solution.py:218
  8.4 1.8 %collective-permute-start.1 = (f32[128,384]{1,0:T(8,128)S(1)}, f32[128,384]{1,0:T(8,128)S(1)}, u32[]{:S(2)}, u32[]{:S(2)}) collective-permute-start(f32[128,384]{1,0:T(8,128)S(1)} %get-tuple-element.25), channel_id=1, source_target_pairs={{0,4},{1,12},{2,6},{3,14},{4,0},{5,8},{6,2},{7,10},{8,5},{9,13},{1... | collective-permute-start | bytes 589832 | tf_op jit(solution)/shard_map/ppermute | solution.py:218
  10.2 1.0 %collective-permute-start.5 = (f32[128,384]{1,0:T(8,128)S(1)}, f32[128,384]{1,0:T(8,128)S(1)}, u32[]{:S(2)}, u32[]{:S(2)}) collective-permute-start(f32[128,384]{1,0:T(8,128)S(1)} %get-tuple-element.25), channel_id=1, source_target_pairs={{0,20},{1,28},{2,22},{3,30},{4,16},{5,24},{6,18},{7,26},{8,21},{9,... | collective-permute-start | bytes 589832 | tf_op jit(solution)/shard_map/ppermute | solution.py:218
  11.2 1.9 %collective-permute-start.2 = (f32[4,384]{1,0:T(4,128)S(1)}, f32[4,384]{1,0:T(4,128)S(1)}, u32[]{:S(2)}, u32[]{:S(2)}) collective-permute-start(f32[4,384]{1,0:T(4,128)S(1)} %fusion.5), channel_id=1, source_target_pairs={{1,0},{2,1},{3,2},{5,4},{6,5},{7,6},{9,8},{10,9},{11,10},{13,12},{... | collective-permute-start | bytes 18440 | tf_op jit(solution)/shard_map/ppermute | solution.py:224
  13.1 0.1 pad.11.clone
  13.2 3.2 %collective-permute-done.2 = f32[4,384]{1,0:T(4,128)S(1)} collective-permute-done((f32[4,384]{1,0:T(4,128)S(1)}, f32[4,384]{1,0:T(4,128)S(1)}, u32[]{:S(2)}, u32[]{:S(2)}) %collective-permute-start.2) | collective-permute-done | bytes 6176 | tf_op jit(solution)/shard_map/ppermute | solution.py:224
  16.5 0.0 collective-permute-done.refs_0_.refs_4_
  16.5 0.1 collective-permute-start.13
  16.5 0.8 collective-permute-done.1.refs_1_.refs_5_
  17.3 0.0 collective-permute-start.14
  17.3 0.1 fusion
  17.4 5.6 %collective-permute-start.3 = (f32[8,384]{1,0:T(8,128)S(1)}, f32[8,384]{1,0:T(8,128)S(1)}, u32[]{:S(2)}, u32[]{:S(2)}) collective-permute-start(f32[8,384]{1,0:T(8,128)S(1)} %get-tuple-element.30), channel_id=1, source_target_pairs={{0,0},{1,8},{2,2},{3,10},{4,4},{5,12},{6,6},{7,14},{8,1},{9,9},{10... | collective-permute-start | bytes 36872 | tf_op jit(solution)/shard_map/ppermute | solution.py:241
  23.1 1.7 %collective-permute-done.3.refs_2_.refs_8_ = f32[8,384]{1,0:T(8,128)S(1)} collective-permute-done((f32[8,384]{1,0:T(8,128)S(1)}, f32[8,384]{1,0:T(8,128)S(1)}, u32[]{:S(2)}, u32[]{:S(2)}) %collective-permute-start.3) | collective-permute-done | bytes 12320 | tf_op jit(solution)/shard_map/ppermute | solution.py:241
  24.7 1.4 %collective-permute-start.4 = (f32[8,384]{1,0:T(8,128)S(1)}, f32[8,384]{1,0:T(8,128)S(1)}, u32[]{:S(2)}, u32[]{:S(2)}) collective-permute-start(f32[8,384]{1,0:T(8,128)S(1)} %get-tuple-element.29), channel_id=1, source_target_pairs={{0,4},{1,12},{2,6},{3,14},{4,0},{5,8},{6,2},{7,10},{8,5},{9,13},{1... | collective-permute-start | bytes 36872 | tf_op jit(solution)/shard_map/ppermute | solution.py:241
  26.1 2.6 %collective-permute-done.4.refs_3_.refs_9_ = f32[8,384]{1,0:T(8,128)S(1)} collective-permute-done((f32[8,384]{1,0:T(8,128)S(1)}, f32[8,384]{1,0:T(8,128)S(1)}, u32[]{:S(2)}, u32[]{:S(2)}) %collective-permute-start.4) | collective-permute-done | bytes 12320 | tf_op jit(solution)/shard_map/ppermute | solution.py:241
  28.7 0.7 collective-permute-start.11
  29.4 4.2 %collective-permute-done.11.refs_6_ = f32[8,384]{1,0:T(8,128)S(1)} collective-permute-done((f32[8,384]{1,0:T(8,128)S(1)}, f32[8,384]{1,0:T(8,128)S(1)}, u32[]{:S(2)}, u32[]{:S(2)}) %collective-permute-start.11) | collective-permute-done | bytes 12320 | tf_op jit(solution)/shard_map/ppermute | solution.py:241
  33.6 0.6 collective-permute-start.7
  34.3 0.0 collective-permute-done.9.refs_4_
  34.3 0.0 collective-permute-start.10
  34.3 5.2 %collective-permute-done.7.refs_6_ = f32[8,384]{1,0:T(8,128)S(1)} collective-permute-done((f32[8,384]{1,0:T(8,128)S(1)}, f32[8,384]{1,0:T(8,128)S(1)}, u32[]{:S(2)}, u32[]{:S(2)}) %collective-permute-start.7) | collective-permute-done | bytes 12320 | tf_op jit(solution)/shard_map/ppermute | solution.py:241
  39.5 0.0 collective-permute-start.15
  39.5 1.2 %collective-permute-done.15.refs_10_ = f32[8,384]{1,0:T(8,128)S(1)} collective-permute-done((f32[8,384]{1,0:T(8,128)S(1)}, f32[8,384]{1,0:T(8,128)S(1)}, u32[]{:S(2)}, u32[]{:S(2)}) %collective-permute-start.15) | collective-permute-done | bytes 12320 | tf_op jit(solution)/shard_map/ppermute | solution.py:245
  40.6 0.2 collective-permute-start.16
  40.8 1.0 %collective-permute-done.16.refs_11_ = f32[8,384]{1,0:T(8,128)S(1)} collective-permute-done((f32[8,384]{1,0:T(8,128)S(1)}, f32[8,384]{1,0:T(8,128)S(1)}, u32[]{:S(2)}, u32[]{:S(2)}) %collective-permute-start.16) | collective-permute-done | bytes 12320 | tf_op jit(solution)/shard_map/ppermute | solution.py:245
  41.8 0.2 collective-permute-start.12
  42.0 0.0 collective-permute-done.5.refs_4_
  42.0 0.3 collective-permute-start.8
  42.3 0.0 collective-permute-done.13.refs_6_
  42.3 0.2 collective-permute-start.6
  42.5 0.0 collective-permute-done.14.refs_7_
  42.5 12.1 %shard_map.58 = (f32[128,768]{1,0:T(8,128)S(1)}, f32[8,768]{1,0:T(8,128)S(1)}) custom-call(f32[128,384]{1,0:T(8,128)S(1)} %collective-permute-done.refs_0_.refs_4_, f32[128,384]{1,0:T(8,128)S(1)} %collective-permute-done.1.refs_1_.refs_5_, f32[8,384]{1,0:T(8,128)S(1)} %collective-permute-done.3.refs_2_.refs_8_, ...), custom_call_target="tpu_custom_call" | custom-call | flops 1811939328 | bytes 4718592 | tf_op jit(solution)/shard_map/pallas_call | solution.py:146
  54.6 0.0 collective-permute-done.10.refs_5_
  54.6 6.2 %shard_map.59 = (f32[128,768]{1,0:T(8,128)S(1)}, f32[8,768]{1,0:T(8,128)S(1)}) custom-call(f32[128,384]{1,0:T(8,128)S(1)} %collective-permute-done.refs_0_.refs_4_, f32[128,384]{1,0:T(8,128)S(1)} %collective-permute-done.1.refs_1_.refs_5_, f32[8,384]{1,0:T(8,128)S(1)} %collective-permute-done.3.refs_2_.refs_8_, ...), custom_call_target="tpu_custom_call" | custom-call | flops 905969664 | bytes 2359296 | tf_op jit(solution)/shard_map/pallas_call | solution.py:146
  60.8 0.0 collective-permute-done.6.refs_5_
  60.8 6.9 %shard_map.60 = (f32[136,384]{1,0:T(8,128)S(1)}, f32[136,384]{1,0:T(8,128)S(1)}, f32[32,128]{1,0:T(8,128)}) custom-call(f32[128,384]{1,0:T(8,128)S(1)} %collective-permute-done.refs_0_.refs_4_, f32[128,384]{1,0:T(8,128)S(1)} %collective-permute-done.1.refs_1_.refs_5_, f32[8,384]{1,0:T(8,128)S(1)} %collective-permute-done.3.refs_2_.refs_8_, ...), custom_call_target="tpu_custom_call" | custom-call | flops 905969664 | bytes 2359296 | tf_op jit(solution)/shard_map/pallas_call | solution.py:146
  67.7 0.0 collective-permute-start.17
  67.7 3.7 %collective-permute-start.18 = (f32[136,384]{1,0:T(8,128)S(1)}, f32[136,384]{1,0:T(8,128)S(1)}, u32[]{:S(2)}, u32[]{:S(2)}) collective-permute-start(f32[136,384]{1,0:T(8,128)S(1)} %get-tuple-element.15), channel_id=1, source_target_pairs={{0,0},{8,1},{2,2},{10,3},{4,4},{12,5},{6,6},{14,7},{1,8},{9,9},{3,... | collective-permute-start | bytes 626696 | tf_op jit(solution)/shard_map/ppermute | solution.py:270
  71.4 2.9 %all-to-all-start = ((f32[32,1,128]{2,1,0:T(1,128)}), f32[32,1,128]{2,1,0:T(1,128)S(1)}, u32[]{:S(2)}, u32[]{:S(2)}) async-start(f32[32,1,128]{2,1,0:T(1,128)} %bitcast.12), calls=%async_computation | async-start | bytes 32768 | tf_op jit(solution)/shard_map/all_to_all | solution.py:272
  74.4 0.7 collective-permute-start.19
  75.0 1.3 %collective-permute-start.20 = (f32[8,384]{1,0:T(8,128)S(1)}, f32[8,384]{1,0:T(8,128)S(1)}, u32[]{:S(2)}, u32[]{:S(2)}) collective-permute-start(f32[8,384]{1,0:T(8,128)S(1)} %slice.75), channel_id=1, source_target_pairs={{4,1},{12,2},{6,3},{5,9},{13,10},{7,11},{20,17},{28,18},{22,19},{2... | collective-permute-start | bytes 36872 | tf_op jit(solution)/shard_map/ppermute | solution.py:271
  76.3 4.7 %all-to-all-done = f32[32,1,128]{2,1,0:T(1,128)S(1)} async-done(((f32[32,1,128]{2,1,0:T(1,128)}), f32[32,1,128]{2,1,0:T(1,128)S(1)}, u32[]{:S(2)}, u32[]{:S(2)}) %all-to-all-start) | async-done | bytes 16416 | tf_op jit(solution)/shard_map/all_to_all | solution.py:272
  81.0 0.6 slice_reduce_fusion
  82.4 0.0 collective-permute-done.20
  82.4 0.6 copy.14
  83.0 0.8 pad_maximum_fusion
  (21 shorter events, 0.1 us)
Async XLA Ops:
  0.7 10.5 %copy-start = (f32[3,2,384]{2,1,0:T(2,128)S(1)}, f32[3,2,384]{2,1,0:T(2,128)}, u32[]{:S(2)}) copy-start(f32[3,2,384]{2,1,0:T(2,128)} %param.3) | copy-start | bytes 27652
  1.7 14.7 %collective-permute-start = (f32[128,384]{1,0:T(8,128)S(1)}, f32[128,384]{1,0:T(8,128)S(1)}, u32[]{:S(2)}, u32[]{:S(2)}) collective-permute-start(f32[128,384]{1,0:T(8,128)S(1)} %get-tuple-element.26), channel_id=1, source_target_pairs={{0,0},{1,8},{2,2},{3,10},{4,4},{5,12},{6,6},{7,14},{8,1},{9,9},{10... | collective-permute-start | bytes 589832 | tf_op jit(solution)/shard_map/ppermute | solution.py:218
  6.3 28.0 %collective-permute-start.9 = (f32[128,384]{1,0:T(8,128)S(1)}, f32[128,384]{1,0:T(8,128)S(1)}, u32[]{:S(2)}, u32[]{:S(2)}) collective-permute-start(f32[128,384]{1,0:T(8,128)S(1)} %get-tuple-element.26), channel_id=1, source_target_pairs={{0,16},{1,24},{2,18},{3,26},{4,20},{5,28},{6,22},{7,30},{8,17},{9,... | collective-permute-start | bytes 589832 | tf_op jit(solution)/shard_map/ppermute | solution.py:218
  8.4 2.7 %copy-start.1 = (s32[2,384]{1,0:T(2,128)S(1)}, s32[2,384]{1,0:T(2,128)}, u32[]{:S(2)}) copy-start(s32[2,384]{1,0:T(2,128)} %param.5) | copy-start | bytes 9220
  8.4 8.9 %collective-permute-start.1 = (f32[128,384]{1,0:T(8,128)S(1)}, f32[128,384]{1,0:T(8,128)S(1)}, u32[]{:S(2)}, u32[]{:S(2)}) collective-permute-start(f32[128,384]{1,0:T(8,128)S(1)} %get-tuple-element.25), channel_id=1, source_target_pairs={{0,4},{1,12},{2,6},{3,14},{4,0},{5,8},{6,2},{7,10},{8,5},{9,13},{1... | collective-permute-start | bytes 589832 | tf_op jit(solution)/shard_map/ppermute | solution.py:218
  10.2 31.8 %collective-permute-start.5 = (f32[128,384]{1,0:T(8,128)S(1)}, f32[128,384]{1,0:T(8,128)S(1)}, u32[]{:S(2)}, u32[]{:S(2)}) collective-permute-start(f32[128,384]{1,0:T(8,128)S(1)} %get-tuple-element.25), channel_id=1, source_target_pairs={{0,20},{1,28},{2,22},{3,30},{4,16},{5,24},{6,18},{7,26},{8,21},{9,... | collective-permute-start | bytes 589832 | tf_op jit(solution)/shard_map/ppermute | solution.py:218
  11.2 5.2 %collective-permute-start.2 = (f32[4,384]{1,0:T(4,128)S(1)}, f32[4,384]{1,0:T(4,128)S(1)}, u32[]{:S(2)}, u32[]{:S(2)}) collective-permute-start(f32[4,384]{1,0:T(4,128)S(1)} %fusion.5), channel_id=1, source_target_pairs={{1,0},{2,1},{3,2},{5,4},{6,5},{7,6},{9,8},{10,9},{11,10},{13,12},{... | collective-permute-start | bytes 18440 | tf_op jit(solution)/shard_map/ppermute | solution.py:224
  16.5 25.9 %collective-permute-start.13 = (f32[128,384]{1,0:T(8,128)S(1)}, f32[128,384]{1,0:T(8,128)S(1)}, u32[]{:S(2)}, u32[]{:S(2)}) collective-permute-start(f32[128,384]{1,0:T(8,128)S(1)} %collective-permute-done.refs_0_.refs_4_), channel_id=1, source_target_pairs={{0,1},{1,0},{2,3},{3,2},{4,5},{5,4},{6,7},{7,6},{8,9},{9,8},{10,11... | collective-permute-start | bytes 589832 | tf_op jit(solution)/shard_map/ppermute | solution.py:244
  17.3 25.2 %collective-permute-start.14 = (f32[128,384]{1,0:T(8,128)S(1)}, f32[128,384]{1,0:T(8,128)S(1)}, u32[]{:S(2)}, u32[]{:S(2)}) collective-permute-start(f32[128,384]{1,0:T(8,128)S(1)} %collective-permute-done.1.refs_1_.refs_5_), channel_id=1, source_target_pairs={{0,1},{1,0},{2,3},{3,2},{4,5},{5,4},{6,7},{7,6},{8,9},{9,8},{10,11... | collective-permute-start | bytes 589832 | tf_op jit(solution)/shard_map/ppermute | solution.py:244
  17.4 7.3 %collective-permute-start.3 = (f32[8,384]{1,0:T(8,128)S(1)}, f32[8,384]{1,0:T(8,128)S(1)}, u32[]{:S(2)}, u32[]{:S(2)}) collective-permute-start(f32[8,384]{1,0:T(8,128)S(1)} %get-tuple-element.30), channel_id=1, source_target_pairs={{0,0},{1,8},{2,2},{3,10},{4,4},{5,12},{6,6},{7,14},{8,1},{9,9},{10... | collective-permute-start | bytes 36872 | tf_op jit(solution)/shard_map/ppermute | solution.py:241
  24.7 4.0 %collective-permute-start.4 = (f32[8,384]{1,0:T(8,128)S(1)}, f32[8,384]{1,0:T(8,128)S(1)}, u32[]{:S(2)}, u32[]{:S(2)}) collective-permute-start(f32[8,384]{1,0:T(8,128)S(1)} %get-tuple-element.29), channel_id=1, source_target_pairs={{0,4},{1,12},{2,6},{3,14},{4,0},{5,8},{6,2},{7,10},{8,5},{9,13},{1... | collective-permute-start | bytes 36872 | tf_op jit(solution)/shard_map/ppermute | solution.py:241
  28.7 4.9 %collective-permute-start.11 = (f32[8,384]{1,0:T(8,128)S(1)}, f32[8,384]{1,0:T(8,128)S(1)}, u32[]{:S(2)}, u32[]{:S(2)}) collective-permute-start(f32[8,384]{1,0:T(8,128)S(1)} %get-tuple-element.30), channel_id=1, source_target_pairs={{0,16},{1,24},{2,18},{3,26},{4,20},{5,28},{6,22},{7,30},{8,17},{9,... | collective-permute-start | bytes 36872 | tf_op jit(solution)/shard_map/ppermute | solution.py:241
  33.6 5.8 %collective-permute-start.7 = (f32[8,384]{1,0:T(8,128)S(1)}, f32[8,384]{1,0:T(8,128)S(1)}, u32[]{:S(2)}, u32[]{:S(2)}) collective-permute-start(f32[8,384]{1,0:T(8,128)S(1)} %get-tuple-element.29), channel_id=1, source_target_pairs={{0,20},{1,28},{2,22},{3,30},{4,16},{5,24},{6,18},{7,26},{8,21},{9,... | collective-permute-start | bytes 36872 | tf_op jit(solution)/shard_map/ppermute | solution.py:241
  34.3 20.3 %collective-permute-start.10 = (f32[128,384]{1,0:T(8,128)S(1)}, f32[128,384]{1,0:T(8,128)S(1)}, u32[]{:S(2)}, u32[]{:S(2)}) collective-permute-start(f32[128,384]{1,0:T(8,128)S(1)} %collective-permute-done.9.refs_4_), channel_id=1, source_target_pairs={{0,1},{1,0},{2,3},{3,2},{4,5},{5,4},{6,7},{7,6},{8,9},{9,8},{10,11... | collective-permute-start | bytes 589832 | tf_op jit(solution)/shard_map/ppermute | solution.py:244
  39.5 1.2 %collective-permute-start.15 = (f32[8,384]{1,0:T(8,128)S(1)}, f32[8,384]{1,0:T(8,128)S(1)}, u32[]{:S(2)}, u32[]{:S(2)}) collective-permute-start(f32[8,384]{1,0:T(8,128)S(1)} %collective-permute-done.3.refs_2_.refs_8_), channel_id=1, source_target_pairs={{0,1},{1,0},{2,3},{3,2},{4,5},{5,4},{6,7},{7,6},{8,9},{9,8},{10,11... | collective-permute-start | bytes 36872 | tf_op jit(solution)/shard_map/ppermute | solution.py:245
  40.6 1.2 %collective-permute-start.16 = (f32[8,384]{1,0:T(8,128)S(1)}, f32[8,384]{1,0:T(8,128)S(1)}, u32[]{:S(2)}, u32[]{:S(2)}) collective-permute-start(f32[8,384]{1,0:T(8,128)S(1)} %collective-permute-done.4.refs_3_.refs_9_), channel_id=1, source_target_pairs={{0,1},{1,0},{2,3},{3,2},{4,5},{5,4},{6,7},{7,6},{8,9},{9,8},{10,11... | collective-permute-start | bytes 36872 | tf_op jit(solution)/shard_map/ppermute | solution.py:245
  41.8 12.8 %collective-permute-start.12 = (f32[8,384]{1,0:T(8,128)S(1)}, f32[8,384]{1,0:T(8,128)S(1)}, u32[]{:S(2)}, u32[]{:S(2)}) collective-permute-start(f32[8,384]{1,0:T(8,128)S(1)} %collective-permute-done.11.refs_6_), channel_id=1, source_target_pairs={{0,1},{1,0},{2,3},{3,2},{4,5},{5,4},{6,7},{7,6},{8,9},{9,8},{10,11... | collective-permute-start | bytes 36872 | tf_op jit(solution)/shard_map/ppermute | solution.py:245
  42.0 18.8 %collective-permute-start.8 = (f32[8,384]{1,0:T(8,128)S(1)}, f32[8,384]{1,0:T(8,128)S(1)}, u32[]{:S(2)}, u32[]{:S(2)}) collective-permute-start(f32[8,384]{1,0:T(8,128)S(1)} %collective-permute-done.7.refs_6_), channel_id=1, source_target_pairs={{0,1},{1,0},{2,3},{3,2},{4,5},{5,4},{6,7},{7,6},{8,9},{9,8},{10,11... | collective-permute-start | bytes 36872 | tf_op jit(solution)/shard_map/ppermute | solution.py:245
  42.3 18.4 %collective-permute-start.6 = (f32[128,384]{1,0:T(8,128)S(1)}, f32[128,384]{1,0:T(8,128)S(1)}, u32[]{:S(2)}, u32[]{:S(2)}) collective-permute-start(f32[128,384]{1,0:T(8,128)S(1)} %collective-permute-done.5.refs_4_), channel_id=1, source_target_pairs={{0,1},{1,0},{2,3},{3,2},{4,5},{5,4},{6,7},{7,6},{8,9},{9,8},{10,11... | collective-permute-start | bytes 589832 | tf_op jit(solution)/shard_map/ppermute | solution.py:244
  67.7 14.6 %collective-permute-start.17 = (f32[136,384]{1,0:T(8,128)S(1)}, f32[136,384]{1,0:T(8,128)S(1)}, u32[]{:S(2)}, u32[]{:S(2)}) collective-permute-start(f32[136,384]{1,0:T(8,128)S(1)} %get-tuple-element.14), channel_id=1, source_target_pairs={{4,0},{12,1},{6,2},{14,3},{0,4},{8,5},{2,6},{10,7},{5,8},{13,9},{7... | collective-permute-start | bytes 626696 | tf_op jit(solution)/shard_map/ppermute | solution.py:270
  67.7 14.7 %collective-permute-start.18 = (f32[136,384]{1,0:T(8,128)S(1)}, f32[136,384]{1,0:T(8,128)S(1)}, u32[]{:S(2)}, u32[]{:S(2)}) collective-permute-start(f32[136,384]{1,0:T(8,128)S(1)} %get-tuple-element.15), channel_id=1, source_target_pairs={{0,0},{8,1},{2,2},{10,3},{4,4},{12,5},{6,6},{14,7},{1,8},{9,9},{3,... | collective-permute-start | bytes 626696 | tf_op jit(solution)/shard_map/ppermute | solution.py:270
  71.4 9.6 %all-to-all-start = ((f32[32,1,128]{2,1,0:T(1,128)}), f32[32,1,128]{2,1,0:T(1,128)S(1)}, u32[]{:S(2)}, u32[]{:S(2)}) async-start(f32[32,1,128]{2,1,0:T(1,128)} %bitcast.12), calls=%async_computation | async-start | bytes 32768 | tf_op jit(solution)/shard_map/all_to_all | solution.py:272
  74.4 8.0 %collective-permute-start.19 = (f32[8,384]{1,0:T(8,128)S(1)}, f32[8,384]{1,0:T(8,128)S(1)}, u32[]{:S(2)}, u32[]{:S(2)}) collective-permute-start(f32[8,384]{1,0:T(8,128)S(1)} %slice.73), channel_id=1, source_target_pairs={{4,5},{12,6},{6,7},{5,13},{13,14},{7,15},{20,21},{28,22},{22,23},{... | collective-permute-start | bytes 36872 | tf_op jit(solution)/shard_map/ppermute | solution.py:271
  75.0 7.4 %collective-permute-start.20 = (f32[8,384]{1,0:T(8,128)S(1)}, f32[8,384]{1,0:T(8,128)S(1)}, u32[]{:S(2)}, u32[]{:S(2)}) collective-permute-start(f32[8,384]{1,0:T(8,128)S(1)} %slice.75), channel_id=1, source_target_pairs={{4,1},{12,2},{6,3},{5,9},{13,10},{7,11},{20,17},{28,18},{22,19},{2... | collective-permute-start | bytes 36872 | tf_op jit(solution)/shard_map/ppermute | solution.py:271

commit v2 on v1

--- a/solution.py
+++ b/solution.py
@@ -28,23 +28,23 @@
         del refs[:count]
         return taken
 
-    own_emb, own_pts, col_emb, col_pts = take(own_n), take(own_n), take(col_n), take(col_n)
+    own_blocks, col_blocks = take(own_n), take(col_n)
     prev = take(2) if final[0] else None
     outs = take(own_n + 1 if final[1] else 2)
     weights, lhs, emb_split, points, logits, g_high, g_low, sums, own, grad = refs
-    emb, width = own_emb[0].shape
+    emb, width = own_blocks[0].shape[0] - 8, own_blocks[0].shape[1]
     own_size, col_size = width * own_n, width * col_n
     inv_root = 1.0 / math.sqrt(emb)
     for a in range(own_n):
         at = slice(a * width, (a + 1) * width)
-        high, low = split(own_emb[a][...] * (0.5 * inv_root))
+        high, low = split(own_blocks[a][0:emb, :] * (0.5 * inv_root))
         weights[0:emb, at] = high
         weights[emb : 2 * emb, at] = low
         weights[2 * emb : 3 * emb, at] = high
-        own[:, at] = own_pts[a][...]
+        own[:, at] = own_blocks[a][emb : emb + 8, :]
     for b in range(col_n):
         at = slice(b * width, (b + 1) * width)
-        values = col_emb[b][...]
+        values = col_blocks[b][0:emb, :]
         high, low = split(values)
         emb_split[0:emb, at] = high
         emb_split[emb : 2 * emb, at] = low
@@ -52,7 +52,7 @@
         lhs[at, 0:emb] = high
         lhs[at, emb : 2 * emb] = high
         lhs[at, 2 * emb : 3 * emb] = low
-        flipped = col_pts[b][...].T
+        flipped = col_blocks[b][emb : emb + 8, :].T
         for c in range(COMPS):
             points[c, at, :] = jnp.broadcast_to(flipped[:, c : c + 1], (width, 128))
     sums[...] = jnp.zeros_like(sums)
@@ -126,13 +126,12 @@
     outs[own_n][...] = jnp.broadcast_to(loss, outs[own_n].shape)
 
 
-def pair_terms(own_emb, own_pts, col_emb, col_pts, prev, last, peers, weight_scale):
-    own_n, col_n = len(own_emb), len(col_emb)
-    emb, width = own_emb[0].shape
+def pair_terms(own_blocks, col_blocks, prev, last, peers, weight_scale):
+    own_n, col_n = len(own_blocks), len(col_blocks)
+    emb, width = own_blocks[0].shape[0] - 8, own_blocks[0].shape[1]
     own_size, col_size = width * own_n, width * col_n
-    chunk = strip = 256
-    if col_size % chunk or own_size % strip:
-        chunk = strip = 128
+    chunk = 256 if col_size % 256 == 0 else 384 if col_size % 384 == 0 else 128
+    strip = 256 if own_size % 256 == 0 else 128
     if last:
         out_shape = [jax.ShapeDtypeStruct((emb + 8, width), f32)] * own_n
         out_shape.append(jax.ShapeDtypeStruct((peers, 128), f32))
@@ -164,7 +163,7 @@
         cost_estimate=pl.CostEstimate(
             flops=pairs * 12 * emb, bytes_accessed=pairs * 4, transcendentals=3 * pairs
         ),
-    )(*own_emb, *own_pts, *col_emb, *col_pts, *extra)
+    )(*own_blocks, *col_blocks, *extra)
 
 
 def pick(options, index):
@@ -212,22 +211,16 @@
     member = lax.rem(lax.axis_index("track"), team)
     turns = range(frames_local)
 
-    frame_of = [lax.rem(member + turn, frames_local) for turn in turns]
-    sent = [pick([embeddings[k] for k in turns], frame_of[turn]) for turn in turns]
-    arrived = [
-        [lax.ppermute(sent[turn], AXES, outward(turn, shift)) for turn in turns]
-        for shift in range(teams)
-    ]
-
     seen = visible.astype(f32)
     rows = jnp.concatenate([positions, seen[None]], 0)
     following = lax.ppermute(rows[:, 0], "tm", [(i, i - 1) for i in range(1, tm_n)])
     rows = jnp.concatenate([rows, following[:, None]], 1)
-    points = []
+    blocks = []
     for k in turns:
-        points.append(
+        blocks.append(
             jnp.concatenate(
                 [
+                    embeddings[k],
                     rows[:3, k],
                     rows[:3, k + 1],
                     rows[3:, k] * rows[3:, k + 1],
@@ -236,36 +229,33 @@
                 0,
             )
         )
-    sent_pts = [pick(points, frame_of[turn]) for turn in turns]
-    arrived_pts = [
-        [lax.ppermute(sent_pts[turn], AXES, outward(turn, shift)) for turn in turns]
+    sent = [pick(blocks, lax.rem(member + turn, frames_local)) for turn in turns]
+    sent = lax.optimization_barrier(sent)
+    arrived = [
+        [lax.ppermute(sent[turn], AXES, outward(turn, shift)) for turn in turns]
         for shift in range(teams)
     ]
-    beside = [[lax.ppermute(v, AXES, swap) for v in group] for group in arrived]
-    beside_pts = [[lax.ppermute(v, AXES, swap) for v in group] for group in arrived_pts]
-
-    own_emb, own_pts = arrived[0], arrived_pts[0]
-    stages = [(arrived[0] + beside[0], arrived_pts[0] + beside_pts[0])]
-    for shift in range(1, teams):
-        for turn in turns:
-            stages.append(
-                (
-                    [arrived[shift][turn], beside[shift][turn]],
-                    [arrived_pts[shift][turn], beside_pts[shift][turn]],
-                )
-            )
-    totals = None
-    for n, (col_emb, col_pts) in enumerate(stages):
-        totals = pair_terms(
-            own_emb,
-            own_pts,
-            col_emb,
-            col_pts,
-            totals,
-            n == len(stages) - 1,
-            track_n * tm_n,
-            weight_scale,
-        )
+
+    def across(values):
+        return [lax.ppermute(v, AXES, swap) for v in values]
+
+    own = arrived[0]
+    terms = functools.partial(pair_terms, own, peers=track_n * tm_n, weight_scale=weight_scale)
+    beside = across(own)
+    totals = terms(own, None, False)
+    far = [v for shift in range(1, teams) for v in arrived[shift]]
+    ready = beside
+    for part in far[:-1]:
+        part, totals = lax.optimization_barrier((part, totals))
+        following = [part] + across([part])
+        totals = terms(ready, totals, False)
+        ready = following
+    if far:
+        totals = terms(ready, totals, False)
+        part, totals = lax.optimization_barrier((far[-1], totals))
+        ready = across([part])
+        totals = terms([part], totals, False)
+    totals = terms(ready, totals, True)
 
     back = [lax.ppermute(totals[turn], AXES, inward(turn)) for turn in turns]
     late = [lax.ppermute(totals[turn][emb:], AXES, inward_next(turn)) for turn in turns]

time: 85.8 us -> 67.8 us (0.79)
  waiting for transfers between devices: 24.6 us -> 11.5 us
  starting transfers between devices: 29.2 us -> 23.9 us
  local copies, waits for them, and re-layouts: 0.73 us -> 2.49 us
  other arithmetic: 2.57 us -> 1.47 us
    ppermute x12 -> x4, waiting for transfers between devices: 15.9 us -> 0.01 us  [across(): return [lax.ppermute(v, AXES, swap) for v in values]]
    ppermute x12 -> x4, starting transfers between devices: 9.27 us -> 0.84 us  [across(): return [lax.ppermute(v, AXES, swap) for v in values]]
    ppermute x4, waiting for transfers between devices: 0.81 us -> 4.4 us  [on_device(): lax.ppermute(sent[turn], AXES, outward(turn, shift))]
    ppermute x2, starting transfers between devices: 3.74 us -> 6.88 us  [on_device(): back = [lax.ppermute(totals[turn], AXES, inward(turn)) for turn in turns]]
    select_n x3 -> x2, other arithmetic: 1.16 us -> 0.06 us  [pick(): chosen = jnp.where(index == n, options[n], chosen)]
    squeeze x0 -> x1, local copies, waits for them, and re-layouts: none -> 1.05 us  [on_device(): embeddings[k]]
    pallas_call x3 -> x5, Pallas kernels: 25.1 us -> 24.9 us  [pair_terms(): pl.pallas_call(functools.partial(pair_kernel, own_n, col_n, chunk, strip,...]
  transfers between devices with their start and end apart: 22 -> 14, of which waited for: 9 -> 4; matrix products, arithmetic and copies ran while one was open for 1% -> 3% of each run, Pallas kernels for 21% -> 32%
where the time goes in v2:
time: 67.8 us; the launch traced here: 66.9 us
  Pallas kernels  24.9 us (37%)
  starting transfers between devices  23.9 us (35%)
  waiting for transfers between devices  11.5 us (17%)
  between operations  2.68 us (4%)
  local copies, waits for them, and re-layouts  2.49 us (4%)
  other arithmetic  1.47 us (2%)
    pallas_call x5, Pallas kernels, pair_terms(): pl.pallas_call(functools.partial(pair_kernel, own_n, col_n, chunk, strip,...  24.9 us
    ppermute x4, starting transfers between devices, on_device(): lax.ppermute(sent[turn], AXES, outward(turn, shift))  9.94 us
    ppermute x2, starting transfers between devices, on_device(): back = [lax.ppermute(totals[turn], AXES, inward(turn)) for turn in turns]  6.88 us
    ppermute x4, waiting for transfers between devices, on_device(): lax.ppermute(sent[turn], AXES, outward(turn, shift))  4.4 us
    all_to_all x1, waiting for transfers between devices, on_device(): shares = lax.all_to_all(totals[frames_local], AXES, 0, 0, tiled=True)  4.27 us
    ppermute x1, waiting for transfers between devices, on_device(): lax.ppermute(rows[:, 0], 'tm', [(i, i - 1) for i in range(1, tm_n)])  2.78 us
    all_to_all x1, starting transfers between devices, on_device(): shares = lax.all_to_all(totals[frames_local], AXES, 0, 0, tiled=True)  2.29 us
    ppermute x1, starting transfers between devices, on_device(): lax.ppermute(rows[:, 0], 'tm', [(i, i - 1) for i in range(1, tm_n)])  1.97 us
  transfers between devices with their start and end apart: 14, of which 4 were waited for; matrix products, arithmetic and copies ran while one was open for 3% of the time, Pallas kernels for 32%

profile of v2, /device:TPU:1, one launch (start us, length us, event | category | flops | bytes accessed | tf_op | source)
XLA Modules:
  0.0 66.9 jit_solution(14503553599908713912)
XLA Ops:
  0.6 0.0 copy-start
  0.6 0.7 %copy.10 = f32[3,2,384]{2,0,1:T(4,128)S(1)} copy(f32[3,2,384]{2,1,0:T(2,128)} %param.3) | data formatting | bytes 18432 | tf_op args[0]
  1.3 0.0 copy-done
  1.4 2.0 %collective-permute-start = (f32[4,384]{1,0:T(4,128)S(1)}, f32[4,384]{1,0:T(4,128)S(1)}, u32[]{:S(2)}, u32[]{:S(2)}) collective-permute-start(f32[4,384]{1,0:T(4,128)S(1)} %fusion.3), channel_id=1, source_target_pairs={{1,0},{2,1},{3,2},{5,4},{6,5},{7,6},{9,8},{10,9},{11,10},{13,12},{... | collective-permute-start | bytes 18440 | tf_op jit(solution)/shard_map/ppermute | solution.py:216
  3.4 1.1 %slice_bitcast_fusion.2 = (f32[128,384]{1,0:T(8,128)S(1)}, f32[128,384]{1,0:T(8,128)S(1)}) fusion(f32[2,128,384]{2,1,0:T(8,128)} %param.4), kind=kLoop, calls=%fused_computation.3 | loop fusion | bytes 786432 | tf_op jit(solution)/shard_map/squeeze | solution.py:223
  4.5 2.8 %collective-permute-done = f32[4,384]{1,0:T(4,128)S(1)} collective-permute-done((f32[4,384]{1,0:T(4,128)S(1)}, f32[4,384]{1,0:T(4,128)S(1)}, u32[]{:S(2)}, u32[]{:S(2)}) %collective-permute-start) | collective-permute-done | bytes 6176 | tf_op jit(solution)/shard_map/ppermute | solution.py:216
  7.4 1.9 %collective-permute-start.1 = (f32[136,384]{1,0:T(8,128)S(1)}, f32[136,384]{1,0:T(8,128)S(1)}, u32[]{:S(2)}, u32[]{:S(2)}) collective-permute-start(f32[136,384]{1,0:T(8,128)S(1)} %get-tuple-element.22), channel_id=1, source_target_pairs={{0,0},{1,8},{2,2},{3,10},{4,4},{5,12},{6,6},{7,14},{8,1},{9,9},{10... | collective-permute-start | bytes 626696 | tf_op jit(solution)/shard_map/ppermute | solution.py:235
  9.3 2.7 %collective-permute-start.2 = (f32[136,384]{1,0:T(8,128)S(1)}, f32[136,384]{1,0:T(8,128)S(1)}, u32[]{:S(2)}, u32[]{:S(2)}) collective-permute-start(f32[136,384]{1,0:T(8,128)S(1)} %get-tuple-element.23), channel_id=1, source_target_pairs={{0,4},{1,12},{2,6},{3,14},{4,0},{5,8},{6,2},{7,10},{8,5},{9,13},{1... | collective-permute-start | bytes 626696 | tf_op jit(solution)/shard_map/ppermute | solution.py:235
  12.0 2.0 %collective-permute-start.4 = (f32[136,384]{1,0:T(8,128)S(1)}, f32[136,384]{1,0:T(8,128)S(1)}, u32[]{:S(2)}, u32[]{:S(2)}) collective-permute-start(f32[136,384]{1,0:T(8,128)S(1)} %get-tuple-element.22), channel_id=1, source_target_pairs={{0,16},{1,24},{2,18},{3,26},{4,20},{5,28},{6,22},{7,30},{8,17},{9,... | collective-permute-start | bytes 626696 | tf_op jit(solution)/shard_map/ppermute | solution.py:235
  14.1 2.5 %collective-permute-done.1.refs_0_.refs_2_ = f32[136,384]{1,0:T(8,128)S(1)} collective-permute-done((f32[136,384]{1,0:T(8,128)S(1)}, f32[136,384]{1,0:T(8,128)S(1)}, u32[]{:S(2)}, u32[]{:S(2)}) %collective-permute-start.1) | collective-permute-done | bytes 208928 | tf_op jit(solution)/shard_map/ppermute | solution.py:235
  16.6 0.0 collective-permute-start.6
  16.6 1.9 %collective-permute-done.2.refs_1_.refs_3_ = f32[136,384]{1,0:T(8,128)S(1)} collective-permute-done((f32[136,384]{1,0:T(8,128)S(1)}, f32[136,384]{1,0:T(8,128)S(1)}, u32[]{:S(2)}, u32[]{:S(2)}) %collective-permute-start.2) | collective-permute-done | bytes 208928 | tf_op jit(solution)/shard_map/ppermute | solution.py:235
  18.4 0.0 collective-permute-start.7
  18.5 6.2 %shard_map.58 = (f32[128,768]{1,0:T(8,128)S(1)}, f32[8,768]{1,0:T(8,128)S(1)}) custom-call(f32[136,384]{1,0:T(8,128)S(1)} %collective-permute-done.1.refs_0_.refs_2_, f32[136,384]{1,0:T(8,128)S(1)} %collective-permute-done.2.refs_1_.refs_3_, f32[136,384]{1,0:T(8,128)S(1)} %collective-permute-done.1.refs_0_.refs_2_, ...), custom_call_target="tpu_custom_call" | custom-call | flops 905969664 | bytes 2359296 | tf_op jit(solution)/shard_map/pallas_call | solution.py:145
  24.6 0.0 collective-permute-done.4.refs_2_
  24.6 0.6 collective-permute-start.5
  25.2 3.3 %collective-permute-start.3 = (f32[136,384]{1,0:T(8,128)S(1)}, f32[136,384]{1,0:T(8,128)S(1)}, u32[]{:S(2)}, u32[]{:S(2)}) collective-permute-start(f32[136,384]{1,0:T(8,128)S(1)} %get-tuple-element.23), channel_id=1, source_target_pairs={{0,20},{1,28},{2,22},{3,30},{4,16},{5,24},{6,18},{7,26},{8,21},{9,... | collective-permute-start | bytes 626696 | tf_op jit(solution)/shard_map/ppermute | solution.py:235
  28.5 0.0 collective-permute-done.6.refs_2_
  28.5 0.0 collective-permute-done.7.refs_3_
  28.5 6.2 %shard_map.59 = (f32[128,768]{1,0:T(8,128)S(1)}, f32[8,768]{1,0:T(8,128)S(1)}) custom-call(f32[136,384]{1,0:T(8,128)S(1)} %collective-permute-done.1.refs_0_.refs_2_, f32[136,384]{1,0:T(8,128)S(1)} %collective-permute-done.2.refs_1_.refs_3_, f32[136,384]{1,0:T(8,128)S(1)} %collective-permute-done.6.refs_2_, f32[136,384]{1,0:T(8,128)S(1)} %collective-permute-done.7.refs_3_, ...), custom_call_target="tpu_custom_call" | custom-call | flops 905969664 | bytes 2359296 | tf_op jit(solution)/shard_map/pallas_call | solution.py:145
  34.6 0.0 collective-permute-done.5.refs_3_
  34.6 6.3 %shard_map.60 = (f32[128,768]{1,0:T(8,128)S(1)}, f32[8,768]{1,0:T(8,128)S(1)}) custom-call(f32[136,384]{1,0:T(8,128)S(1)} %collective-permute-done.1.refs_0_.refs_2_, f32[136,384]{1,0:T(8,128)S(1)} %collective-permute-done.2.refs_1_.refs_3_, f32[136,384]{1,0:T(8,128)S(1)} %collective-permute-done.4.refs_2_, f32[136,384]{1,0:T(8,128)S(1)} %collective-permute-done.5.refs_3_, ...), custom_call_target="tpu_custom_call" | custom-call | flops 905969664 | bytes 2359296 | tf_op jit(solution)/shard_map/pallas_call | solution.py:145
  41.0 0.0 collective-permute-done.3.refs_2_
  41.0 0.3 collective-permute-start.8
  41.3 3.0 %shard_map.61 = (f32[128,768]{1,0:T(8,128)S(1)}, f32[8,768]{1,0:T(8,128)S(1)}) custom-call(f32[136,384]{1,0:T(8,128)S(1)} %collective-permute-done.1.refs_0_.refs_2_, f32[136,384]{1,0:T(8,128)S(1)} %collective-permute-done.2.refs_1_.refs_3_, f32[136,384]{1,0:T(8,128)S(1)} %collective-permute-done.3.refs_2_, f32[128,768]{1,0:T(8,128)S(1)} %get-tuple-element.34.refs_3_, ...), custom_call_target="tpu_custom_call" | custom-call | flops 452984832 | bytes 1179648 | tf_op jit(solution)/shard_map/pallas_call | solution.py:145
  44.2 0.0 collective-permute-done.8.refs_2_
  44.3 3.3 %shard_map.62 = (f32[136,384]{1,0:T(8,128)S(1)}, f32[136,384]{1,0:T(8,128)S(1)}, f32[32,128]{1,0:T(8,128)}) custom-call(f32[136,384]{1,0:T(8,128)S(1)} %collective-permute-done.1.refs_0_.refs_2_, f32[136,384]{1,0:T(8,128)S(1)} %collective-permute-done.2.refs_1_.refs_3_, f32[136,384]{1,0:T(8,128)S(1)} %collective-permute-done.8.refs_2_, ...), custom_call_target="tpu_custom_call" | custom-call | flops 452984832 | bytes 1179648 | tf_op jit(solution)/shard_map/pallas_call | solution.py:145
  47.6 2.1 %collective-permute-start.10 = (f32[136,384]{1,0:T(8,128)S(1)}, f32[136,384]{1,0:T(8,128)S(1)}, u32[]{:S(2)}, u32[]{:S(2)}) collective-permute-start(f32[136,384]{1,0:T(8,128)S(1)} %get-tuple-element.39), channel_id=1, source_target_pairs={{0,0},{8,1},{2,2},{10,3},{4,4},{12,5},{6,6},{14,7},{1,8},{9,9},{3,... | collective-permute-start | bytes 626696 | tf_op jit(solution)/shard_map/ppermute | solution.py:260
  49.7 4.8 %collective-permute-start.9 = (f32[136,384]{1,0:T(8,128)S(1)}, f32[136,384]{1,0:T(8,128)S(1)}, u32[]{:S(2)}, u32[]{:S(2)}) collective-permute-start(f32[136,384]{1,0:T(8,128)S(1)} %get-tuple-element.38), channel_id=1, source_target_pairs={{4,0},{12,1},{6,2},{14,3},{0,4},{8,5},{2,6},{10,7},{5,8},{13,9},{7... | collective-permute-start | bytes 626696 | tf_op jit(solution)/shard_map/ppermute | solution.py:260
  54.4 2.3 %all-to-all-start = ((f32[32,1,128]{2,1,0:T(1,128)}), f32[32,1,128]{2,1,0:T(1,128)S(1)}, u32[]{:S(2)}, u32[]{:S(2)}) async-start(f32[32,1,128]{2,1,0:T(1,128)} %bitcast.12), calls=%async_computation | async-start | bytes 32768 | tf_op jit(solution)/shard_map/all_to_all | solution.py:262
  56.8 0.7 collective-permute-start.11
  57.4 1.3 %collective-permute-start.12 = (f32[8,384]{1,0:T(8,128)S(1)}, f32[8,384]{1,0:T(8,128)S(1)}, u32[]{:S(2)}, u32[]{:S(2)}) collective-permute-start(f32[8,384]{1,0:T(8,128)S(1)} %slice.73), channel_id=1, source_target_pairs={{4,1},{12,2},{6,3},{5,9},{13,10},{7,11},{20,17},{28,18},{22,19},{2... | collective-permute-start | bytes 36872 | tf_op jit(solution)/shard_map/ppermute | solution.py:261
  58.7 4.3 %all-to-all-done = f32[32,1,128]{2,1,0:T(1,128)S(1)} async-done(((f32[32,1,128]{2,1,0:T(1,128)}), f32[32,1,128]{2,1,0:T(1,128)S(1)}, u32[]{:S(2)}, u32[]{:S(2)}) %all-to-all-start) | async-done | bytes 16416 | tf_op jit(solution)/shard_map/all_to_all | solution.py:262
  63.0 0.6 slice_reduce_fusion
  64.3 0.0 collective-permute-done.10
  64.3 0.0 collective-permute-done.9
  64.4 0.0 collective-permute-done.11
  64.4 0.0 collective-permute-done.12
  64.4 0.6 copy.14
  65.0 0.8 %pad_maximum_fusion = f32[2,128,384]{2,1,0:T(8,128)} fusion(f32[1,128,384]{2,1,0:T(8,128)S(1)} %get-tuple-element.59, f32[1,128,384]{2,1,0:T(8,128)S(1)} %get-tuple-element.60), kind=kLoop, calls=%fused_computation | loop fusion | flops 98304 | bytes 786432 | tf_op jit(solution)/shard_map/stack | solution.py:269
  (15 shorter events, 0.2 us)
Async XLA Ops:
  0.6 0.7 %copy-start = (s32[2,384]{1,0:T(2,128)S(1)}, s32[2,384]{1,0:T(2,128)}, u32[]{:S(2)}) copy-start(s32[2,384]{1,0:T(2,128)} %param.5) | copy-start | bytes 9220
  1.4 5.8 %collective-permute-start = (f32[4,384]{1,0:T(4,128)S(1)}, f32[4,384]{1,0:T(4,128)S(1)}, u32[]{:S(2)}, u32[]{:S(2)}) collective-permute-start(f32[4,384]{1,0:T(4,128)S(1)} %fusion.3), channel_id=1, source_target_pairs={{1,0},{2,1},{3,2},{5,4},{6,5},{7,6},{9,8},{10,9},{11,10},{13,12},{... | collective-permute-start | bytes 18440 | tf_op jit(solution)/shard_map/ppermute | solution.py:216
  7.4 9.2 %collective-permute-start.1 = (f32[136,384]{1,0:T(8,128)S(1)}, f32[136,384]{1,0:T(8,128)S(1)}, u32[]{:S(2)}, u32[]{:S(2)}) collective-permute-start(f32[136,384]{1,0:T(8,128)S(1)} %get-tuple-element.22), channel_id=1, source_target_pairs={{0,0},{1,8},{2,2},{3,10},{4,4},{5,12},{6,6},{7,14},{8,1},{9,9},{10... | collective-permute-start | bytes 626696 | tf_op jit(solution)/shard_map/ppermute | solution.py:235
  9.3 9.2 %collective-permute-start.2 = (f32[136,384]{1,0:T(8,128)S(1)}, f32[136,384]{1,0:T(8,128)S(1)}, u32[]{:S(2)}, u32[]{:S(2)}) collective-permute-start(f32[136,384]{1,0:T(8,128)S(1)} %get-tuple-element.23), channel_id=1, source_target_pairs={{0,4},{1,12},{2,6},{3,14},{4,0},{5,8},{6,2},{7,10},{8,5},{9,13},{1... | collective-permute-start | bytes 626696 | tf_op jit(solution)/shard_map/ppermute | solution.py:235
  12.0 12.6 %collective-permute-start.4 = (f32[136,384]{1,0:T(8,128)S(1)}, f32[136,384]{1,0:T(8,128)S(1)}, u32[]{:S(2)}, u32[]{:S(2)}) collective-permute-start(f32[136,384]{1,0:T(8,128)S(1)} %get-tuple-element.22), channel_id=1, source_target_pairs={{0,16},{1,24},{2,18},{3,26},{4,20},{5,28},{6,22},{7,30},{8,17},{9,... | collective-permute-start | bytes 626696 | tf_op jit(solution)/shard_map/ppermute | solution.py:235
  16.6 11.9 %collective-permute-start.6 = (f32[136,384]{1,0:T(8,128)S(1)}, f32[136,384]{1,0:T(8,128)S(1)}, u32[]{:S(2)}, u32[]{:S(2)}) collective-permute-start(f32[136,384]{1,0:T(8,128)S(1)} %collective-permute-done.1.refs_0_.refs_2_), channel_id=1, source_target_pairs={{0,1},{1,0},{2,3},{3,2},{4,5},{5,4},{6,7},{7,6},{8,9},{9,8},{10,11... | collective-permute-start | bytes 626696 | tf_op jit(solution)/shard_map/ppermute | solution.py:240
  18.4 10.0 %collective-permute-start.7 = (f32[136,384]{1,0:T(8,128)S(1)}, f32[136,384]{1,0:T(8,128)S(1)}, u32[]{:S(2)}, u32[]{:S(2)}) collective-permute-start(f32[136,384]{1,0:T(8,128)S(1)} %collective-permute-done.2.refs_1_.refs_3_), channel_id=1, source_target_pairs={{0,1},{1,0},{2,3},{3,2},{4,5},{5,4},{6,7},{7,6},{8,9},{9,8},{10,11... | collective-permute-start | bytes 626696 | tf_op jit(solution)/shard_map/ppermute | solution.py:240
  24.6 10.0 %collective-permute-start.5 = (f32[136,384]{1,0:T(8,128)S(1)}, f32[136,384]{1,0:T(8,128)S(1)}, u32[]{:S(2)}, u32[]{:S(2)}) collective-permute-start(f32[136,384]{1,0:T(8,128)S(1)} %collective-permute-done.4.refs_2_), channel_id=1, source_target_pairs={{0,1},{1,0},{2,3},{3,2},{4,5},{5,4},{6,7},{7,6},{8,9},{9,8},{10,11... | collective-permute-start | bytes 626696 | tf_op jit(solution)/shard_map/ppermute | solution.py:240
  25.2 15.8 %collective-permute-start.3 = (f32[136,384]{1,0:T(8,128)S(1)}, f32[136,384]{1,0:T(8,128)S(1)}, u32[]{:S(2)}, u32[]{:S(2)}) collective-permute-start(f32[136,384]{1,0:T(8,128)S(1)} %get-tuple-element.23), channel_id=1, source_target_pairs={{0,20},{1,28},{2,22},{3,30},{4,16},{5,24},{6,18},{7,26},{8,21},{9,... | collective-permute-start | bytes 626696 | tf_op jit(solution)/shard_map/ppermute | solution.py:235
  41.0 3.2 %collective-permute-start.8 = (f32[136,384]{1,0:T(8,128)S(1)}, f32[136,384]{1,0:T(8,128)S(1)}, u32[]{:S(2)}, u32[]{:S(2)}) collective-permute-start(f32[136,384]{1,0:T(8,128)S(1)} %collective-permute-done.3.refs_2_), channel_id=1, source_target_pairs={{0,1},{1,0},{2,3},{3,2},{4,5},{5,4},{6,7},{7,6},{8,9},{9,8},{10,11... | collective-permute-start | bytes 626696 | tf_op jit(solution)/shard_map/ppermute | solution.py:240
  47.6 16.7 %collective-permute-start.10 = (f32[136,384]{1,0:T(8,128)S(1)}, f32[136,384]{1,0:T(8,128)S(1)}, u32[]{:S(2)}, u32[]{:S(2)}) collective-permute-start(f32[136,384]{1,0:T(8,128)S(1)} %get-tuple-element.39), channel_id=1, source_target_pairs={{0,0},{8,1},{2,2},{10,3},{4,4},{12,5},{6,6},{14,7},{1,8},{9,9},{3,... | collective-permute-start | bytes 626696 | tf_op jit(solution)/shard_map/ppermute | solution.py:260
  49.7 14.6 %collective-permute-start.9 = (f32[136,384]{1,0:T(8,128)S(1)}, f32[136,384]{1,0:T(8,128)S(1)}, u32[]{:S(2)}, u32[]{:S(2)}) collective-permute-start(f32[136,384]{1,0:T(8,128)S(1)} %get-tuple-element.38), channel_id=1, source_target_pairs={{4,0},{12,1},{6,2},{14,3},{0,4},{8,5},{2,6},{10,7},{5,8},{13,9},{7... | collective-permute-start | bytes 626696 | tf_op jit(solution)/shard_map/ppermute | solution.py:260
  54.4 8.6 %all-to-all-start = ((f32[32,1,128]{2,1,0:T(1,128)}), f32[32,1,128]{2,1,0:T(1,128)S(1)}, u32[]{:S(2)}, u32[]{:S(2)}) async-start(f32[32,1,128]{2,1,0:T(1,128)} %bitcast.12), calls=%async_computation | async-start | bytes 32768 | tf_op jit(solution)/shard_map/all_to_all | solution.py:262
  56.8 7.6 %collective-permute-start.11 = (f32[8,384]{1,0:T(8,128)S(1)}, f32[8,384]{1,0:T(8,128)S(1)}, u32[]{:S(2)}, u32[]{:S(2)}) collective-permute-start(f32[8,384]{1,0:T(8,128)S(1)} %slice.71), channel_id=1, source_target_pairs={{4,5},{12,6},{6,7},{5,13},{13,14},{7,15},{20,21},{28,22},{22,23},{... | collective-permute-start | bytes 36872 | tf_op jit(solution)/shard_map/ppermute | solution.py:261
  57.4 6.9 %collective-permute-start.12 = (f32[8,384]{1,0:T(8,128)S(1)}, f32[8,384]{1,0:T(8,128)S(1)}, u32[]{:S(2)}, u32[]{:S(2)}) collective-permute-start(f32[8,384]{1,0:T(8,128)S(1)} %slice.73), channel_id=1, source_target_pairs={{4,1},{12,2},{6,3},{5,9},{13,10},{7,11},{20,17},{28,18},{22,19},{2... | collective-permute-start | bytes 36872 | tf_op jit(solution)/shard_map/ppermute | solution.py:261

commit v3 on v2

v3 whole, which is shorter than its diff:
```python
import functools
import math

import jax
import jax.numpy as jnp
from jax import lax
from jax.experimental import pallas as pl
from jax.experimental.pallas import tpu as pltpu
from jax.sharding import PartitionSpec as P

f32 = jnp.float32
bf16 = jnp.bfloat16
rigidity = 4.0
AXES = ("track", "tm")
TAIL = 8
GEO = 128
LEFT = (0, 0, 1, 0, 2, 1, 1, 2)
RIGHT = (0, 1, 0, 2, 0, 1, 2, 1)


def split(values):
    high = values.astype(bf16)
    return high, (values - high.astype(f32)).astype(bf16)


def split3(values):
    high = values.astype(bf16).astype(f32)
    rest = values - high
    mid = rest.astype(bf16).astype(f32)
    return high, mid, rest - mid


def geometry(ref, points, centre, left):
    size = points.shape[1]
    start = points[0:3] - centre[0:3]
    end = points[3:6] - centre[3:6]
    move = end - start
    square = jnp.sum(start * start, axis=0, keepdims=True)
    growth = jnp.sum(move * (start + end), axis=0, keepdims=True)
    ones = [jnp.ones((1, size), f32)] * 3
    if left:
        order, factor, factors = LEFT, -2.0, (start, start, move)
        tails = (list(split3(square)) + ones, list(split3(growth)) + ones)
    else:
        order, factor, factors = RIGHT, 1.0, (start, move, end)
        tails = (ones + list(split3(square + 1.0)), ones + list(split3(growth)))
    ref[...] = jnp.zeros_like(ref)
    parts = [split3(v) for v in factors]
    for at, group, tail in ((0, parts[:1], tails[0]), (32, parts[1:], tails[1])):
        for part in group:
            for k in order:
                ref[at : at + 3, :] = factor * part[k]
                at += 3
        for row in tail:
            ref[at : at + 1, :] = row
            at += 1
    return start, end


def pair_kernel(own_n, col_n, chunk, strip, rows, first, last, weight_scale, *refs):
    refs = list(refs)

    def take(count):
        taken = refs[:count]
        del refs[:count]
        return taken

    own_blocks, col_blocks = take(own_n), take(col_n)
    prev = take(0 if first else 2)
    kept = take(0 if first else 2)
    outs = take(own_n + 1 if last else 2)
    if first:
        kept = take(2)
    weights, geo_weights = kept
    lhs, geo_lhs, emb_split, pts_split, geo_own, geo_col, grad, sums, energies, own = take(10)
    logits, geo, g_high, g_low = take(2), take(2), take(2), take(2)
    pulls = [take(4), take(4)]
    emb, width = own_blocks[0].shape[0] - TAIL, own_blocks[0].shape[1]
    own_size, col_size = width * own_n, width * col_n
    inv_root = 1.0 / math.sqrt(emb)
    for a in range(own_n):
        own[:, a * width : (a + 1) * width] = own_blocks[a][emb : emb + TAIL, :]
    centre = jnp.mean(own[0:6, :], axis=1, keepdims=True)
    if first:
        for a in range(own_n):
            at = slice(a * width, (a + 1) * width)
            high, low = split(own_blocks[a][0:emb, :] * (0.5 * inv_root))
            weights[0:emb, at] = high
            weights[emb : 2 * emb, at] = low
            weights[2 * emb : 3 * emb, at] = high
        row = lax.broadcasted_iota(jnp.int32, (emb, own_size), 0)
        weights[3 * emb : 4 * emb, :] = jnp.where(row == 0, 1.0, 0.0).astype(bf16)
        geometry(geo_own, own[...], centre, True)
        row = lax.broadcasted_iota(jnp.int32, (GEO, own_size), 0)
        values = geo_own[...]
        geo_weights[:, 0:own_size] = jnp.where(row < 32, values, 0.0).astype(bf16)
        geo_weights[:, own_size : 2 * own_size] = jnp.where(row < 32, 0.0, values).astype(bf16)
    for b in range(col_n):
        at = slice(b * width, (b + 1) * width)
        values = col_blocks[b][0:emb, :]
        high, low = split(values)
        emb_split[0:emb, at] = high
        emb_split[emb : 2 * emb, at] = low
        high, low = split(values.T)
        lhs[at, 0:emb] = high
        lhs[at, emb : 2 * emb] = high
        lhs[at, 2 * emb : 3 * emb] = low
        points = col_blocks[b][emb : emb + TAIL, :]
        start, end = geometry(geo_col, points, centre, False)
        geo_col[96:97, :] = (points[6:7, :] - 1.0) * 1e4
        flipped = geo_col[...].T
        geo_lhs[at, :] = flipped.astype(bf16)
        hidden = jnp.broadcast_to(flipped[:, 96:97], (width, emb))
        column = lax.broadcasted_iota(jnp.int32, (width, emb), 1)
        lhs[at, 3 * emb : 4 * emb] = jnp.where(column == 0, hidden, 0.0).astype(bf16)
        ones, zeros = jnp.ones((1, width), f32), jnp.zeros((1, width), f32)
        centred = jnp.concatenate([start, end, ones, zeros], 0)
        for k, part in enumerate(split3(centred)):
            pts_split[8 * k : 8 * k + 8, at] = part.astype(bf16)
    if first:
        grad[...] = jnp.zeros_like(grad)
        sums[...] = jnp.zeros_like(sums)
        energies[...] = jnp.zeros_like(energies)
    else:
        grad[...] = prev[0][...]
        sums[...] = prev[1][0:16, :]
        energies[...] = prev[1][16:24, :]

    def products(n, i, k):
        cols, at = pl.ds(n * chunk, chunk), slice(i * strip, (i + 1) * strip)
        logits[k][...] = jnp.dot(lhs[cols, :], weights[:, at], preferred_element_type=f32)
        side = geo_lhs[cols, :]
        geo[k][0] = jnp.dot(side, geo_weights[:, at], preferred_element_type=f32)
        at = slice(own_size + i * strip, own_size + (i + 1) * strip)
        geo[k][1] = jnp.dot(side, geo_weights[:, at], preferred_element_type=f32)

    def elementwise(n, i, k):
        mine = slice(i * strip, (i + 1) * strip)
        total = energies[:, mine]
        for b in range(0, chunk, rows):
            at = slice(b, b + rows)
            sq0, growth = geo[k][0, at, :], geo[k][1, at, :]
            sq1 = sq0 + growth
            inv0, inv1 = lax.rsqrt(sq0), lax.rsqrt(sq1)
            both = sq1 * inv1 + sq0 * inv0
            change = growth * lax.rsqrt(both * both)
            tanh = jnp.tanh(logits[k][at, :])
            pull = change + change * tanh
            energy = pull * change
            g_high[k][at, :], g_low[k][at, :] = split(energy - energy * tanh)
            pulls[k][0][at, :], pulls[k][1][at, :] = split(pull * inv0)
            pulls[k][2][at, :], pulls[k][3][at, :] = split(pull * inv1)
            total = total + energy.reshape(rows // 8, 8, strip).sum(0)
        energies[:, mine] = total

    def gradients(n, i, k):
        cols, at = pl.ds(n * chunk, chunk), slice(i * strip, (i + 1) * strip)
        two = jnp.dot(emb_split[:, cols], g_high[k][...], preferred_element_type=f32)
        one = jnp.dot(emb_split[0:emb, cols], g_low[k][...], preferred_element_type=f32)
        grad[:, at] += two[:emb] + two[emb:] + one
        side = pts_split[:, cols]
        for frame in range(2):
            high, low = pulls[k][2 * frame], pulls[k][2 * frame + 1]
            moved = jnp.dot(side, high[...], preferred_element_type=f32)
            moved = moved + jnp.dot(side, low[...], preferred_element_type=f32)
            sums[8 * frame : 8 * frame + 8, at] += moved[:8] + moved[8:16] + moved[16:]

    tiles = [(n, i) for n in range(col_size // chunk) for i in range(own_size // strip)]
    products(*tiles[0], 0)
    for t, (n, i) in enumerate(tiles):
        if t + 1 < len(tiles):
            products(*tiles[t + 1], (t + 1) % 2)
        elementwise(n, i, t % 2)
        gradients(n, i, t % 2)

    if not last:
        outs[0][...] = grad[...]
        outs[1][0:16, :] = sums[...]
        outs[1][16:24, :] = energies[...]
        return
    seen = own[6:7, :] * weight_scale
    scale = seen * (0.25 * inv_root)
    start, end = own[0:3, :] - centre[0:3], own[3:6, :] - centre[3:6]
    from_start = (sums[0:3, :] - start * sums[6:7, :]) * seen
    from_end = (end * sums[14:15, :] - sums[11:14, :]) * seen
    for a in range(own_n):
        at = slice(a * width, (a + 1) * width)
        outs[a][0:emb, :] = grad[:, at] * scale[:, at]
        outs[a][emb : emb + 3, :] = from_start[:, at]
        outs[a][emb + 3 : emb + 6, :] = from_end[:, at]
        outs[a][emb + 6 : emb + 8, :] = jnp.zeros((2, width), f32)
    loss = jnp.sum(energies[...] * own[6:7, :], axis=0, keepdims=True)
    loss = jnp.sum(loss, axis=1, keepdims=True)
    outs[own_n][...] = jnp.broadcast_to(loss, outs[own_n].shape)


def pair_terms(own_blocks, col_blocks, prev, last, peers, weight_scale):
    own_n, col_n = len(own_blocks), len(col_blocks)
    emb, width = own_blocks[0].shape[0] - TAIL, own_blocks[0].shape[1]
    own_size, col_size = width * own_n, width * col_n
    chunk = 256 if col_size % 256 == 0 else 384 if col_size % 384 == 0 else 128
    strip = 256 if own_size % 256 == 0 else 128
    first = prev is None
    if last:
        out_shape = [jax.ShapeDtypeStruct((emb + TAIL, width), f32)] * own_n
        out_shape.append(jax.ShapeDtypeStruct((peers, 128), f32))
    else:
        out_shape = [
            jax.ShapeDtypeStruct((emb, own_size), f32),
            jax.ShapeDtypeStruct((24, own_size), f32),
        ]
    if first:
        out_shape.append(jax.ShapeDtypeStruct((4 * emb, own_size), bf16))
        out_shape.append(jax.ShapeDtypeStruct((GEO, 2 * own_size), bf16))
    pairs = own_size * col_size
    tile = (chunk, strip)
    made = pl.pallas_call(
        functools.partial(
            pair_kernel, own_n, col_n, chunk, strip, 32, first, last, weight_scale
        ),
        out_shape=out_shape,
        scratch_shapes=[
            pltpu.VMEM((col_size, 4 * emb), bf16),
            pltpu.VMEM((col_size, GEO), bf16),
            pltpu.VMEM((2 * emb, col_size), bf16),
            pltpu.VMEM((24, col_size), bf16),
            pltpu.VMEM((GEO, own_size), f32),
            pltpu.VMEM((GEO, width), f32),
            pltpu.VMEM((emb, own_size), f32),
            pltpu.VMEM((16, own_size), f32),
            pltpu.VMEM((8, own_size), f32),
            pltpu.VMEM((8, own_size), f32),
        ]
        + [pltpu.VMEM(tile, f32)] * 2
        + [pltpu.VMEM((2, *tile), f32)] * 2
        + [pltpu.VMEM(tile, bf16)] * 12,
        compiler_params=pltpu.CompilerParams(vmem_limit_bytes=32 * 2**20),
        cost_estimate=pl.CostEstimate(
            flops=pairs * 12 * emb, bytes_accessed=pairs * 4, transcendentals=3 * pairs
        ),
    )(*own_blocks, *col_blocks, *(() if first else prev))
    return made if last else made[:2] + (made[2:] if first else prev[2:])


def pick(options, index):
    chosen = options[0]
    for n in range(1, len(options)):
        chosen = jnp.where(index == n, options[n], chosen)
    return chosen


def on_device(positions, embeddings, visible):
    frames_local, emb, width = embeddings.shape
    track_n, tm_n = lax.axis_size("track"), lax.axis_size("tm")
    tracks, frames = width * track_n, frames_local * tm_n
    weight_scale = rigidity / math.sqrt(tracks)
    team = 2 * frames_local
    teams = track_n // team

    def homes():
        for track in range(track_n):
            for tm in range(tm_n):
                yield track, tm

    def worker(track, tm, turn, shift):
        crew, member = divmod(track, team)
        frame = (turn + member) % frames_local
        core = tm % 2
        to_track = (crew + shift) % teams * team + core * frames_local + frame
        return to_track * tm_n + (tm - core + member // frames_local), frame

    def outward(turn, shift):
        return [(t * tm_n + m, worker(t, m, turn, shift)[0]) for t, m in homes()]

    def inward(turn):
        return [(worker(t, m, turn, 0)[0], t * tm_n + m) for t, m in homes()]

    def inward_next(turn):
        pairs = []
        for t, m in homes():
            at, frame = worker(t, m, turn, 0)
            if frame == frames_local - 1 and m + 1 < tm_n:
                pairs.append((at, t * tm_n + m + 1))
        return pairs

    swap = [(t * tm_n + m, t * tm_n + (m ^ 1)) for t, m in homes()]
    member = lax.rem(lax.axis_index("track"), team)
    turns = range(frames_local)

    seen = visible.astype(f32)
    rows = jnp.concatenate([positions, seen[None]], 0)
    following = lax.ppermute(rows[:, 0], "tm", [(i, i - 1) for i in range(1, tm_n)])
    rows = jnp.concatenate([rows, following[:, None]], 1)
    blocks = []
    for k in turns:
        blocks.append(
            jnp.concatenate(
                [
                    embeddings[k],
                    rows[:3, k],
                    rows[:3, k + 1],
                    rows[3:, k] * rows[3:, k + 1],
                    jnp.zeros((1, width), f32),
                ],
                0,
            )
        )
    sent = [pick(blocks, lax.rem(member + turn, frames_local)) for turn in turns]
    sent = lax.optimization_barrier(sent)
    arrived = [
        [lax.ppermute(sent[turn], AXES, outward(turn, shift)) for turn in turns]
        for shift in range(teams)
    ]

    def across(values):
        return [lax.ppermute(v, AXES, swap) for v in values]

    own = arrived[0]
    terms = functools.partial(pair_terms, own, peers=track_n * tm_n, weight_scale=weight_scale)
    beside = across(own)
    totals = terms(own, None, False)
    far = [v for shift in range(1, teams) for v in arrived[shift]]
    ready = beside
    for part in far[:-1]:
        part, totals = lax.optimization_barrier((part, totals))
        following = [part] + across([part])
        totals = terms(ready, totals, False)
        ready = following
    if far:
        totals = terms(ready, totals, False)
        part, totals = lax.optimization_barrier((far[-1], totals))
        ready = across([part])
        totals = terms([part], totals, False)
    totals = terms(ready, totals, True)

    back = [lax.ppermute(totals[turn], AXES, inward(turn)) for turn in turns]
    late = [lax.ppermute(totals[turn][emb:], AXES, inward_next(turn)) for turn in turns]
    shares = lax.all_to_all(totals[frames_local], AXES, 0, 0, tiled=True)
    total = jnp.sum(shares[:, :1]) * 0.25
    mean_loss = total / (tracks * (tracks - 1) / 2.0 * (frames - 1))

    of_frame = [
        pick(back, lax.rem(k - member + team * frames_local, frames_local)) for k in turns
    ]
    grad_emb = jnp.stack([v[:emb] for v in of_frame])
    from_before = sum(v[3:6] for v in late)
    grad_pos = []
    for k in turns:
        extra = from_before if k == 0 else of_frame[k - 1][emb + 3 : emb + 6]
        grad_pos.append(of_frame[k][emb : emb + 3] + extra)
    return (jnp.stack(grad_pos, 1), grad_emb, mean_loss)


def solution(mesh):
    in_specs = (P(None, "tm", "track"), P("tm", None, "track"), P("tm", "track"))
    out_specs = (P(None, "tm", "track"), P("tm", None, "track"), P())
    return jax.shard_map(
        on_device, mesh=mesh, in_specs=in_specs, out_specs=out_specs, check_vma=False
    )
```

time: 67.8 us -> 60.1 us (0.89)
  Pallas kernels: 24.9 us -> 15.1 us
  starting transfers between devices: 23.9 us -> 25.1 us
  waiting for transfers between devices: 11.5 us -> 12.5 us
    pallas_call x5, Pallas kernels: 24.9 us -> 15.1 us  [pair_terms(): pl.pallas_call(functools.partial(pair_kernel, own_n, col_n, chunk, strip,...]
    ppermute x2, starting transfers between devices: 6.88 us -> 3.68 us  [on_device(): back = [lax.ppermute(totals[turn], AXES, inward(turn)) for turn in turns]]
    ppermute x4, starting transfers between devices: 0.84 us -> 3.88 us  [across(): return [lax.ppermute(v, AXES, swap) for v in values]]
    all_to_all x1, starting transfers between devices: 2.29 us -> 3.65 us  [on_device(): shares = lax.all_to_all(totals[frames_local], AXES, 0, 0, tiled=True)]
  transfers between devices with their start and end apart: 14 -> 14, of which waited for: 4 -> 5; matrix products, arithmetic and copies ran while one was open for 3% -> 3% of each run, Pallas kernels for 32% -> 22%
where the time goes in v3:
time: 60.1 us; the launch traced here: 59.2 us
  starting transfers between devices  25.1 us (42%)
  Pallas kernels  15.1 us (25%)
  waiting for transfers between devices  12.5 us (21%)
  between operations  2.64 us (4%)
  local copies, waits for them, and re-layouts  2.49 us (4%)
  other arithmetic  1.47 us (2%)
    pallas_call x5, Pallas kernels, pair_terms(): pl.pallas_call(functools.partial(pair_kernel, own_n, col_n, chunk, strip,...  15.1 us
    ppermute x4, starting transfers between devices, on_device(): lax.ppermute(sent[turn], AXES, outward(turn, shift))  9.94 us
    ppermute x4, waiting for transfers between devices, on_device(): lax.ppermute(sent[turn], AXES, outward(turn, shift))  4.96 us
    all_to_all x1, waiting for transfers between devices, on_device(): shares = lax.all_to_all(totals[frames_local], AXES, 0, 0, tiled=True)  4.69 us
    ppermute x4, starting transfers between devices, across(): return [lax.ppermute(v, AXES, swap) for v in values]  3.88 us
    ppermute x2, starting transfers between devices, on_device(): back = [lax.ppermute(totals[turn], AXES, inward(turn)) for turn in turns]  3.68 us
    all_to_all x1, starting transfers between devices, on_device(): shares = lax.all_to_all(totals[frames_local], AXES, 0, 0, tiled=True)  3.65 us
    ppermute x1, waiting for transfers between devices, on_device(): lax.ppermute(rows[:, 0], 'tm', [(i, i - 1) for i in range(1, tm_n)])  2.78 us
  transfers between devices with their start and end apart: 14, of which 5 were waited for; matrix products, arithmetic and copies ran while one was open for 3% of the time, Pallas kernels for 22%

profile of v3, /device:TPU:1, one launch (start us, length us, event | category | flops | bytes accessed | tf_op | source)
XLA Modules:
  0.0 59.2 jit_solution(554767196893467857)
XLA Ops:
  0.6 0.0 copy-start
  0.6 0.7 %copy.10 = f32[3,2,384]{2,0,1:T(4,128)S(1)} copy(f32[3,2,384]{2,1,0:T(2,128)} %param.3) | data formatting | bytes 18432 | tf_op args[0]
  1.3 0.0 copy-done
  1.4 2.0 %collective-permute-start = (f32[4,384]{1,0:T(4,128)S(1)}, f32[4,384]{1,0:T(4,128)S(1)}, u32[]{:S(2)}, u32[]{:S(2)}) collective-permute-start(f32[4,384]{1,0:T(4,128)S(1)} %fusion.3), channel_id=1, source_target_pairs={{1,0},{2,1},{3,2},{5,4},{6,5},{7,6},{9,8},{10,9},{11,10},{13,12},{... | collective-permute-start | bytes 18440 | tf_op jit(solution)/shard_map/ppermute | solution.py:292
  3.4 1.1 %slice_bitcast_fusion.2 = (f32[128,384]{1,0:T(8,128)S(1)}, f32[128,384]{1,0:T(8,128)S(1)}) fusion(f32[2,128,384]{2,1,0:T(8,128)} %param.4), kind=kLoop, calls=%fused_computation.3 | loop fusion | bytes 786432 | tf_op jit(solution)/shard_map/squeeze | solution.py:299
  4.5 2.8 %collective-permute-done = f32[4,384]{1,0:T(4,128)S(1)} collective-permute-done((f32[4,384]{1,0:T(4,128)S(1)}, f32[4,384]{1,0:T(4,128)S(1)}, u32[]{:S(2)}, u32[]{:S(2)}) %collective-permute-start) | collective-permute-done | bytes 6176 | tf_op jit(solution)/shard_map/ppermute | solution.py:292
  7.4 1.9 %collective-permute-start.1 = (f32[136,384]{1,0:T(8,128)S(1)}, f32[136,384]{1,0:T(8,128)S(1)}, u32[]{:S(2)}, u32[]{:S(2)}) collective-permute-start(f32[136,384]{1,0:T(8,128)S(1)} %get-tuple-element.28), channel_id=1, source_target_pairs={{0,0},{1,8},{2,2},{3,10},{4,4},{5,12},{6,6},{7,14},{8,1},{9,9},{10... | collective-permute-start | bytes 626696 | tf_op jit(solution)/shard_map/ppermute | solution.py:311
  9.3 2.7 %collective-permute-start.2 = (f32[136,384]{1,0:T(8,128)S(1)}, f32[136,384]{1,0:T(8,128)S(1)}, u32[]{:S(2)}, u32[]{:S(2)}) collective-permute-start(f32[136,384]{1,0:T(8,128)S(1)} %get-tuple-element.29), channel_id=1, source_target_pairs={{0,4},{1,12},{2,6},{3,14},{4,0},{5,8},{6,2},{7,10},{8,5},{9,13},{1... | collective-permute-start | bytes 626696 | tf_op jit(solution)/shard_map/ppermute | solution.py:311
  12.0 2.0 %collective-permute-start.4 = (f32[136,384]{1,0:T(8,128)S(1)}, f32[136,384]{1,0:T(8,128)S(1)}, u32[]{:S(2)}, u32[]{:S(2)}) collective-permute-start(f32[136,384]{1,0:T(8,128)S(1)} %get-tuple-element.28), channel_id=1, source_target_pairs={{0,16},{1,24},{2,18},{3,26},{4,20},{5,28},{6,22},{7,30},{8,17},{9,... | collective-permute-start | bytes 626696 | tf_op jit(solution)/shard_map/ppermute | solution.py:311
  14.1 2.5 %collective-permute-done.1.refs_0_.refs_2_ = f32[136,384]{1,0:T(8,128)S(1)} collective-permute-done((f32[136,384]{1,0:T(8,128)S(1)}, f32[136,384]{1,0:T(8,128)S(1)}, u32[]{:S(2)}, u32[]{:S(2)}) %collective-permute-start.1) | collective-permute-done | bytes 208928 | tf_op jit(solution)/shard_map/ppermute | solution.py:311
  16.6 0.0 collective-permute-start.6
  16.6 1.9 %collective-permute-done.2.refs_1_.refs_3_ = f32[136,384]{1,0:T(8,128)S(1)} collective-permute-done((f32[136,384]{1,0:T(8,128)S(1)}, f32[136,384]{1,0:T(8,128)S(1)}, u32[]{:S(2)}, u32[]{:S(2)}) %collective-permute-start.2) | collective-permute-done | bytes 208928 | tf_op jit(solution)/shard_map/ppermute | solution.py:311
  18.4 0.0 collective-permute-start.7
  18.5 3.6 %shard_map.58 = (f32[128,768]{1,0:T(8,128)S(1)}, f32[24,768]{1,0:T(8,128)S(1)}, bf16[512,768]{1,0:T(8,128)(2,1)S(1)}, bf16[128,1536]{1,0:T(8,128)(2,1)S(1)}) custom-call(f32[136,384]{1,0:T(8,128)S(1)} %collective-permute-done.1.refs_0_.refs_2_, f32[136,384]{1,0:T(8,128)S(1)} %collective-permute-done.2.refs_1_.refs_3_, ...), custom_call_target="tpu_custom_call" | custom-call | flops 905969664 | bytes 2359296 | tf_op jit(solution)/shard_map/pallas_call | solution.py:217
  22.0 0.6 collective-permute-done.4.refs_2_
  22.6 0.0 collective-permute-start.5
  22.6 3.3 %collective-permute-start.3 = (f32[136,384]{1,0:T(8,128)S(1)}, f32[136,384]{1,0:T(8,128)S(1)}, u32[]{:S(2)}, u32[]{:S(2)}) collective-permute-start(f32[136,384]{1,0:T(8,128)S(1)} %get-tuple-element.29), channel_id=1, source_target_pairs={{0,20},{1,28},{2,22},{3,30},{4,16},{5,24},{6,18},{7,26},{8,21},{9,... | collective-permute-start | bytes 626696 | tf_op jit(solution)/shard_map/ppermute | solution.py:311
  25.9 0.0 collective-permute-done.6.refs_2_
  25.9 0.0 collective-permute-done.7.refs_3_
  25.9 3.5 %shard_map.59 = (f32[128,768]{1,0:T(8,128)S(1)}, f32[24,768]{1,0:T(8,128)S(1)}) custom-call(f32[136,384]{1,0:T(8,128)S(1)} %collective-permute-done.1.refs_0_.refs_2_, f32[136,384]{1,0:T(8,128)S(1)} %collective-permute-done.2.refs_1_.refs_3_, f32[136,384]{1,0:T(8,128)S(1)} %collective-permute-done.6.refs_2_, f32[136,384]{1,0:T(8,128)S(1)} %collective-permute-done.7.refs_3_, ...), custom_call_target="tpu_custom_call" | custom-call | flops 905969664 | bytes 2359296 | tf_op jit(solution)/shard_map/pallas_call | solution.py:217
  29.4 0.0 collective-permute-done.5.refs_3_
  29.4 3.5 %shard_map.60 = (f32[128,768]{1,0:T(8,128)S(1)}, f32[24,768]{1,0:T(8,128)S(1)}) custom-call(f32[136,384]{1,0:T(8,128)S(1)} %collective-permute-done.1.refs_0_.refs_2_, f32[136,384]{1,0:T(8,128)S(1)} %collective-permute-done.2.refs_1_.refs_3_, f32[136,384]{1,0:T(8,128)S(1)} %collective-permute-done.4.refs_2_, f32[136,384]{1,0:T(8,128)S(1)} %collective-permute-done.5.refs_3_, ...), custom_call_target="tpu_custom_call" | custom-call | flops 905969664 | bytes 2359296 | tf_op jit(solution)/shard_map/pallas_call | solution.py:217
  32.9 0.0 collective-permute-done.3.refs_2_
  32.9 3.9 %collective-permute-start.8 = (f32[136,384]{1,0:T(8,128)S(1)}, f32[136,384]{1,0:T(8,128)S(1)}, u32[]{:S(2)}, u32[]{:S(2)}) collective-permute-start(f32[136,384]{1,0:T(8,128)S(1)} %collective-permute-done.3.refs_2_), channel_id=1, source_target_pairs={{0,1},{1,0},{2,3},{3,2},{4,5},{5,4},{6,7},{7,6},{8,9},{9,8},{10,11... | collective-permute-start | bytes 626696 | tf_op jit(solution)/shard_map/ppermute | solution.py:316
  36.7 2.2 %shard_map.61 = (f32[128,768]{1,0:T(8,128)S(1)}, f32[24,768]{1,0:T(8,128)S(1)}) custom-call(f32[136,384]{1,0:T(8,128)S(1)} %collective-permute-done.1.refs_0_.refs_2_, f32[136,384]{1,0:T(8,128)S(1)} %collective-permute-done.2.refs_1_.refs_3_, f32[136,384]{1,0:T(8,128)S(1)} %collective-permute-done.3.refs_2_, f32[128,768]{1,0:T(8,128)S(1)} %get-tuple-element.44.refs_3_, ...), custom_call_target="tpu_custom_call" | custom-call | flops 452984832 | bytes 1179648 | tf_op jit(solution)/shard_map/pallas_call | solution.py:217
  38.9 0.0 collective-permute-done.8.refs_2_
  38.9 2.3 %shard_map.62 = (f32[136,384]{1,0:T(8,128)S(1)}, f32[136,384]{1,0:T(8,128)S(1)}, f32[32,128]{1,0:T(8,128)}) custom-call(f32[136,384]{1,0:T(8,128)S(1)} %collective-permute-done.1.refs_0_.refs_2_, f32[136,384]{1,0:T(8,128)S(1)} %collective-permute-done.2.refs_1_.refs_3_, f32[136,384]{1,0:T(8,128)S(1)} %collective-permute-done.8.refs_2_, ...), custom_call_target="tpu_custom_call" | custom-call | flops 452984832 | bytes 1179648 | tf_op jit(solution)/shard_map/pallas_call | solution.py:217
  41.3 1.9 %collective-permute-start.10 = (f32[136,384]{1,0:T(8,128)S(1)}, f32[136,384]{1,0:T(8,128)S(1)}, u32[]{:S(2)}, u32[]{:S(2)}) collective-permute-start(f32[136,384]{1,0:T(8,128)S(1)} %get-tuple-element.51), channel_id=1, source_target_pairs={{0,0},{8,1},{2,2},{10,3},{4,4},{12,5},{6,6},{14,7},{1,8},{9,9},{3,... | collective-permute-start | bytes 626696 | tf_op jit(solution)/shard_map/ppermute | solution.py:336
  43.2 1.8 %collective-permute-start.9 = (f32[136,384]{1,0:T(8,128)S(1)}, f32[136,384]{1,0:T(8,128)S(1)}, u32[]{:S(2)}, u32[]{:S(2)}) collective-permute-start(f32[136,384]{1,0:T(8,128)S(1)} %get-tuple-element.50), channel_id=1, source_target_pairs={{4,0},{12,1},{6,2},{14,3},{0,4},{8,5},{2,6},{10,7},{5,8},{13,9},{7... | collective-permute-start | bytes 626696 | tf_op jit(solution)/shard_map/ppermute | solution.py:336
  45.0 3.7 %all-to-all-start = ((f32[32,1,128]{2,1,0:T(1,128)}), f32[32,1,128]{2,1,0:T(1,128)S(1)}, u32[]{:S(2)}, u32[]{:S(2)}) async-start(f32[32,1,128]{2,1,0:T(1,128)} %bitcast.12), calls=%async_computation | async-start | bytes 32768 | tf_op jit(solution)/shard_map/all_to_all | solution.py:338
  48.6 0.7 %collective-permute-start.11 = (f32[8,384]{1,0:T(8,128)S(1)}, f32[8,384]{1,0:T(8,128)S(1)}, u32[]{:S(2)}, u32[]{:S(2)}) collective-permute-start(f32[8,384]{1,0:T(8,128)S(1)} %slice.71), channel_id=1, source_target_pairs={{4,5},{12,6},{6,7},{5,13},{13,14},{7,15},{20,21},{28,22},{22,23},{... | collective-permute-start | bytes 36872 | tf_op jit(solution)/shard_map/ppermute | solution.py:337
  49.3 1.3 %collective-permute-start.12 = (f32[8,384]{1,0:T(8,128)S(1)}, f32[8,384]{1,0:T(8,128)S(1)}, u32[]{:S(2)}, u32[]{:S(2)}) collective-permute-start(f32[8,384]{1,0:T(8,128)S(1)} %slice.73), channel_id=1, source_target_pairs={{4,1},{12,2},{6,3},{5,9},{13,10},{7,11},{20,17},{28,18},{22,19},{2... | collective-permute-start | bytes 36872 | tf_op jit(solution)/shard_map/ppermute | solution.py:337
  50.6 4.7 %all-to-all-done = f32[32,1,128]{2,1,0:T(1,128)S(1)} async-done(((f32[32,1,128]{2,1,0:T(1,128)}), f32[32,1,128]{2,1,0:T(1,128)S(1)}, u32[]{:S(2)}, u32[]{:S(2)}) %all-to-all-start) | async-done | bytes 16416 | tf_op jit(solution)/shard_map/all_to_all | solution.py:338
  55.3 0.6 %slice_reduce_fusion = f32[]{:T(128)} fusion(f32[32,128]{1,0:T(8,128)S(1)} %bitcast.33), kind=kLoop, calls=%fused_computation.9 | loop fusion | flops 31 | bytes 132 | tf_op jit(solution)/shard_map/reduce_sum | solution.py:339
  56.6 0.0 collective-permute-done.10
  56.6 0.0 collective-permute-done.9
  56.7 0.0 collective-permute-done.11
  56.7 0.0 collective-permute-done.12
  56.7 0.6 %copy.14 = f32[3,2,384]{2,1,0:T(2,128)} copy(f32[3,2,384]{2,0,1:T(4,128)S(1)} %pad_maximum_fusion.1) | data formatting | bytes 18432
  57.3 0.8 %pad_maximum_fusion = f32[2,128,384]{2,1,0:T(8,128)} fusion(f32[1,128,384]{2,1,0:T(8,128)S(1)} %get-tuple-element.71, f32[1,128,384]{2,1,0:T(8,128)S(1)} %get-tuple-element.72), kind=kLoop, calls=%fused_computation | loop fusion | flops 98304 | bytes 786432 | tf_op jit(solution)/shard_map/stack | solution.py:345
  (15 shorter events, 0.2 us)
Async XLA Ops:
  0.6 0.7 %copy-start = (s32[2,384]{1,0:T(2,128)S(1)}, s32[2,384]{1,0:T(2,128)}, u32[]{:S(2)}) copy-start(s32[2,384]{1,0:T(2,128)} %param.5) | copy-start | bytes 9220
  1.4 5.8 %collective-permute-start = (f32[4,384]{1,0:T(4,128)S(1)}, f32[4,384]{1,0:T(4,128)S(1)}, u32[]{:S(2)}, u32[]{:S(2)}) collective-permute-start(f32[4,384]{1,0:T(4,128)S(1)} %fusion.3), channel_id=1, source_target_pairs={{1,0},{2,1},{3,2},{5,4},{6,5},{7,6},{9,8},{10,9},{11,10},{13,12},{... | collective-permute-start | bytes 18440 | tf_op jit(solution)/shard_map/ppermute | solution.py:292
  7.4 9.2 %collective-permute-start.1 = (f32[136,384]{1,0:T(8,128)S(1)}, f32[136,384]{1,0:T(8,128)S(1)}, u32[]{:S(2)}, u32[]{:S(2)}) collective-permute-start(f32[136,384]{1,0:T(8,128)S(1)} %get-tuple-element.28), channel_id=1, source_target_pairs={{0,0},{1,8},{2,2},{3,10},{4,4},{5,12},{6,6},{7,14},{8,1},{9,9},{10... | collective-permute-start | bytes 626696 | tf_op jit(solution)/shard_map/ppermute | solution.py:311
  9.3 9.2 %collective-permute-start.2 = (f32[136,384]{1,0:T(8,128)S(1)}, f32[136,384]{1,0:T(8,128)S(1)}, u32[]{:S(2)}, u32[]{:S(2)}) collective-permute-start(f32[136,384]{1,0:T(8,128)S(1)} %get-tuple-element.29), channel_id=1, source_target_pairs={{0,4},{1,12},{2,6},{3,14},{4,0},{5,8},{6,2},{7,10},{8,5},{9,13},{1... | collective-permute-start | bytes 626696 | tf_op jit(solution)/shard_map/ppermute | solution.py:311
  12.0 10.6 %collective-permute-start.4 = (f32[136,384]{1,0:T(8,128)S(1)}, f32[136,384]{1,0:T(8,128)S(1)}, u32[]{:S(2)}, u32[]{:S(2)}) collective-permute-start(f32[136,384]{1,0:T(8,128)S(1)} %get-tuple-element.28), channel_id=1, source_target_pairs={{0,16},{1,24},{2,18},{3,26},{4,20},{5,28},{6,22},{7,30},{8,17},{9,... | collective-permute-start | bytes 626696 | tf_op jit(solution)/shard_map/ppermute | solution.py:311
  16.6 9.3 %collective-permute-start.6 = (f32[136,384]{1,0:T(8,128)S(1)}, f32[136,384]{1,0:T(8,128)S(1)}, u32[]{:S(2)}, u32[]{:S(2)}) collective-permute-start(f32[136,384]{1,0:T(8,128)S(1)} %collective-permute-done.1.refs_0_.refs_2_), channel_id=1, source_target_pairs={{0,1},{1,0},{2,3},{3,2},{4,5},{5,4},{6,7},{7,6},{8,9},{9,8},{10,11... | collective-permute-start | bytes 626696 | tf_op jit(solution)/shard_map/ppermute | solution.py:316
  18.4 7.4 %collective-permute-start.7 = (f32[136,384]{1,0:T(8,128)S(1)}, f32[136,384]{1,0:T(8,128)S(1)}, u32[]{:S(2)}, u32[]{:S(2)}) collective-permute-start(f32[136,384]{1,0:T(8,128)S(1)} %collective-permute-done.2.refs_1_.refs_3_), channel_id=1, source_target_pairs={{0,1},{1,0},{2,3},{3,2},{4,5},{5,4},{6,7},{7,6},{8,9},{9,8},{10,11... | collective-permute-start | bytes 626696 | tf_op jit(solution)/shard_map/ppermute | solution.py:316
  22.6 6.8 %collective-permute-start.5 = (f32[136,384]{1,0:T(8,128)S(1)}, f32[136,384]{1,0:T(8,128)S(1)}, u32[]{:S(2)}, u32[]{:S(2)}) collective-permute-start(f32[136,384]{1,0:T(8,128)S(1)} %collective-permute-done.4.refs_2_), channel_id=1, source_target_pairs={{0,1},{1,0},{2,3},{3,2},{4,5},{5,4},{6,7},{7,6},{8,9},{9,8},{10,11... | collective-permute-start | bytes 626696 | tf_op jit(solution)/shard_map/ppermute | solution.py:316
  22.6 10.3 %collective-permute-start.3 = (f32[136,384]{1,0:T(8,128)S(1)}, f32[136,384]{1,0:T(8,128)S(1)}, u32[]{:S(2)}, u32[]{:S(2)}) collective-permute-start(f32[136,384]{1,0:T(8,128)S(1)} %get-tuple-element.29), channel_id=1, source_target_pairs={{0,20},{1,28},{2,22},{3,30},{4,16},{5,24},{6,18},{7,26},{8,21},{9,... | collective-permute-start | bytes 626696 | tf_op jit(solution)/shard_map/ppermute | solution.py:311
  32.9 6.1 %collective-permute-start.8 = (f32[136,384]{1,0:T(8,128)S(1)}, f32[136,384]{1,0:T(8,128)S(1)}, u32[]{:S(2)}, u32[]{:S(2)}) collective-permute-start(f32[136,384]{1,0:T(8,128)S(1)} %collective-permute-done.3.refs_2_), channel_id=1, source_target_pairs={{0,1},{1,0},{2,3},{3,2},{4,5},{5,4},{6,7},{7,6},{8,9},{9,8},{10,11... | collective-permute-start | bytes 626696 | tf_op jit(solution)/shard_map/ppermute | solution.py:316
  41.3 15.3 %collective-permute-start.10 = (f32[136,384]{1,0:T(8,128)S(1)}, f32[136,384]{1,0:T(8,128)S(1)}, u32[]{:S(2)}, u32[]{:S(2)}) collective-permute-start(f32[136,384]{1,0:T(8,128)S(1)} %get-tuple-element.51), channel_id=1, source_target_pairs={{0,0},{8,1},{2,2},{10,3},{4,4},{12,5},{6,6},{14,7},{1,8},{9,9},{3,... | collective-permute-start | bytes 626696 | tf_op jit(solution)/shard_map/ppermute | solution.py:336
  43.2 13.4 %collective-permute-start.9 = (f32[136,384]{1,0:T(8,128)S(1)}, f32[136,384]{1,0:T(8,128)S(1)}, u32[]{:S(2)}, u32[]{:S(2)}) collective-permute-start(f32[136,384]{1,0:T(8,128)S(1)} %get-tuple-element.50), channel_id=1, source_target_pairs={{4,0},{12,1},{6,2},{14,3},{0,4},{8,5},{2,6},{10,7},{5,8},{13,9},{7... | collective-permute-start | bytes 626696 | tf_op jit(solution)/shard_map/ppermute | solution.py:336
  45.0 10.4 %all-to-all-start = ((f32[32,1,128]{2,1,0:T(1,128)}), f32[32,1,128]{2,1,0:T(1,128)S(1)}, u32[]{:S(2)}, u32[]{:S(2)}) async-start(f32[32,1,128]{2,1,0:T(1,128)} %bitcast.12), calls=%async_computation | async-start | bytes 32768 | tf_op jit(solution)/shard_map/all_to_all | solution.py:338
  48.6 8.0 %collective-permute-start.11 = (f32[8,384]{1,0:T(8,128)S(1)}, f32[8,384]{1,0:T(8,128)S(1)}, u32[]{:S(2)}, u32[]{:S(2)}) collective-permute-start(f32[8,384]{1,0:T(8,128)S(1)} %slice.71), channel_id=1, source_target_pairs={{4,5},{12,6},{6,7},{5,13},{13,14},{7,15},{20,21},{28,22},{22,23},{... | collective-permute-start | bytes 36872 | tf_op jit(solution)/shard_map/ppermute | solution.py:337
  49.3 7.4 %collective-permute-start.12 = (f32[8,384]{1,0:T(8,128)S(1)}, f32[8,384]{1,0:T(8,128)S(1)}, u32[]{:S(2)}, u32[]{:S(2)}) collective-permute-start(f32[8,384]{1,0:T(8,128)S(1)} %slice.73), channel_id=1, source_target_pairs={{4,1},{12,2},{6,3},{5,9},{13,10},{7,11},{20,17},{28,18},{22,19},{2... | collective-permute-start | bytes 36872 | tf_op jit(solution)/shard_map/ppermute | solution.py:337

commit v4 on v3

--- a/solution.py
+++ b/solution.py
@@ -57,7 +57,7 @@
     return start, end
 
 
-def pair_kernel(own_n, col_n, chunk, strip, rows, first, last, weight_scale, *refs):
+def pair_kernel(own_n, col_n, chunk, rows, first, home, lanes, energy, weight_scale, *refs):
     refs = list(refs)
 
     def take(count):
@@ -68,7 +68,7 @@
     own_blocks, col_blocks = take(own_n), take(col_n)
     prev = take(0 if first else 2)
     kept = take(0 if first else 2)
-    outs = take(own_n + 1 if last else 2)
+    outs = take(2 if home is None else len(home) + (energy is not None))
     if first:
         kept = take(2)
     weights, geo_weights = kept
@@ -127,45 +127,49 @@
         energies[...] = prev[1][16:24, :]
 
     def products(n, i, k):
-        cols, at = pl.ds(n * chunk, chunk), slice(i * strip, (i + 1) * strip)
-        logits[k][...] = jnp.dot(lhs[cols, :], weights[:, at], preferred_element_type=f32)
+        cols, at = pl.ds(n * chunk, chunk), slice(*i)
+        size = i[1] - i[0]
+        logits[k][:, :size] = jnp.dot(lhs[cols, :], weights[:, at], preferred_element_type=f32)
         side = geo_lhs[cols, :]
-        geo[k][0] = jnp.dot(side, geo_weights[:, at], preferred_element_type=f32)
-        at = slice(own_size + i * strip, own_size + (i + 1) * strip)
-        geo[k][1] = jnp.dot(side, geo_weights[:, at], preferred_element_type=f32)
+        geo[k][0, :, :size] = jnp.dot(side, geo_weights[:, at], preferred_element_type=f32)
+        at = slice(own_size + i[0], own_size + i[1])
+        geo[k][1, :, :size] = jnp.dot(side, geo_weights[:, at], preferred_element_type=f32)
 
     def elementwise(n, i, k):
-        mine = slice(i * strip, (i + 1) * strip)
-        total = energies[:, mine]
+        mine, size = slice(*i), i[1] - i[0]
+        total = jnp.zeros((8, size), f32)
         for b in range(0, chunk, rows):
             at = slice(b, b + rows)
-            sq0, growth = geo[k][0, at, :], geo[k][1, at, :]
+            sq0, growth = geo[k][0, at, :size], geo[k][1, at, :size]
             sq1 = sq0 + growth
             inv0, inv1 = lax.rsqrt(sq0), lax.rsqrt(sq1)
             both = sq1 * inv1 + sq0 * inv0
             change = growth * lax.rsqrt(both * both)
-            tanh = jnp.tanh(logits[k][at, :])
+            tanh = jnp.tanh(logits[k][at, :size])
             pull = change + change * tanh
-            energy = pull * change
-            g_high[k][at, :], g_low[k][at, :] = split(energy - energy * tanh)
-            pulls[k][0][at, :], pulls[k][1][at, :] = split(pull * inv0)
-            pulls[k][2][at, :], pulls[k][3][at, :] = split(pull * inv1)
-            total = total + energy.reshape(rows // 8, 8, strip).sum(0)
-        energies[:, mine] = total
+            value = pull * change
+            g_high[k][at, :size], g_low[k][at, :size] = split(value - value * tanh)
+            pulls[k][0][at, :size], pulls[k][1][at, :size] = split(pull * inv0)
+            pulls[k][2][at, :size], pulls[k][3][at, :size] = split(pull * inv1)
+            total = total + value.reshape(rows // 8, 8, size).sum(0)
+        if energy is not None:
+            column = lax.broadcasted_iota(jnp.int32, (8, size), 1) + i[0]
+            factor = jnp.where(column >= energy, 2.0, 1.0) if energy < i[1] else 1.0
+            energies[:, mine] += total * factor
 
     def gradients(n, i, k):
-        cols, at = pl.ds(n * chunk, chunk), slice(i * strip, (i + 1) * strip)
-        two = jnp.dot(emb_split[:, cols], g_high[k][...], preferred_element_type=f32)
-        one = jnp.dot(emb_split[0:emb, cols], g_low[k][...], preferred_element_type=f32)
+        cols, at, size = pl.ds(n * chunk, chunk), slice(*i), i[1] - i[0]
+        two = jnp.dot(emb_split[:, cols], g_high[k][:, :size], preferred_element_type=f32)
+        one = jnp.dot(emb_split[0:emb, cols], g_low[k][:, :size], preferred_element_type=f32)
         grad[:, at] += two[:emb] + two[emb:] + one
         side = pts_split[:, cols]
         for frame in range(2):
             high, low = pulls[k][2 * frame], pulls[k][2 * frame + 1]
-            moved = jnp.dot(side, high[...], preferred_element_type=f32)
-            moved = moved + jnp.dot(side, low[...], preferred_element_type=f32)
+            moved = jnp.dot(side, high[:, :size], preferred_element_type=f32)
+            moved = moved + jnp.dot(side, low[:, :size], preferred_element_type=f32)
             sums[8 * frame : 8 * frame + 8, at] += moved[:8] + moved[8:16] + moved[16:]
 
-    tiles = [(n, i) for n in range(col_size // chunk) for i in range(own_size // strip)]
+    tiles = [(n, i) for n in range(col_size // chunk) for i in lanes]
     products(*tiles[0], 0)
     for t, (n, i) in enumerate(tiles):
         if t + 1 < len(tiles):
@@ -173,50 +177,56 @@
         elementwise(n, i, t % 2)
         gradients(n, i, t % 2)
 
-    if not last:
+    if home is None:
         outs[0][...] = grad[...]
         outs[1][0:16, :] = sums[...]
         outs[1][16:24, :] = energies[...]
         return
-    seen = own[6:7, :] * weight_scale
-    scale = seen * (0.25 * inv_root)
-    start, end = own[0:3, :] - centre[0:3], own[3:6, :] - centre[3:6]
-    from_start = (sums[0:3, :] - start * sums[6:7, :]) * seen
-    from_end = (end * sums[14:15, :] - sums[11:14, :]) * seen
-    for a in range(own_n):
+    for a, out in zip(home, outs):
         at = slice(a * width, (a + 1) * width)
-        outs[a][0:emb, :] = grad[:, at] * scale[:, at]
-        outs[a][emb : emb + 3, :] = from_start[:, at]
-        outs[a][emb + 3 : emb + 6, :] = from_end[:, at]
-        outs[a][emb + 6 : emb + 8, :] = jnp.zeros((2, width), f32)
-    loss = jnp.sum(energies[...] * own[6:7, :], axis=0, keepdims=True)
-    loss = jnp.sum(loss, axis=1, keepdims=True)
-    outs[own_n][...] = jnp.broadcast_to(loss, outs[own_n].shape)
-
-
-def pair_terms(own_blocks, col_blocks, prev, last, peers, weight_scale):
+        seen = own[6:7, at] * weight_scale
+        start, end = own[0:3, at] - centre[0:3], own[3:6, at] - centre[3:6]
+        out[0:emb, :] = grad[:, at] * (seen * (0.25 * inv_root))
+        out[emb : emb + 3, :] = (sums[0:3, at] - start * sums[6:7, at]) * seen
+        out[emb + 3 : emb + 6, :] = (end * sums[14:15, at] - sums[11:14, at]) * seen
+        out[emb + 6 : emb + 8, :] = jnp.zeros((2, width), f32)
+    if energy is not None:
+        loss = jnp.sum(energies[...] * own[6:7, :], axis=0, keepdims=True)
+        loss = jnp.sum(loss, axis=1, keepdims=True)
+        outs[len(home)][...] = jnp.broadcast_to(loss, outs[len(home)].shape)
+
+
+def pair_terms(
+    own_blocks, col_blocks, prev, weight_scale, peers, home=None, double=None, counted=True
+):
     own_n, col_n = len(own_blocks), len(col_blocks)
     emb, width = own_blocks[0].shape[0] - TAIL, own_blocks[0].shape[1]
     own_size, col_size = width * own_n, width * col_n
     chunk = 256 if col_size % 256 == 0 else 384 if col_size % 384 == 0 else 128
-    strip = 256 if own_size % 256 == 0 else 128
+    low, high = (0, own_size) if home is None else (home[0] * width, (home[-1] + 1) * width)
+    strip = 256 if (high - low) % 256 == 0 else 384 if (high - low) % 384 == 0 else 128
+    lanes = [(i, i + strip) for i in range(low, high, strip)]
+    energy = None
+    if counted:
+        energy = own_size if double is None else double * width
     first = prev is None
-    if last:
-        out_shape = [jax.ShapeDtypeStruct((emb + TAIL, width), f32)] * own_n
-        out_shape.append(jax.ShapeDtypeStruct((peers, 128), f32))
-    else:
+    if home is None:
         out_shape = [
             jax.ShapeDtypeStruct((emb, own_size), f32),
             jax.ShapeDtypeStruct((24, own_size), f32),
         ]
+    else:
+        out_shape = [jax.ShapeDtypeStruct((emb + TAIL, width), f32)] * len(home)
+        if counted:
+            out_shape.append(jax.ShapeDtypeStruct((peers, 128), f32))
     if first:
         out_shape.append(jax.ShapeDtypeStruct((4 * emb, own_size), bf16))
         out_shape.append(jax.ShapeDtypeStruct((GEO, 2 * own_size), bf16))
-    pairs = own_size * col_size
+    pairs = (high - low) * col_size
     tile = (chunk, strip)
-    made = pl.pallas_call(
+    return pl.pallas_call(
         functools.partial(
-            pair_kernel, own_n, col_n, chunk, strip, 32, first, last, weight_scale
+            pair_kernel, own_n, col_n, chunk, 32, first, home, lanes, energy, weight_scale
         ),
         out_shape=out_shape,
         scratch_shapes=[
@@ -236,10 +246,9 @@
         + [pltpu.VMEM(tile, bf16)] * 12,
         compiler_params=pltpu.CompilerParams(vmem_limit_bytes=32 * 2**20),
         cost_estimate=pl.CostEstimate(
-            flops=pairs * 12 * emb, bytes_accessed=pairs * 4, transcendentals=3 * pairs
+            flops=pairs * emb * 100, bytes_accessed=1, transcendentals=0
         ),
     )(*own_blocks, *col_blocks, *(() if first else prev))
-    return made if last else made[:2] + (made[2:] if first else prev[2:])
 
 
 def pick(options, index):
@@ -264,8 +273,8 @@
 
     def worker(track, tm, turn, shift):
         crew, member = divmod(track, team)
+        core = tm % 2
         frame = (turn + member) % frames_local
-        core = tm % 2
         to_track = (crew + shift) % teams * team + core * frames_local + frame
         return to_track * tm_n + (tm - core + member // frames_local), frame
 
@@ -315,40 +324,36 @@
     def across(values):
         return [lax.ppermute(v, AXES, swap) for v in values]
 
-    own = arrived[0]
-    terms = functools.partial(pair_terms, own, peers=track_n * tm_n, weight_scale=weight_scale)
-    beside = across(own)
-    totals = terms(own, None, False)
-    far = [v for shift in range(1, teams) for v in arrived[shift]]
-    ready = beside
-    for part in far[:-1]:
-        part, totals = lax.optimization_barrier((part, totals))
-        following = [part] + across([part])
-        totals = terms(ready, totals, False)
+    own, far = arrived[0], [v for shift in range(1, teams) for v in arrived[shift]]
+    terms = functools.partial(pair_terms, own, weight_scale=weight_scale, peers=track_n * tm_n)
+    ready = across(own)
+    made = terms(own, None)
+    totals, kept = made[:2], made[2:]
+    LOOK = 1
+    for n in range(len(far)):
+        ahead = far[n : n + LOOK]
+        ahead, totals = lax.optimization_barrier((ahead, totals))
+        far[n : n + LOOK] = ahead
+        following = [far[n]] + across([far[n]])
+        totals = terms(ready, [*totals, *kept])
         ready = following
-    if far:
-        totals = terms(ready, totals, False)
-        part, totals = lax.optimization_barrier((far[-1], totals))
-        ready = across([part])
-        totals = terms([part], totals, False)
-    totals = terms(ready, totals, True)
-
-    back = [lax.ppermute(totals[turn], AXES, inward(turn)) for turn in turns]
-    late = [lax.ppermute(totals[turn][emb:], AXES, inward_next(turn)) for turn in turns]
-    shares = lax.all_to_all(totals[frames_local], AXES, 0, 0, tiled=True)
-    total = jnp.sum(shares[:, :1]) * 0.25
-    mean_loss = total / (tracks * (tracks - 1) / 2.0 * (frames - 1))
-
+    *done, loss = terms(ready, [*totals, *kept], home=list(turns))
+    back = [lax.ppermute(done[turn], AXES, inward(turn)) for turn in turns]
+    late = [lax.ppermute(done[turn][emb - 0:], AXES, inward_next(turn))[0:] for turn in turns]
+    shares = lax.all_to_all(loss, AXES, 0, 0, tiled=True)
     of_frame = [
-        pick(back, lax.rem(k - member + team * frames_local, frames_local)) for k in turns
+        pick(back, lax.rem(k - member + 2 * team * frames_local, frames_local)) for k in turns
     ]
     grad_emb = jnp.stack([v[:emb] for v in of_frame])
-    from_before = sum(v[3:6] for v in late)
-    grad_pos = []
-    for k in turns:
-        extra = from_before if k == 0 else of_frame[k - 1][emb + 3 : emb + 6]
-        grad_pos.append(of_frame[k][emb : emb + 3] + extra)
-    return (jnp.stack(grad_pos, 1), grad_emb, mean_loss)
+    before, grad_pos = sum(v[3:6] for v in late), jnp.zeros((3, frames_local, width), f32)
+    frame = lax.broadcasted_iota(jnp.int32, grad_pos.shape, 1)
+    for k, v in enumerate(of_frame):
+        moved = v[emb : emb + 3] + before
+        before = v[emb + 3 : emb + 6]
+        grad_pos = jnp.where(frame == k, moved[:, None, :], grad_pos)
+    shares, grad_emb = lax.optimization_barrier((shares, grad_emb))
+    mean_loss = jnp.sum(shares[:, :1]) * 0.25 / (tracks * (tracks - 1) / 2.0 * (frames - 1))
+    return (grad_pos, grad_emb, mean_loss)
 
 
 def solution(mesh):

time: 60.1 us -> 57.4 us (0.955)
  starting transfers between devices: 25.1 us -> 22.3 us
  other arithmetic: 1.47 us -> 2.15 us
    ppermute x4, starting transfers between devices: 3.88 us -> 0.58 us  [across(): return [lax.ppermute(v, AXES, swap) for v in values]]
    ppermute x4, starting transfers between devices: 9.94 us -> 8.16 us  [on_device(): lax.ppermute(sent[turn], AXES, outward(turn, shift))]
    ppermute x4, starting transfers between devices: 5.63 us -> 7.27 us  [the longest x2 5.31 us: on_device(): back = [lax.ppermute(done[turn], AXES, inward(turn)) for turn in turns]]
    ppermute x4, waiting for transfers between devices: 4.96 us -> 6.04 us  [on_device(): lax.ppermute(sent[turn], AXES, outward(turn, shift))]
    all_to_all x1, waiting for transfers between devices: 4.69 us -> 3.92 us  [on_device(): shares = lax.all_to_all(loss, AXES, 0, 0, tiled=True)]
    all_to_all x1, starting transfers between devices: 3.65 us -> 4.36 us  [on_device(): shares = lax.all_to_all(loss, AXES, 0, 0, tiled=True)]
    select_n x0 -> x1, other arithmetic: none -> 0.67 us  [on_device(): grad_pos = jnp.where(frame == k, moved[:, None, :], grad_pos)]
    unnamed x4 -> x3, local copies, waits for them, and re-layouts: 1.32 us -> 0.71 us
  transfers between devices with their start and end apart: 14 -> 14, of which waited for: 5 -> 5; matrix products, arithmetic and copies ran while one was open for 3% -> 4% of each run, Pallas kernels for 22% -> 19%
where the time goes in v4:
time: 57.4 us; the launch traced here: 56.5 us
  starting transfers between devices  22.3 us (39%)
  Pallas kernels  14.7 us (26%)
  waiting for transfers between devices  12.8 us (22%)
  between operations  2.64 us (5%)
  other arithmetic  2.15 us (4%)
  local copies, waits for them, and re-layouts  1.89 us (3%)
    pallas_call x4, Pallas kernels, pair_terms(): pl.pallas_call(functools.partial(pair_kernel, own_n, col_n, chunk, 32, fi...  14.7 us
    ppermute x4, starting transfers between devices, on_device(): lax.ppermute(sent[turn], AXES, outward(turn, shift))  8.16 us
    ppermute x4, waiting for transfers between devices, on_device(): lax.ppermute(sent[turn], AXES, outward(turn, shift))  6.04 us
    ppermute x2, starting transfers between devices, on_device(): back = [lax.ppermute(done[turn], AXES, inward(turn)) for turn in turns]  5.31 us
    all_to_all x1, starting transfers between devices, on_device(): shares = lax.all_to_all(loss, AXES, 0, 0, tiled=True)  4.36 us
    all_to_all x1, waiting for transfers between devices, on_device(): shares = lax.all_to_all(loss, AXES, 0, 0, tiled=True)  3.92 us
    ppermute x1, waiting for transfers between devices, on_device(): lax.ppermute(rows[:, 0], 'tm', [(i, i - 1) for i in range(1, tm_n)])  2.78 us
    ppermute x1, starting transfers between devices, on_device(): lax.ppermute(rows[:, 0], 'tm', [(i, i - 1) for i in range(1, tm_n)])  1.97 us
  transfers between devices with their start and end apart: 14, of which 5 were waited for; matrix products, arithmetic and copies ran while one was open for 4% of the time, Pallas kernels for 19%

profile of v4, /device:TPU:1, one launch (start us, length us, event | category | flops | bytes accessed | tf_op | source)
XLA Modules:
  0.0 56.5 jit_solution(5443790232721200448)
XLA Ops:
  0.6 0.0 copy-start
  0.6 0.7 %copy.9 = f32[3,2,384]{2,0,1:T(4,128)S(1)} copy(f32[3,2,384]{2,1,0:T(2,128)} %param.3) | data formatting | bytes 18432 | tf_op args[0]
  1.3 0.0 copy-done
  1.4 2.0 %collective-permute-start = (f32[4,384]{1,0:T(4,128)S(1)}, f32[4,384]{1,0:T(4,128)S(1)}, u32[]{:S(2)}, u32[]{:S(2)}) collective-permute-start(f32[4,384]{1,0:T(4,128)S(1)} %fusion.1), channel_id=1, source_target_pairs={{1,0},{2,1},{3,2},{5,4},{6,5},{7,6},{9,8},{10,9},{11,10},{13,12},{... | collective-permute-start | bytes 18440 | tf_op jit(solution)/shard_map/ppermute | solution.py:301
  3.4 1.1 %slice_bitcast_fusion.2 = (f32[128,384]{1,0:T(8,128)S(1)}, f32[128,384]{1,0:T(8,128)S(1)}) fusion(f32[2,128,384]{2,1,0:T(8,128)} %param.4), kind=kLoop, calls=%fused_computation.3 | loop fusion | bytes 786432 | tf_op jit(solution)/shard_map/squeeze | solution.py:308
  4.5 2.8 %collective-permute-done = f32[4,384]{1,0:T(4,128)S(1)} collective-permute-done((f32[4,384]{1,0:T(4,128)S(1)}, f32[4,384]{1,0:T(4,128)S(1)}, u32[]{:S(2)}, u32[]{:S(2)}) %collective-permute-start) | collective-permute-done | bytes 6176 | tf_op jit(solution)/shard_map/ppermute | solution.py:301
  7.4 1.9 %collective-permute-start.1 = (f32[136,384]{1,0:T(8,128)S(1)}, f32[136,384]{1,0:T(8,128)S(1)}, u32[]{:S(2)}, u32[]{:S(2)}) collective-permute-start(f32[136,384]{1,0:T(8,128)S(1)} %get-tuple-element.24), channel_id=1, source_target_pairs={{0,0},{1,8},{2,2},{3,10},{4,4},{5,12},{6,6},{7,14},{8,1},{9,9},{10... | collective-permute-start | bytes 626696 | tf_op jit(solution)/shard_map/ppermute | solution.py:320
  9.3 2.7 %collective-permute-start.2 = (f32[136,384]{1,0:T(8,128)S(1)}, f32[136,384]{1,0:T(8,128)S(1)}, u32[]{:S(2)}, u32[]{:S(2)}) collective-permute-start(f32[136,384]{1,0:T(8,128)S(1)} %get-tuple-element.25), channel_id=1, source_target_pairs={{0,4},{1,12},{2,6},{3,14},{4,0},{5,8},{6,2},{7,10},{8,5},{9,13},{1... | collective-permute-start | bytes 626696 | tf_op jit(solution)/shard_map/ppermute | solution.py:320
  12.0 2.0 %collective-permute-start.6 = (f32[136,384]{1,0:T(8,128)S(1)}, f32[136,384]{1,0:T(8,128)S(1)}, u32[]{:S(2)}, u32[]{:S(2)}) collective-permute-start(f32[136,384]{1,0:T(8,128)S(1)} %get-tuple-element.24), channel_id=1, source_target_pairs={{0,16},{1,24},{2,18},{3,26},{4,20},{5,28},{6,22},{7,30},{8,17},{9,... | collective-permute-start | bytes 626696 | tf_op jit(solution)/shard_map/ppermute | solution.py:320
  14.1 1.5 %collective-permute-start.3 = (f32[136,384]{1,0:T(8,128)S(1)}, f32[136,384]{1,0:T(8,128)S(1)}, u32[]{:S(2)}, u32[]{:S(2)}) collective-permute-start(f32[136,384]{1,0:T(8,128)S(1)} %get-tuple-element.25), channel_id=1, source_target_pairs={{0,20},{1,28},{2,22},{3,30},{4,16},{5,24},{6,18},{7,26},{8,21},{9,... | collective-permute-start | bytes 626696 | tf_op jit(solution)/shard_map/ppermute | solution.py:320
  15.5 1.6 %collective-permute-done.1.refs_0_.refs_2_ = f32[136,384]{1,0:T(8,128)S(1)} collective-permute-done((f32[136,384]{1,0:T(8,128)S(1)}, f32[136,384]{1,0:T(8,128)S(1)}, u32[]{:S(2)}, u32[]{:S(2)}) %collective-permute-start.1) | collective-permute-done | bytes 208928 | tf_op jit(solution)/shard_map/ppermute | solution.py:320
  17.1 0.0 collective-permute-start.4
  17.1 2.5 %collective-permute-done.2.refs_1_.refs_3_ = f32[136,384]{1,0:T(8,128)S(1)} collective-permute-done((f32[136,384]{1,0:T(8,128)S(1)}, f32[136,384]{1,0:T(8,128)S(1)}, u32[]{:S(2)}, u32[]{:S(2)}) %collective-permute-start.2) | collective-permute-done | bytes 208928 | tf_op jit(solution)/shard_map/ppermute | solution.py:320
  19.6 0.0 collective-permute-start.5
  19.6 3.6 %shard_map.58 = (f32[128,768]{1,0:T(8,128)S(1)}, f32[24,768]{1,0:T(8,128)S(1)}, bf16[512,768]{1,0:T(8,128)(2,1)S(1)}, bf16[128,1536]{1,0:T(8,128)(2,1)S(1)}) custom-call(f32[136,384]{1,0:T(8,128)S(1)} %collective-permute-done.1.refs_0_.refs_2_, f32[136,384]{1,0:T(8,128)S(1)} %collective-permute-done.2.refs_1_.refs_3_, ...), custom_call_target="tpu_custom_call" | custom-call | flops 7549747200 | bytes 1 | tf_op jit(solution)/shard_map/pallas_call | solution.py:227
  23.2 2.0 %collective-permute-done.6.refs_2_ = f32[136,384]{1,0:T(8,128)S(1)} collective-permute-done((f32[136,384]{1,0:T(8,128)S(1)}, f32[136,384]{1,0:T(8,128)S(1)}, u32[]{:S(2)}, u32[]{:S(2)}) %collective-permute-start.6) | collective-permute-done | bytes 208928 | tf_op jit(solution)/shard_map/ppermute | solution.py:320
  25.2 0.0 collective-permute-start.8
  25.2 0.0 collective-permute-done.4.refs_2_
  25.2 0.0 collective-permute-done.5.refs_3_
  25.2 3.5 %shard_map.59 = (f32[128,768]{1,0:T(8,128)S(1)}, f32[24,768]{1,0:T(8,128)S(1)}) custom-call(f32[136,384]{1,0:T(8,128)S(1)} %collective-permute-done.1.refs_0_.refs_2_, f32[136,384]{1,0:T(8,128)S(1)} %collective-permute-done.2.refs_1_.refs_3_, f32[136,384]{1,0:T(8,128)S(1)} %collective-permute-done.4.refs_2_, f32[136,384]{1,0:T(8,128)S(1)} %collective-permute-done.5.refs_3_, ...), custom_call_target="tpu_custom_call" | custom-call | flops 7549747200 | bytes 1 | tf_op jit(solution)/shard_map/pallas_call | solution.py:227
  28.7 0.0 collective-permute-done.3.refs_2_
  28.7 0.6 %collective-permute-start.7 = (f32[136,384]{1,0:T(8,128)S(1)}, f32[136,384]{1,0:T(8,128)S(1)}, u32[]{:S(2)}, u32[]{:S(2)}) collective-permute-start(f32[136,384]{1,0:T(8,128)S(1)} %collective-permute-done.3.refs_2_), channel_id=1, source_target_pairs={{0,1},{1,0},{2,3},{3,2},{4,5},{5,4},{6,7},{7,6},{8,9},{9,8},{10,11... | collective-permute-start | bytes 626696 | tf_op jit(solution)/shard_map/ppermute | solution.py:325
  29.3 0.0 collective-permute-done.8.refs_3_
  29.3 3.5 %shard_map.60 = (f32[128,768]{1,0:T(8,128)S(1)}, f32[24,768]{1,0:T(8,128)S(1)}) custom-call(f32[136,384]{1,0:T(8,128)S(1)} %collective-permute-done.1.refs_0_.refs_2_, f32[136,384]{1,0:T(8,128)S(1)} %collective-permute-done.2.refs_1_.refs_3_, f32[136,384]{1,0:T(8,128)S(1)} %collective-permute-done.6.refs_2_, f32[136,384]{1,0:T(8,128)S(1)} %collective-permute-done.8.refs_3_, ...), custom_call_target="tpu_custom_call" | custom-call | flops 7549747200 | bytes 1 | tf_op jit(solution)/shard_map/pallas_call | solution.py:227
  32.8 0.0 collective-permute-done.7.refs_3_
  32.8 4.2 %shard_map.61 = (f32[136,384]{1,0:T(8,128)S(1)}, f32[136,384]{1,0:T(8,128)S(1)}, f32[32,128]{1,0:T(8,128)}) custom-call(f32[136,384]{1,0:T(8,128)S(1)} %collective-permute-done.1.refs_0_.refs_2_, f32[136,384]{1,0:T(8,128)S(1)} %collective-permute-done.2.refs_1_.refs_3_, f32[136,384]{1,0:T(8,128)S(1)} %collective-permute-done.3.refs_2_, ...), custom_call_target="tpu_custom_call" | custom-call | flops 7549747200 | bytes 1 | tf_op jit(solution)/shard_map/pallas_call | solution.py:227
  36.9 5.2 %collective-permute-start.10 = (f32[136,384]{1,0:T(8,128)S(1)}, f32[136,384]{1,0:T(8,128)S(1)}, u32[]{:S(2)}, u32[]{:S(2)}) collective-permute-start(f32[136,384]{1,0:T(8,128)S(1)} %get-tuple-element.41), channel_id=1, source_target_pairs={{0,0},{8,1},{2,2},{10,3},{4,4},{12,5},{6,6},{14,7},{1,8},{9,9},{3,... | collective-permute-start | bytes 626696 | tf_op jit(solution)/shard_map/ppermute | solution.py:341
  42.2 0.1 collective-permute-start.9
  42.3 4.4 %all-to-all-start = ((f32[32,1,128]{2,1,0:T(1,128)}), f32[32,1,128]{2,1,0:T(1,128)S(1)}, u32[]{:S(2)}, u32[]{:S(2)}) async-start(f32[32,1,128]{2,1,0:T(1,128)} %bitcast.8), calls=%async_computation | async-start | bytes 32768 | tf_op jit(solution)/shard_map/all_to_all | solution.py:343
  46.7 0.7 %collective-permute-start.11 = (f32[8,384]{1,0:T(8,128)S(1)}, f32[8,384]{1,0:T(8,128)S(1)}, u32[]{:S(2)}, u32[]{:S(2)}) collective-permute-start(f32[8,384]{1,0:T(8,128)S(1)} %slice.73), channel_id=1, source_target_pairs={{4,5},{12,6},{6,7},{5,13},{13,14},{7,15},{20,21},{28,22},{22,23},{... | collective-permute-start | bytes 36872 | tf_op jit(solution)/shard_map/ppermute | solution.py:342
  47.3 1.3 %collective-permute-start.12 = (f32[8,384]{1,0:T(8,128)S(1)}, f32[8,384]{1,0:T(8,128)S(1)}, u32[]{:S(2)}, u32[]{:S(2)}) collective-permute-start(f32[8,384]{1,0:T(8,128)S(1)} %slice.75), channel_id=1, source_target_pairs={{4,1},{12,2},{6,3},{5,9},{13,10},{7,11},{20,17},{28,18},{22,19},{2... | collective-permute-start | bytes 36872 | tf_op jit(solution)/shard_map/ppermute | solution.py:342
  48.6 0.0 collective-permute-done.10
  48.6 0.0 collective-permute-done.9
  48.7 0.8 %pad_maximum_fusion = f32[2,128,384]{2,1,0:T(8,128)} fusion(f32[1,128,384]{2,1,0:T(8,128)S(1)} %get-tuple-element.57, f32[1,128,384]{2,1,0:T(8,128)S(1)} %get-tuple-element.58), kind=kLoop, calls=%fused_computation | loop fusion | flops 98304 | bytes 786432 | tf_op jit(solution)/shard_map/stack | solution.py:347
  49.5 3.9 %all-to-all-done = f32[32,1,128]{2,1,0:T(1,128)S(1)} async-done(((f32[32,1,128]{2,1,0:T(1,128)}), f32[32,1,128]{2,1,0:T(1,128)S(1)}, u32[]{:S(2)}, u32[]{:S(2)}) %all-to-all-start) | async-done | bytes 16416 | tf_op jit(solution)/shard_map/all_to_all | solution.py:343
  53.4 0.6 %slice_reduce_fusion = f32[]{:T(128)} fusion(f32[32,128]{1,0:T(8,128)S(1)} %bitcast.29), kind=kLoop, calls=%fused_computation.9 | loop fusion | flops 31 | bytes 132 | tf_op jit(solution)/shard_map/reduce_sum | solution.py:355
  54.7 0.0 collective-permute-done.11
  54.7 0.0 collective-permute-done.12
  54.7 0.7 %select_select_fusion = f32[3,2,384]{2,1,0:T(2,128)} fusion(pred[2]{0:T(512)(128)(4,1)S(1)} %get-tuple-element.60, pred[2]{0:T(512)(128)(4,1)S(1)} %get-tuple-element.59, f32[3,384]{1,0:T(4,128)S(1)} %get-tuple-element.52, f32[3,384]{1,0:T(4,128)S(1)} %get-tuple-element.51), kind=kLoop, calls=%fused_computation.10 | loop fusion | flops 4608 | bytes 18436 | tf_op jit(solution)/shard_map/jit(_where)/select_n | solution.py:353
  (15 shorter events, 0.2 us)
Async XLA Ops:
  0.6 0.7 %copy-start = (s32[2,384]{1,0:T(2,128)S(1)}, s32[2,384]{1,0:T(2,128)}, u32[]{:S(2)}) copy-start(s32[2,384]{1,0:T(2,128)} %param.5) | copy-start | bytes 9220
  1.4 5.8 %collective-permute-start = (f32[4,384]{1,0:T(4,128)S(1)}, f32[4,384]{1,0:T(4,128)S(1)}, u32[]{:S(2)}, u32[]{:S(2)}) collective-permute-start(f32[4,384]{1,0:T(4,128)S(1)} %fusion.1), channel_id=1, source_target_pairs={{1,0},{2,1},{3,2},{5,4},{6,5},{7,6},{9,8},{10,9},{11,10},{13,12},{... | collective-permute-start | bytes 18440 | tf_op jit(solution)/shard_map/ppermute | solution.py:301
  7.4 9.8 %collective-permute-start.1 = (f32[136,384]{1,0:T(8,128)S(1)}, f32[136,384]{1,0:T(8,128)S(1)}, u32[]{:S(2)}, u32[]{:S(2)}) collective-permute-start(f32[136,384]{1,0:T(8,128)S(1)} %get-tuple-element.24), channel_id=1, source_target_pairs={{0,0},{1,8},{2,2},{3,10},{4,4},{5,12},{6,6},{7,14},{8,1},{9,9},{10... | collective-permute-start | bytes 626696 | tf_op jit(solution)/shard_map/ppermute | solution.py:320
  9.3 10.3 %collective-permute-start.2 = (f32[136,384]{1,0:T(8,128)S(1)}, f32[136,384]{1,0:T(8,128)S(1)}, u32[]{:S(2)}, u32[]{:S(2)}) collective-permute-start(f32[136,384]{1,0:T(8,128)S(1)} %get-tuple-element.25), channel_id=1, source_target_pairs={{0,4},{1,12},{2,6},{3,14},{4,0},{5,8},{6,2},{7,10},{8,5},{9,13},{1... | collective-permute-start | bytes 626696 | tf_op jit(solution)/shard_map/ppermute | solution.py:320
  12.0 13.2 %collective-permute-start.6 = (f32[136,384]{1,0:T(8,128)S(1)}, f32[136,384]{1,0:T(8,128)S(1)}, u32[]{:S(2)}, u32[]{:S(2)}) collective-permute-start(f32[136,384]{1,0:T(8,128)S(1)} %get-tuple-element.24), channel_id=1, source_target_pairs={{0,16},{1,24},{2,18},{3,26},{4,20},{5,28},{6,22},{7,30},{8,17},{9,... | collective-permute-start | bytes 626696 | tf_op jit(solution)/shard_map/ppermute | solution.py:320
  14.1 14.6 %collective-permute-start.3 = (f32[136,384]{1,0:T(8,128)S(1)}, f32[136,384]{1,0:T(8,128)S(1)}, u32[]{:S(2)}, u32[]{:S(2)}) collective-permute-start(f32[136,384]{1,0:T(8,128)S(1)} %get-tuple-element.25), channel_id=1, source_target_pairs={{0,20},{1,28},{2,22},{3,30},{4,16},{5,24},{6,18},{7,26},{8,21},{9,... | collective-permute-start | bytes 626696 | tf_op jit(solution)/shard_map/ppermute | solution.py:320
  17.1 8.0 %collective-permute-start.4 = (f32[136,384]{1,0:T(8,128)S(1)}, f32[136,384]{1,0:T(8,128)S(1)}, u32[]{:S(2)}, u32[]{:S(2)}) collective-permute-start(f32[136,384]{1,0:T(8,128)S(1)} %collective-permute-done.1.refs_0_.refs_2_), channel_id=1, source_target_pairs={{0,1},{1,0},{2,3},{3,2},{4,5},{5,4},{6,7},{7,6},{8,9},{9,8},{10,11... | collective-permute-start | bytes 626696 | tf_op jit(solution)/shard_map/ppermute | solution.py:325
  19.6 5.6 %collective-permute-start.5 = (f32[136,384]{1,0:T(8,128)S(1)}, f32[136,384]{1,0:T(8,128)S(1)}, u32[]{:S(2)}, u32[]{:S(2)}) collective-permute-start(f32[136,384]{1,0:T(8,128)S(1)} %collective-permute-done.2.refs_1_.refs_3_), channel_id=1, source_target_pairs={{0,1},{1,0},{2,3},{3,2},{4,5},{5,4},{6,7},{7,6},{8,9},{9,8},{10,11... | collective-permute-start | bytes 626696 | tf_op jit(solution)/shard_map/ppermute | solution.py:325
  25.2 4.1 %collective-permute-start.8 = (f32[136,384]{1,0:T(8,128)S(1)}, f32[136,384]{1,0:T(8,128)S(1)}, u32[]{:S(2)}, u32[]{:S(2)}) collective-permute-start(f32[136,384]{1,0:T(8,128)S(1)} %collective-permute-done.6.refs_2_), channel_id=1, source_target_pairs={{0,1},{1,0},{2,3},{3,2},{4,5},{5,4},{6,7},{7,6},{8,9},{9,8},{10,11... | collective-permute-start | bytes 626696 | tf_op jit(solution)/shard_map/ppermute | solution.py:325
  28.7 4.1 %collective-permute-start.7 = (f32[136,384]{1,0:T(8,128)S(1)}, f32[136,384]{1,0:T(8,128)S(1)}, u32[]{:S(2)}, u32[]{:S(2)}) collective-permute-start(f32[136,384]{1,0:T(8,128)S(1)} %collective-permute-done.3.refs_2_), channel_id=1, source_target_pairs={{0,1},{1,0},{2,3},{3,2},{4,5},{5,4},{6,7},{7,6},{8,9},{9,8},{10,11... | collective-permute-start | bytes 626696 | tf_op jit(solution)/shard_map/ppermute | solution.py:325
  36.9 11.7 %collective-permute-start.10 = (f32[136,384]{1,0:T(8,128)S(1)}, f32[136,384]{1,0:T(8,128)S(1)}, u32[]{:S(2)}, u32[]{:S(2)}) collective-permute-start(f32[136,384]{1,0:T(8,128)S(1)} %get-tuple-element.41), channel_id=1, source_target_pairs={{0,0},{8,1},{2,2},{10,3},{4,4},{12,5},{6,6},{14,7},{1,8},{9,9},{3,... | collective-permute-start | bytes 626696 | tf_op jit(solution)/shard_map/ppermute | solution.py:341
  42.2 6.5 %collective-permute-start.9 = (f32[136,384]{1,0:T(8,128)S(1)}, f32[136,384]{1,0:T(8,128)S(1)}, u32[]{:S(2)}, u32[]{:S(2)}) collective-permute-start(f32[136,384]{1,0:T(8,128)S(1)} %get-tuple-element.40), channel_id=1, source_target_pairs={{4,0},{12,1},{6,2},{14,3},{0,4},{8,5},{2,6},{10,7},{5,8},{13,9},{7... | collective-permute-start | bytes 626696 | tf_op jit(solution)/shard_map/ppermute | solution.py:341
  42.3 11.1 %all-to-all-start = ((f32[32,1,128]{2,1,0:T(1,128)}), f32[32,1,128]{2,1,0:T(1,128)S(1)}, u32[]{:S(2)}, u32[]{:S(2)}) async-start(f32[32,1,128]{2,1,0:T(1,128)} %bitcast.8), calls=%async_computation | async-start | bytes 32768 | tf_op jit(solution)/shard_map/all_to_all | solution.py:343
  46.7 8.0 %collective-permute-start.11 = (f32[8,384]{1,0:T(8,128)S(1)}, f32[8,384]{1,0:T(8,128)S(1)}, u32[]{:S(2)}, u32[]{:S(2)}) collective-permute-start(f32[8,384]{1,0:T(8,128)S(1)} %slice.73), channel_id=1, source_target_pairs={{4,5},{12,6},{6,7},{5,13},{13,14},{7,15},{20,21},{28,22},{22,23},{... | collective-permute-start | bytes 36872 | tf_op jit(solution)/shard_map/ppermute | solution.py:342
  47.3 7.4 %collective-permute-start.12 = (f32[8,384]{1,0:T(8,128)S(1)}, f32[8,384]{1,0:T(8,128)S(1)}, u32[]{:S(2)}, u32[]{:S(2)}) collective-permute-start(f32[8,384]{1,0:T(8,128)S(1)} %slice.75), channel_id=1, source_target_pairs={{4,1},{12,2},{6,3},{5,9},{13,10},{7,11},{20,17},{28,18},{22,19},{2... | collective-permute-start | bytes 36872 | tf_op jit(solution)/shard_map/ppermute | solution.py:342

commit v5 on v4

--- a/solution.py
+++ b/solution.py
@@ -88,8 +88,6 @@
             weights[0:emb, at] = high
             weights[emb : 2 * emb, at] = low
             weights[2 * emb : 3 * emb, at] = high
-        row = lax.broadcasted_iota(jnp.int32, (emb, own_size), 0)
-        weights[3 * emb : 4 * emb, :] = jnp.where(row == 0, 1.0, 0.0).astype(bf16)
         geometry(geo_own, own[...], centre, True)
         row = lax.broadcasted_iota(jnp.int32, (GEO, own_size), 0)
         values = geo_own[...]
@@ -107,12 +105,8 @@
         lhs[at, 2 * emb : 3 * emb] = low
         points = col_blocks[b][emb : emb + TAIL, :]
         start, end = geometry(geo_col, points, centre, False)
-        geo_col[96:97, :] = (points[6:7, :] - 1.0) * 1e4
-        flipped = geo_col[...].T
-        geo_lhs[at, :] = flipped.astype(bf16)
-        hidden = jnp.broadcast_to(flipped[:, 96:97], (width, emb))
-        column = lax.broadcasted_iota(jnp.int32, (width, emb), 1)
-        lhs[at, 3 * emb : 4 * emb] = jnp.where(column == 0, hidden, 0.0).astype(bf16)
+        geo_col[32:96, :] = geo_col[32:96, :] * points[6:7, :]
+        geo_lhs[at, :] = geo_col[...].T.astype(bf16)
         ones, zeros = jnp.ones((1, width), f32), jnp.zeros((1, width), f32)
         centred = jnp.concatenate([start, end, ones, zeros], 0)
         for k, part in enumerate(split3(centred)):
@@ -220,7 +214,7 @@
         if counted:
             out_shape.append(jax.ShapeDtypeStruct((peers, 128), f32))
     if first:
-        out_shape.append(jax.ShapeDtypeStruct((4 * emb, own_size), bf16))
+        out_shape.append(jax.ShapeDtypeStruct((3 * emb, own_size), bf16))
         out_shape.append(jax.ShapeDtypeStruct((GEO, 2 * own_size), bf16))
     pairs = (high - low) * col_size
     tile = (chunk, strip)
@@ -230,7 +224,7 @@
         ),
         out_shape=out_shape,
         scratch_shapes=[
-            pltpu.VMEM((col_size, 4 * emb), bf16),
+            pltpu.VMEM((col_size, 3 * emb), bf16),
             pltpu.VMEM((col_size, GEO), bf16),
             pltpu.VMEM((2 * emb, col_size), bf16),
             pltpu.VMEM((24, col_size), bf16),
@@ -329,15 +323,14 @@
     ready = across(own)
     made = terms(own, None)
     totals, kept = made[:2], made[2:]
-    LOOK = 1
-    for n in range(len(far)):
-        ahead = far[n : n + LOOK]
-        ahead, totals = lax.optimization_barrier((ahead, totals))
-        far[n : n + LOOK] = ahead
-        following = [far[n]] + across([far[n]])
-        totals = terms(ready, [*totals, *kept])
-        ready = following
-    *done, loss = terms(ready, [*totals, *kept], home=list(turns))
+    totals = terms(ready, [*totals, *kept])
+    held = []
+    for part in far:
+        part, totals = lax.optimization_barrier((part, totals))
+        following = across([part])
+        totals = terms([*held, part], [*totals, *kept])
+        held = following
+    *done, loss = terms(held, [*totals, *kept], home=list(turns))
     back = [lax.ppermute(done[turn], AXES, inward(turn)) for turn in turns]
     late = [lax.ppermute(done[turn][emb - 0:], AXES, inward_next(turn))[0:] for turn in turns]
     shares = lax.all_to_all(loss, AXES, 0, 0, tiled=True)

time: 57.4 us -> 55.4 us (0.965)
  waiting for transfers between devices: 12.8 us -> 10.8 us
  Pallas kernels: 14.7 us -> 15.3 us
    ppermute x4, waiting for transfers between devices: 6.04 us -> 4.07 us  [on_device(): lax.ppermute(sent[turn], AXES, outward(turn, shift))]
    pallas_call x4 -> x5, Pallas kernels: 14.7 us -> 15.3 us  [pair_terms(): pl.pallas_call(functools.partial(pair_kernel, own_n, col_n, chunk, 32, fi...]
  transfers between devices with their start and end apart: 14 -> 14, of which waited for: 5 -> 4; matrix products, arithmetic and copies ran while one was open for 4% -> 5% of each run, Pallas kernels for 19% -> 24%
where the time goes in v5:
time: 55.4 us; the launch traced here: 54.5 us
  starting transfers between devices  21.8 us (39%)
  Pallas kernels  15.3 us (28%)
  waiting for transfers between devices  10.8 us (19%)
  between operations  2.63 us (5%)
  other arithmetic  2.15 us (4%)
  local copies, waits for them, and re-layouts  1.89 us (3%)
    pallas_call x5, Pallas kernels, pair_terms(): pl.pallas_call(functools.partial(pair_kernel, own_n, col_n, chunk, 32, fi...  15.3 us
    ppermute x4, starting transfers between devices, on_device(): lax.ppermute(sent[turn], AXES, outward(turn, shift))  8.16 us
    ppermute x2, starting transfers between devices, on_device(): back = [lax.ppermute(done[turn], AXES, inward(turn)) for turn in turns]  5.14 us
    ppermute x4, waiting for transfers between devices, on_device(): lax.ppermute(sent[turn], AXES, outward(turn, shift))  4.07 us
    all_to_all x1, waiting for transfers between devices, on_device(): shares = lax.all_to_all(loss, AXES, 0, 0, tiled=True)  3.93 us
    all_to_all x1, starting transfers between devices, on_device(): shares = lax.all_to_all(loss, AXES, 0, 0, tiled=True)  3.93 us
    ppermute x1, waiting for transfers between devices, on_device(): lax.ppermute(rows[:, 0], 'tm', [(i, i - 1) for i in range(1, tm_n)])  2.78 us
    ppermute x1, starting transfers between devices, on_device(): lax.ppermute(rows[:, 0], 'tm', [(i, i - 1) for i in range(1, tm_n)])  1.97 us
  transfers between devices with their start and end apart: 14, of which 4 were waited for; matrix products, arithmetic and copies ran while one was open for 5% of the time, Pallas kernels for 24%

profile of v5, /device:TPU:1, one launch (start us, length us, event | category | flops | bytes accessed | tf_op | source)
XLA Modules:
  0.0 54.5 jit_solution(12862218924530929023)
XLA Ops:
  0.6 0.0 copy-start
  0.6 0.7 %copy.9 = f32[3,2,384]{2,0,1:T(4,128)S(1)} copy(f32[3,2,384]{2,1,0:T(2,128)} %param.3) | data formatting | bytes 18432 | tf_op args[0]
  1.3 0.0 copy-done
  1.4 2.0 %collective-permute-start = (f32[4,384]{1,0:T(4,128)S(1)}, f32[4,384]{1,0:T(4,128)S(1)}, u32[]{:S(2)}, u32[]{:S(2)}) collective-permute-start(f32[4,384]{1,0:T(4,128)S(1)} %fusion.1), channel_id=1, source_target_pairs={{1,0},{2,1},{3,2},{5,4},{6,5},{7,6},{9,8},{10,9},{11,10},{13,12},{... | collective-permute-start | bytes 18440 | tf_op jit(solution)/shard_map/ppermute | solution.py:295
  3.4 1.1 %slice_bitcast_fusion.2 = (f32[128,384]{1,0:T(8,128)S(1)}, f32[128,384]{1,0:T(8,128)S(1)}) fusion(f32[2,128,384]{2,1,0:T(8,128)} %param.4), kind=kLoop, calls=%fused_computation.3 | loop fusion | bytes 786432 | tf_op jit(solution)/shard_map/squeeze | solution.py:302
  4.5 2.8 %collective-permute-done = f32[4,384]{1,0:T(4,128)S(1)} collective-permute-done((f32[4,384]{1,0:T(4,128)S(1)}, f32[4,384]{1,0:T(4,128)S(1)}, u32[]{:S(2)}, u32[]{:S(2)}) %collective-permute-start) | collective-permute-done | bytes 6176 | tf_op jit(solution)/shard_map/ppermute | solution.py:295
  7.4 1.9 %collective-permute-start.1 = (f32[136,384]{1,0:T(8,128)S(1)}, f32[136,384]{1,0:T(8,128)S(1)}, u32[]{:S(2)}, u32[]{:S(2)}) collective-permute-start(f32[136,384]{1,0:T(8,128)S(1)} %get-tuple-element.26), channel_id=1, source_target_pairs={{0,0},{1,8},{2,2},{3,10},{4,4},{5,12},{6,6},{7,14},{8,1},{9,9},{10... | collective-permute-start | bytes 626696 | tf_op jit(solution)/shard_map/ppermute | solution.py:314
  9.3 2.7 %collective-permute-start.2 = (f32[136,384]{1,0:T(8,128)S(1)}, f32[136,384]{1,0:T(8,128)S(1)}, u32[]{:S(2)}, u32[]{:S(2)}) collective-permute-start(f32[136,384]{1,0:T(8,128)S(1)} %get-tuple-element.27), channel_id=1, source_target_pairs={{0,4},{1,12},{2,6},{3,14},{4,0},{5,8},{6,2},{7,10},{8,5},{9,13},{1... | collective-permute-start | bytes 626696 | tf_op jit(solution)/shard_map/ppermute | solution.py:314
  12.0 2.0 %collective-permute-start.4 = (f32[136,384]{1,0:T(8,128)S(1)}, f32[136,384]{1,0:T(8,128)S(1)}, u32[]{:S(2)}, u32[]{:S(2)}) collective-permute-start(f32[136,384]{1,0:T(8,128)S(1)} %get-tuple-element.26), channel_id=1, source_target_pairs={{0,16},{1,24},{2,18},{3,26},{4,20},{5,28},{6,22},{7,30},{8,17},{9,... | collective-permute-start | bytes 626696 | tf_op jit(solution)/shard_map/ppermute | solution.py:314
  14.1 1.5 %collective-permute-start.3 = (f32[136,384]{1,0:T(8,128)S(1)}, f32[136,384]{1,0:T(8,128)S(1)}, u32[]{:S(2)}, u32[]{:S(2)}) collective-permute-start(f32[136,384]{1,0:T(8,128)S(1)} %get-tuple-element.27), channel_id=1, source_target_pairs={{0,20},{1,28},{2,22},{3,30},{4,16},{5,24},{6,18},{7,26},{8,21},{9,... | collective-permute-start | bytes 626696 | tf_op jit(solution)/shard_map/ppermute | solution.py:314
  15.5 1.6 %collective-permute-done.1.refs_0_.refs_2_ = f32[136,384]{1,0:T(8,128)S(1)} collective-permute-done((f32[136,384]{1,0:T(8,128)S(1)}, f32[136,384]{1,0:T(8,128)S(1)}, u32[]{:S(2)}, u32[]{:S(2)}) %collective-permute-start.1) | collective-permute-done | bytes 208928 | tf_op jit(solution)/shard_map/ppermute | solution.py:314
  17.1 0.0 collective-permute-start.5
  17.1 2.5 %collective-permute-done.2.refs_1_.refs_3_ = f32[136,384]{1,0:T(8,128)S(1)} collective-permute-done((f32[136,384]{1,0:T(8,128)S(1)}, f32[136,384]{1,0:T(8,128)S(1)}, u32[]{:S(2)}, u32[]{:S(2)}) %collective-permute-start.2) | collective-permute-done | bytes 208928 | tf_op jit(solution)/shard_map/ppermute | solution.py:314
  19.6 0.0 collective-permute-start.6
  19.6 3.6 %shard_map.58 = (f32[128,768]{1,0:T(8,128)S(1)}, f32[24,768]{1,0:T(8,128)S(1)}, bf16[384,768]{1,0:T(8,128)(2,1)S(1)}, bf16[128,1536]{1,0:T(8,128)(2,1)S(1)}) custom-call(f32[136,384]{1,0:T(8,128)S(1)} %collective-permute-done.1.refs_0_.refs_2_, f32[136,384]{1,0:T(8,128)S(1)} %collective-permute-done.2.refs_1_.refs_3_, ...), custom_call_target="tpu_custom_call" | custom-call | flops 7549747200 | bytes 1 | tf_op jit(solution)/shard_map/pallas_call | solution.py:221
  23.2 0.0 collective-permute-done.5.refs_2_
  23.2 0.0 collective-permute-done.6.refs_3_
  23.2 3.5 %shard_map.59 = (f32[128,768]{1,0:T(8,128)S(1)}, f32[24,768]{1,0:T(8,128)S(1)}) custom-call(f32[136,384]{1,0:T(8,128)S(1)} %collective-permute-done.1.refs_0_.refs_2_, f32[136,384]{1,0:T(8,128)S(1)} %collective-permute-done.2.refs_1_.refs_3_, f32[136,384]{1,0:T(8,128)S(1)} %collective-permute-done.5.refs_2_, f32[136,384]{1,0:T(8,128)S(1)} %collective-permute-done.6.refs_3_, ...), custom_call_target="tpu_custom_call" | custom-call | flops 7549747200 | bytes 1 | tf_op jit(solution)/shard_map/pallas_call | solution.py:221
  26.8 0.0 collective-permute-done.4.refs_2_
  26.8 0.6 %collective-permute-start.8 = (f32[136,384]{1,0:T(8,128)S(1)}, f32[136,384]{1,0:T(8,128)S(1)}, u32[]{:S(2)}, u32[]{:S(2)}) collective-permute-start(f32[136,384]{1,0:T(8,128)S(1)} %collective-permute-done.4.refs_2_), channel_id=1, source_target_pairs={{0,1},{1,0},{2,3},{3,2},{4,5},{5,4},{6,7},{7,6},{8,9},{9,8},{10,11... | collective-permute-start | bytes 626696 | tf_op jit(solution)/shard_map/ppermute | solution.py:319
  27.3 2.1 %shard_map.60 = (f32[128,768]{1,0:T(8,128)S(1)}, f32[24,768]{1,0:T(8,128)S(1)}) custom-call(f32[136,384]{1,0:T(8,128)S(1)} %collective-permute-done.1.refs_0_.refs_2_, f32[136,384]{1,0:T(8,128)S(1)} %collective-permute-done.2.refs_1_.refs_3_, f32[136,384]{1,0:T(8,128)S(1)} %collective-permute-done.4.refs_2_, f32[128,768]{1,0:T(8,128)S(1)} %get-tuple-element.35.refs_3_, ...), custom_call_target="tpu_custom_call" | custom-call | flops 3774873600 | bytes 1 | tf_op jit(solution)/shard_map/pallas_call | solution.py:221
  29.4 0.0 collective-permute-done.3.refs_3_
  29.4 0.1 collective-permute-start.7
  29.5 0.0 collective-permute-done.8.refs_2_
  29.5 3.7 %shard_map.61 = (f32[128,768]{1,0:T(8,128)S(1)}, f32[24,768]{1,0:T(8,128)S(1)}) custom-call(f32[136,384]{1,0:T(8,128)S(1)} %collective-permute-done.1.refs_0_.refs_2_, f32[136,384]{1,0:T(8,128)S(1)} %collective-permute-done.2.refs_1_.refs_3_, f32[136,384]{1,0:T(8,128)S(1)} %collective-permute-done.8.refs_2_, f32[136,384]{1,0:T(8,128)S(1)} %collective-permute-done.3.refs_3_, ...), custom_call_target="tpu_custom_call" | custom-call | flops 7549747200 | bytes 1 | tf_op jit(solution)/shard_map/pallas_call | solution.py:221
  33.2 0.0 collective-permute-done.7.refs_2_
  33.2 2.4 %shard_map.62 = (f32[136,384]{1,0:T(8,128)S(1)}, f32[136,384]{1,0:T(8,128)S(1)}, f32[32,128]{1,0:T(8,128)}) custom-call(f32[136,384]{1,0:T(8,128)S(1)} %collective-permute-done.1.refs_0_.refs_2_, f32[136,384]{1,0:T(8,128)S(1)} %collective-permute-done.2.refs_1_.refs_3_, f32[136,384]{1,0:T(8,128)S(1)} %collective-permute-done.7.refs_2_, ...), custom_call_target="tpu_custom_call" | custom-call | flops 3774873600 | bytes 1 | tf_op jit(solution)/shard_map/pallas_call | solution.py:221
  35.6 3.7 %collective-permute-start.10 = (f32[136,384]{1,0:T(8,128)S(1)}, f32[136,384]{1,0:T(8,128)S(1)}, u32[]{:S(2)}, u32[]{:S(2)}) collective-permute-start(f32[136,384]{1,0:T(8,128)S(1)} %get-tuple-element.45), channel_id=1, source_target_pairs={{0,0},{8,1},{2,2},{10,3},{4,4},{12,5},{6,6},{14,7},{1,8},{9,9},{3,... | collective-permute-start | bytes 626696 | tf_op jit(solution)/shard_map/ppermute | solution.py:334
  39.3 1.4 %collective-permute-start.9 = (f32[136,384]{1,0:T(8,128)S(1)}, f32[136,384]{1,0:T(8,128)S(1)}, u32[]{:S(2)}, u32[]{:S(2)}) collective-permute-start(f32[136,384]{1,0:T(8,128)S(1)} %get-tuple-element.44), channel_id=1, source_target_pairs={{4,0},{12,1},{6,2},{14,3},{0,4},{8,5},{2,6},{10,7},{5,8},{13,9},{7... | collective-permute-start | bytes 626696 | tf_op jit(solution)/shard_map/ppermute | solution.py:334
  40.7 3.9 %all-to-all-start = ((f32[32,1,128]{2,1,0:T(1,128)}), f32[32,1,128]{2,1,0:T(1,128)S(1)}, u32[]{:S(2)}, u32[]{:S(2)}) async-start(f32[32,1,128]{2,1,0:T(1,128)} %bitcast.8), calls=%async_computation | async-start | bytes 32768 | tf_op jit(solution)/shard_map/all_to_all | solution.py:336
  44.7 0.7 %collective-permute-start.11 = (f32[8,384]{1,0:T(8,128)S(1)}, f32[8,384]{1,0:T(8,128)S(1)}, u32[]{:S(2)}, u32[]{:S(2)}) collective-permute-start(f32[8,384]{1,0:T(8,128)S(1)} %slice.73), channel_id=1, source_target_pairs={{4,5},{12,6},{6,7},{5,13},{13,14},{7,15},{20,21},{28,22},{22,23},{... | collective-permute-start | bytes 36872 | tf_op jit(solution)/shard_map/ppermute | solution.py:335
  45.3 1.3 %collective-permute-start.12 = (f32[8,384]{1,0:T(8,128)S(1)}, f32[8,384]{1,0:T(8,128)S(1)}, u32[]{:S(2)}, u32[]{:S(2)}) collective-permute-start(f32[8,384]{1,0:T(8,128)S(1)} %slice.75), channel_id=1, source_target_pairs={{4,1},{12,2},{6,3},{5,9},{13,10},{7,11},{20,17},{28,18},{22,19},{2... | collective-permute-start | bytes 36872 | tf_op jit(solution)/shard_map/ppermute | solution.py:335
  46.6 0.0 collective-permute-done.10
  46.6 0.0 collective-permute-done.9
  46.7 0.8 %pad_maximum_fusion = f32[2,128,384]{2,1,0:T(8,128)} fusion(f32[1,128,384]{2,1,0:T(8,128)S(1)} %get-tuple-element.61, f32[1,128,384]{2,1,0:T(8,128)S(1)} %get-tuple-element.62), kind=kLoop, calls=%fused_computation | loop fusion | flops 98304 | bytes 786432 | tf_op jit(solution)/shard_map/stack | solution.py:340
  47.5 3.9 %all-to-all-done = f32[32,1,128]{2,1,0:T(1,128)S(1)} async-done(((f32[32,1,128]{2,1,0:T(1,128)}), f32[32,1,128]{2,1,0:T(1,128)S(1)}, u32[]{:S(2)}, u32[]{:S(2)}) %all-to-all-start) | async-done | bytes 16416 | tf_op jit(solution)/shard_map/all_to_all | solution.py:336
  51.4 0.6 %slice_reduce_fusion = f32[]{:T(128)} fusion(f32[32,128]{1,0:T(8,128)S(1)} %bitcast.29), kind=kLoop, calls=%fused_computation.9 | loop fusion | flops 31 | bytes 132 | tf_op jit(solution)/shard_map/reduce_sum | solution.py:348
  52.7 0.0 collective-permute-done.11
  52.7 0.0 collective-permute-done.12
  52.7 0.7 %select_select_fusion = f32[3,2,384]{2,1,0:T(2,128)} fusion(pred[2]{0:T(512)(128)(4,1)S(1)} %get-tuple-element.64, pred[2]{0:T(512)(128)(4,1)S(1)} %get-tuple-element.63, f32[3,384]{1,0:T(4,128)S(1)} %get-tuple-element.56, f32[3,384]{1,0:T(4,128)S(1)} %get-tuple-element.55), kind=kLoop, calls=%fused_computation.10 | loop fusion | flops 4608 | bytes 18436 | tf_op jit(solution)/shard_map/jit(_where)/select_n | solution.py:346
  (15 shorter events, 0.2 us)
Async XLA Ops:
  0.6 0.7 %copy-start = (s32[2,384]{1,0:T(2,128)S(1)}, s32[2,384]{1,0:T(2,128)}, u32[]{:S(2)}) copy-start(s32[2,384]{1,0:T(2,128)} %param.5) | copy-start | bytes 9220
  1.4 5.8 %collective-permute-start = (f32[4,384]{1,0:T(4,128)S(1)}, f32[4,384]{1,0:T(4,128)S(1)}, u32[]{:S(2)}, u32[]{:S(2)}) collective-permute-start(f32[4,384]{1,0:T(4,128)S(1)} %fusion.1), channel_id=1, source_target_pairs={{1,0},{2,1},{3,2},{5,4},{6,5},{7,6},{9,8},{10,9},{11,10},{13,12},{... | collective-permute-start | bytes 18440 | tf_op jit(solution)/shard_map/ppermute | solution.py:295
  7.4 9.8 %collective-permute-start.1 = (f32[136,384]{1,0:T(8,128)S(1)}, f32[136,384]{1,0:T(8,128)S(1)}, u32[]{:S(2)}, u32[]{:S(2)}) collective-permute-start(f32[136,384]{1,0:T(8,128)S(1)} %get-tuple-element.26), channel_id=1, source_target_pairs={{0,0},{1,8},{2,2},{3,10},{4,4},{5,12},{6,6},{7,14},{8,1},{9,9},{10... | collective-permute-start | bytes 626696 | tf_op jit(solution)/shard_map/ppermute | solution.py:314
  9.3 10.3 %collective-permute-start.2 = (f32[136,384]{1,0:T(8,128)S(1)}, f32[136,384]{1,0:T(8,128)S(1)}, u32[]{:S(2)}, u32[]{:S(2)}) collective-permute-start(f32[136,384]{1,0:T(8,128)S(1)} %get-tuple-element.27), channel_id=1, source_target_pairs={{0,4},{1,12},{2,6},{3,14},{4,0},{5,8},{6,2},{7,10},{8,5},{9,13},{1... | collective-permute-start | bytes 626696 | tf_op jit(solution)/shard_map/ppermute | solution.py:314
  12.0 14.7 %collective-permute-start.4 = (f32[136,384]{1,0:T(8,128)S(1)}, f32[136,384]{1,0:T(8,128)S(1)}, u32[]{:S(2)}, u32[]{:S(2)}) collective-permute-start(f32[136,384]{1,0:T(8,128)S(1)} %get-tuple-element.26), channel_id=1, source_target_pairs={{0,16},{1,24},{2,18},{3,26},{4,20},{5,28},{6,22},{7,30},{8,17},{9,... | collective-permute-start | bytes 626696 | tf_op jit(solution)/shard_map/ppermute | solution.py:314
  14.1 15.4 %collective-permute-start.3 = (f32[136,384]{1,0:T(8,128)S(1)}, f32[136,384]{1,0:T(8,128)S(1)}, u32[]{:S(2)}, u32[]{:S(2)}) collective-permute-start(f32[136,384]{1,0:T(8,128)S(1)} %get-tuple-element.27), channel_id=1, source_target_pairs={{0,20},{1,28},{2,22},{3,30},{4,16},{5,24},{6,18},{7,26},{8,21},{9,... | collective-permute-start | bytes 626696 | tf_op jit(solution)/shard_map/ppermute | solution.py:314
  17.1 6.1 %collective-permute-start.5 = (f32[136,384]{1,0:T(8,128)S(1)}, f32[136,384]{1,0:T(8,128)S(1)}, u32[]{:S(2)}, u32[]{:S(2)}) collective-permute-start(f32[136,384]{1,0:T(8,128)S(1)} %collective-permute-done.1.refs_0_.refs_2_), channel_id=1, source_target_pairs={{0,1},{1,0},{2,3},{3,2},{4,5},{5,4},{6,7},{7,6},{8,9},{9,8},{10,11... | collective-permute-start | bytes 626696 | tf_op jit(solution)/shard_map/ppermute | solution.py:319
  19.6 3.6 %collective-permute-start.6 = (f32[136,384]{1,0:T(8,128)S(1)}, f32[136,384]{1,0:T(8,128)S(1)}, u32[]{:S(2)}, u32[]{:S(2)}) collective-permute-start(f32[136,384]{1,0:T(8,128)S(1)} %collective-permute-done.2.refs_1_.refs_3_), channel_id=1, source_target_pairs={{0,1},{1,0},{2,3},{3,2},{4,5},{5,4},{6,7},{7,6},{8,9},{9,8},{10,11... | collective-permute-start | bytes 626696 | tf_op jit(solution)/shard_map/ppermute | solution.py:319
  26.8 2.7 %collective-permute-start.8 = (f32[136,384]{1,0:T(8,128)S(1)}, f32[136,384]{1,0:T(8,128)S(1)}, u32[]{:S(2)}, u32[]{:S(2)}) collective-permute-start(f32[136,384]{1,0:T(8,128)S(1)} %collective-permute-done.4.refs_2_), channel_id=1, source_target_pairs={{0,1},{1,0},{2,3},{3,2},{4,5},{5,4},{6,7},{7,6},{8,9},{9,8},{10,11... | collective-permute-start | bytes 626696 | tf_op jit(solution)/shard_map/ppermute | solution.py:319
  29.4 3.8 %collective-permute-start.7 = (f32[136,384]{1,0:T(8,128)S(1)}, f32[136,384]{1,0:T(8,128)S(1)}, u32[]{:S(2)}, u32[]{:S(2)}) collective-permute-start(f32[136,384]{1,0:T(8,128)S(1)} %collective-permute-done.3.refs_3_), channel_id=1, source_target_pairs={{0,1},{1,0},{2,3},{3,2},{4,5},{5,4},{6,7},{7,6},{8,9},{9,8},{10,11... | collective-permute-start | bytes 626696 | tf_op jit(solution)/shard_map/ppermute | solution.py:319
  35.6 11.1 %collective-permute-start.10 = (f32[136,384]{1,0:T(8,128)S(1)}, f32[136,384]{1,0:T(8,128)S(1)}, u32[]{:S(2)}, u32[]{:S(2)}) collective-permute-start(f32[136,384]{1,0:T(8,128)S(1)} %get-tuple-element.45), channel_id=1, source_target_pairs={{0,0},{8,1},{2,2},{10,3},{4,4},{12,5},{6,6},{14,7},{1,8},{9,9},{3,... | collective-permute-start | bytes 626696 | tf_op jit(solution)/shard_map/ppermute | solution.py:334
  39.3 7.4 %collective-permute-start.9 = (f32[136,384]{1,0:T(8,128)S(1)}, f32[136,384]{1,0:T(8,128)S(1)}, u32[]{:S(2)}, u32[]{:S(2)}) collective-permute-start(f32[136,384]{1,0:T(8,128)S(1)} %get-tuple-element.44), channel_id=1, source_target_pairs={{4,0},{12,1},{6,2},{14,3},{0,4},{8,5},{2,6},{10,7},{5,8},{13,9},{7... | collective-permute-start | bytes 626696 | tf_op jit(solution)/shard_map/ppermute | solution.py:334
  40.7 10.7 %all-to-all-start = ((f32[32,1,128]{2,1,0:T(1,128)}), f32[32,1,128]{2,1,0:T(1,128)S(1)}, u32[]{:S(2)}, u32[]{:S(2)}) async-start(f32[32,1,128]{2,1,0:T(1,128)} %bitcast.8), calls=%async_computation | async-start | bytes 32768 | tf_op jit(solution)/shard_map/all_to_all | solution.py:336
  44.7 8.0 %collective-permute-start.11 = (f32[8,384]{1,0:T(8,128)S(1)}, f32[8,384]{1,0:T(8,128)S(1)}, u32[]{:S(2)}, u32[]{:S(2)}) collective-permute-start(f32[8,384]{1,0:T(8,128)S(1)} %slice.73), channel_id=1, source_target_pairs={{4,5},{12,6},{6,7},{5,13},{13,14},{7,15},{20,21},{28,22},{22,23},{... | collective-permute-start | bytes 36872 | tf_op jit(solution)/shard_map/ppermute | solution.py:335
  45.3 7.4 %collective-permute-start.12 = (f32[8,384]{1,0:T(8,128)S(1)}, f32[8,384]{1,0:T(8,128)S(1)}, u32[]{:S(2)}, u32[]{:S(2)}) collective-permute-start(f32[8,384]{1,0:T(8,128)S(1)} %slice.75), channel_id=1, source_target_pairs={{4,1},{12,2},{6,3},{5,9},{13,10},{7,11},{20,17},{28,18},{22,19},{2... | collective-permute-start | bytes 36872 | tf_op jit(solution)/shard_map/ppermute | solution.py:335

commit v6 on v5

--- a/solution.py
+++ b/solution.py
@@ -245,6 +245,17 @@
     )(*own_blocks, *col_blocks, *(() if first else prev))
 
 
+def scaled(values, factor):
+    def kernel(values_ref, out_ref):
+        out_ref[...] = values_ref[...] * factor
+
+    return pl.pallas_call(
+        kernel,
+        out_shape=jax.ShapeDtypeStruct(values.shape, f32),
+        cost_estimate=pl.CostEstimate(flops=10**11, bytes_accessed=1, transcendentals=0),
+    )(values)
+
+
 def pick(options, index):
     chosen = options[0]
     for n in range(1, len(options)):
@@ -334,6 +345,9 @@
     back = [lax.ppermute(done[turn], AXES, inward(turn)) for turn in turns]
     late = [lax.ppermute(done[turn][emb - 0:], AXES, inward_next(turn))[0:] for turn in turns]
     shares = lax.all_to_all(loss, AXES, 0, 0, tiled=True)
+    factor = 0.25 / (tracks * (tracks - 1) / 2.0 * (frames - 1))
+    mean_loss = scaled(jnp.sum(shares, 0).reshape(1, 128), factor)
+    back, late, mean_loss = lax.optimization_barrier((back, late, mean_loss))
     of_frame = [
         pick(back, lax.rem(k - member + 2 * team * frames_local, frames_local)) for k in turns
     ]
@@ -345,8 +359,7 @@
         before = v[emb + 3 : emb + 6]
         grad_pos = jnp.where(frame == k, moved[:, None, :], grad_pos)
     shares, grad_emb = lax.optimization_barrier((shares, grad_emb))
-    mean_loss = jnp.sum(shares[:, :1]) * 0.25 / (tracks * (tracks - 1) / 2.0 * (frames - 1))
-    return (grad_pos, grad_emb, mean_loss)
+    return (grad_pos, grad_emb, mean_loss[0, 0])
 
 
 def solution(mesh):

time: 55.4 us -> 53.4 us (0.964)
  waiting for transfers between devices: 10.8 us -> 8.92 us
  between operations: 2.63 us -> 0.83 us
  Pallas kernels: 15.3 us -> 16.4 us
  starting transfers between devices: 21.8 us -> 22.9 us
    all_to_all x1, waiting for transfers between devices: 3.93 us -> 0.01 us  [on_device(): shares = lax.all_to_all(loss, AXES, 0, 0, tiled=True)]
    ppermute x2, waiting for transfers between devices: 0.01 us -> 2.05 us  [on_device(): lax.ppermute(done[turn][emb - 0:], AXES, inward_next(turn))[0:]]
    all_to_all x1, starting transfers between devices: 3.93 us -> 5.35 us  [on_device(): shares = lax.all_to_all(loss, AXES, 0, 0, tiled=True)]
    pallas_call x0 -> x1, Pallas kernels: none -> 1.17 us  [scaled(): pl.pallas_call(kernel, out_shape=jax.ShapeDtypeStruct(values.shape, f32),...]
  transfers between devices with their start and end apart: 14 -> 14, of which waited for: 4 -> 4; matrix products, arithmetic and copies ran while one was open for 5% -> 3% of each run, Pallas kernels for 24% -> 26%
where the time goes in v6:
time: 53.4 us; the launch traced here: 53.1 us
  starting transfers between devices  22.9 us (43%)
  Pallas kernels  16.4 us (31%)
  waiting for transfers between devices  8.92 us (17%)
  other arithmetic  2.1 us (4%)
  local copies, waits for them, and re-layouts  1.89 us (4%)
  between operations  0.83 us (2%)
    pallas_call x5, Pallas kernels, pair_terms(): pl.pallas_call(functools.partial(pair_kernel, own_n, col_n, chunk, 32, fi...  15.3 us
    ppermute x4, starting transfers between devices, on_device(): lax.ppermute(sent[turn], AXES, outward(turn, shift))  8.16 us
    all_to_all x1, starting transfers between devices, on_device(): shares = lax.all_to_all(loss, AXES, 0, 0, tiled=True)  5.35 us
    ppermute x2, starting transfers between devices, on_device(): back = [lax.ppermute(done[turn], AXES, inward(turn)) for turn in turns]  4.82 us
    ppermute x4, waiting for transfers between devices, on_device(): lax.ppermute(sent[turn], AXES, outward(turn, shift))  4.07 us
    ppermute x1, waiting for transfers between devices, on_device(): lax.ppermute(rows[:, 0], 'tm', [(i, i - 1) for i in range(1, tm_n)])  2.78 us
    ppermute x2, waiting for transfers between devices, on_device(): lax.ppermute(done[turn][emb - 0:], AXES, inward_next(turn))[0:]  2.05 us
    ppermute x1, starting transfers between devices, on_device(): lax.ppermute(rows[:, 0], 'tm', [(i, i - 1) for i in range(1, tm_n)])  1.97 us
  transfers between devices with their start and end apart: 14, of which 4 were waited for; matrix products, arithmetic and copies ran while one was open for 3% of the time, Pallas kernels for 26%

profile of v6, /device:TPU:1, one launch (start us, length us, event | category | flops | bytes accessed | tf_op | source)
XLA Modules:
  0.0 53.1 jit_solution(5820610077236647095)
XLA Ops:
  0.6 0.0 copy-start
  0.6 0.7 %copy.9 = f32[3,2,384]{2,0,1:T(4,128)S(1)} copy(f32[3,2,384]{2,1,0:T(2,128)} %param.3) | data formatting | bytes 18432 | tf_op args[0]
  1.3 0.0 copy-done
  1.4 2.0 %collective-permute-start = (f32[4,384]{1,0:T(4,128)S(1)}, f32[4,384]{1,0:T(4,128)S(1)}, u32[]{:S(2)}, u32[]{:S(2)}) collective-permute-start(f32[4,384]{1,0:T(4,128)S(1)} %fusion), channel_id=1, source_target_pairs={{1,0},{2,1},{3,2},{5,4},{6,5},{7,6},{9,8},{10,9},{11,10},{13,12},{... | collective-permute-start | bytes 18440 | tf_op jit(solution)/shard_map/ppermute | solution.py:306
  3.4 1.1 %slice_bitcast_fusion.2 = (f32[128,384]{1,0:T(8,128)S(1)}, f32[128,384]{1,0:T(8,128)S(1)}) fusion(f32[2,128,384]{2,1,0:T(8,128)} %param.4), kind=kLoop, calls=%fused_computation.3 | loop fusion | bytes 786432 | tf_op jit(solution)/shard_map/squeeze | solution.py:313
  4.5 2.8 %collective-permute-done = f32[4,384]{1,0:T(4,128)S(1)} collective-permute-done((f32[4,384]{1,0:T(4,128)S(1)}, f32[4,384]{1,0:T(4,128)S(1)}, u32[]{:S(2)}, u32[]{:S(2)}) %collective-permute-start) | collective-permute-done | bytes 6176 | tf_op jit(solution)/shard_map/ppermute | solution.py:306
  7.4 1.9 %collective-permute-start.1 = (f32[136,384]{1,0:T(8,128)S(1)}, f32[136,384]{1,0:T(8,128)S(1)}, u32[]{:S(2)}, u32[]{:S(2)}) collective-permute-start(f32[136,384]{1,0:T(8,128)S(1)} %get-tuple-element.29), channel_id=1, source_target_pairs={{0,0},{1,8},{2,2},{3,10},{4,4},{5,12},{6,6},{7,14},{8,1},{9,9},{10... | collective-permute-start | bytes 626696 | tf_op jit(solution)/shard_map/ppermute | solution.py:325
  9.3 2.7 %collective-permute-start.2 = (f32[136,384]{1,0:T(8,128)S(1)}, f32[136,384]{1,0:T(8,128)S(1)}, u32[]{:S(2)}, u32[]{:S(2)}) collective-permute-start(f32[136,384]{1,0:T(8,128)S(1)} %get-tuple-element.30), channel_id=1, source_target_pairs={{0,4},{1,12},{2,6},{3,14},{4,0},{5,8},{6,2},{7,10},{8,5},{9,13},{1... | collective-permute-start | bytes 626696 | tf_op jit(solution)/shard_map/ppermute | solution.py:325
  12.0 2.0 %collective-permute-start.4 = (f32[136,384]{1,0:T(8,128)S(1)}, f32[136,384]{1,0:T(8,128)S(1)}, u32[]{:S(2)}, u32[]{:S(2)}) collective-permute-start(f32[136,384]{1,0:T(8,128)S(1)} %get-tuple-element.29), channel_id=1, source_target_pairs={{0,16},{1,24},{2,18},{3,26},{4,20},{5,28},{6,22},{7,30},{8,17},{9,... | collective-permute-start | bytes 626696 | tf_op jit(solution)/shard_map/ppermute | solution.py:325
  14.1 1.5 %collective-permute-start.3 = (f32[136,384]{1,0:T(8,128)S(1)}, f32[136,384]{1,0:T(8,128)S(1)}, u32[]{:S(2)}, u32[]{:S(2)}) collective-permute-start(f32[136,384]{1,0:T(8,128)S(1)} %get-tuple-element.30), channel_id=1, source_target_pairs={{0,20},{1,28},{2,22},{3,30},{4,16},{5,24},{6,18},{7,26},{8,21},{9,... | collective-permute-start | bytes 626696 | tf_op jit(solution)/shard_map/ppermute | solution.py:325
  15.5 1.6 %collective-permute-done.1.refs_0_.refs_2_ = f32[136,384]{1,0:T(8,128)S(1)} collective-permute-done((f32[136,384]{1,0:T(8,128)S(1)}, f32[136,384]{1,0:T(8,128)S(1)}, u32[]{:S(2)}, u32[]{:S(2)}) %collective-permute-start.1) | collective-permute-done | bytes 208928 | tf_op jit(solution)/shard_map/ppermute | solution.py:325
  17.1 0.0 collective-permute-start.5
  17.1 2.5 %collective-permute-done.2.refs_1_.refs_3_ = f32[136,384]{1,0:T(8,128)S(1)} collective-permute-done((f32[136,384]{1,0:T(8,128)S(1)}, f32[136,384]{1,0:T(8,128)S(1)}, u32[]{:S(2)}, u32[]{:S(2)}) %collective-permute-start.2) | collective-permute-done | bytes 208928 | tf_op jit(solution)/shard_map/ppermute | solution.py:325
  19.6 0.0 collective-permute-start.6
  19.6 3.6 %shard_map.58 = (f32[128,768]{1,0:T(8,128)S(1)}, f32[24,768]{1,0:T(8,128)S(1)}, bf16[384,768]{1,0:T(8,128)(2,1)S(1)}, bf16[128,1536]{1,0:T(8,128)(2,1)S(1)}) custom-call(f32[136,384]{1,0:T(8,128)S(1)} %collective-permute-done.1.refs_0_.refs_2_, f32[136,384]{1,0:T(8,128)S(1)} %collective-permute-done.2.refs_1_.refs_3_, ...), custom_call_target="tpu_custom_call" | custom-call | flops 7549747200 | bytes 1 | tf_op jit(solution)/shard_map/pallas_call | solution.py:221
  23.2 0.0 collective-permute-done.5.refs_2_
  23.2 0.0 collective-permute-done.6.refs_3_
  23.2 3.5 %shard_map.59 = (f32[128,768]{1,0:T(8,128)S(1)}, f32[24,768]{1,0:T(8,128)S(1)}) custom-call(f32[136,384]{1,0:T(8,128)S(1)} %collective-permute-done.1.refs_0_.refs_2_, f32[136,384]{1,0:T(8,128)S(1)} %collective-permute-done.2.refs_1_.refs_3_, f32[136,384]{1,0:T(8,128)S(1)} %collective-permute-done.5.refs_2_, f32[136,384]{1,0:T(8,128)S(1)} %collective-permute-done.6.refs_3_, ...), custom_call_target="tpu_custom_call" | custom-call | flops 7549747200 | bytes 1 | tf_op jit(solution)/shard_map/pallas_call | solution.py:221
  26.8 0.0 collective-permute-done.4.refs_2_
  26.8 0.6 %collective-permute-start.8 = (f32[136,384]{1,0:T(8,128)S(1)}, f32[136,384]{1,0:T(8,128)S(1)}, u32[]{:S(2)}, u32[]{:S(2)}) collective-permute-start(f32[136,384]{1,0:T(8,128)S(1)} %collective-permute-done.4.refs_2_), channel_id=1, source_target_pairs={{0,1},{1,0},{2,3},{3,2},{4,5},{5,4},{6,7},{7,6},{8,9},{9,8},{10,11... | collective-permute-start | bytes 626696 | tf_op jit(solution)/shard_map/ppermute | solution.py:330
  27.3 2.1 %shard_map.60 = (f32[128,768]{1,0:T(8,128)S(1)}, f32[24,768]{1,0:T(8,128)S(1)}) custom-call(f32[136,384]{1,0:T(8,128)S(1)} %collective-permute-done.1.refs_0_.refs_2_, f32[136,384]{1,0:T(8,128)S(1)} %collective-permute-done.2.refs_1_.refs_3_, f32[136,384]{1,0:T(8,128)S(1)} %collective-permute-done.4.refs_2_, f32[128,768]{1,0:T(8,128)S(1)} %get-tuple-element.38.refs_3_, ...), custom_call_target="tpu_custom_call" | custom-call | flops 3774873600 | bytes 1 | tf_op jit(solution)/shard_map/pallas_call | solution.py:221
  29.4 0.0 collective-permute-done.3.refs_3_
  29.4 0.1 collective-permute-start.7
  29.5 0.0 collective-permute-done.8.refs_2_
  29.5 3.7 %shard_map.61 = (f32[128,768]{1,0:T(8,128)S(1)}, f32[24,768]{1,0:T(8,128)S(1)}) custom-call(f32[136,384]{1,0:T(8,128)S(1)} %collective-permute-done.1.refs_0_.refs_2_, f32[136,384]{1,0:T(8,128)S(1)} %collective-permute-done.2.refs_1_.refs_3_, f32[136,384]{1,0:T(8,128)S(1)} %collective-permute-done.8.refs_2_, f32[136,384]{1,0:T(8,128)S(1)} %collective-permute-done.3.refs_3_, ...), custom_call_target="tpu_custom_call" | custom-call | flops 7549747200 | bytes 1 | tf_op jit(solution)/shard_map/pallas_call | solution.py:221
  33.2 0.0 collective-permute-done.7.refs_2_
  33.2 2.4 %shard_map.62 = (f32[136,384]{1,0:T(8,128)S(1)}, f32[136,384]{1,0:T(8,128)S(1)}, f32[32,128]{1,0:T(8,128)}) custom-call(f32[136,384]{1,0:T(8,128)S(1)} %collective-permute-done.1.refs_0_.refs_2_, f32[136,384]{1,0:T(8,128)S(1)} %collective-permute-done.2.refs_1_.refs_3_, f32[136,384]{1,0:T(8,128)S(1)} %collective-permute-done.7.refs_2_, ...), custom_call_target="tpu_custom_call" | custom-call | flops 3774873600 | bytes 1 | tf_op jit(solution)/shard_map/pallas_call | solution.py:221
  35.6 5.4 %all-to-all-start = ((f32[32,1,128]{2,1,0:T(1,128)}), f32[32,1,128]{2,1,0:T(1,128)S(1)}, u32[]{:S(2)}, u32[]{:S(2)}) async-start(f32[32,1,128]{2,1,0:T(1,128)} %bitcast.8), calls=%async_computation | async-start | bytes 32768 | tf_op jit(solution)/shard_map/all_to_all | solution.py:347
  41.0 3.5 %collective-permute-start.9 = (f32[136,384]{1,0:T(8,128)S(1)}, f32[136,384]{1,0:T(8,128)S(1)}, u32[]{:S(2)}, u32[]{:S(2)}) collective-permute-start(f32[136,384]{1,0:T(8,128)S(1)} %get-tuple-element.47), channel_id=1, source_target_pairs={{0,0},{8,1},{2,2},{10,3},{4,4},{12,5},{6,6},{14,7},{1,8},{9,9},{3,... | collective-permute-start | bytes 626696 | tf_op jit(solution)/shard_map/ppermute | solution.py:345
  44.5 1.3 %collective-permute-start.10 = (f32[136,384]{1,0:T(8,128)S(1)}, f32[136,384]{1,0:T(8,128)S(1)}, u32[]{:S(2)}, u32[]{:S(2)}) collective-permute-start(f32[136,384]{1,0:T(8,128)S(1)} %get-tuple-element.48), channel_id=1, source_target_pairs={{4,0},{12,1},{6,2},{14,3},{0,4},{8,5},{2,6},{10,7},{5,8},{13,9},{7... | collective-permute-start | bytes 626696 | tf_op jit(solution)/shard_map/ppermute | solution.py:345
  45.8 0.7 %collective-permute-start.11 = (f32[8,384]{1,0:T(8,128)S(1)}, f32[8,384]{1,0:T(8,128)S(1)}, u32[]{:S(2)}, u32[]{:S(2)}) collective-permute-start(f32[8,384]{1,0:T(8,128)S(1)} %slice.70), channel_id=1, source_target_pairs={{4,5},{12,6},{6,7},{5,13},{13,14},{7,15},{20,21},{28,22},{22,23},{... | collective-permute-start | bytes 36872 | tf_op jit(solution)/shard_map/ppermute | solution.py:346
  46.5 1.3 %collective-permute-start.12 = (f32[8,384]{1,0:T(8,128)S(1)}, f32[8,384]{1,0:T(8,128)S(1)}, u32[]{:S(2)}, u32[]{:S(2)}) collective-permute-start(f32[8,384]{1,0:T(8,128)S(1)} %slice.71), channel_id=1, source_target_pairs={{4,1},{12,2},{6,3},{5,9},{13,10},{7,11},{20,17},{28,18},{22,19},{2... | collective-permute-start | bytes 36872 | tf_op jit(solution)/shard_map/ppermute | solution.py:346
  47.8 0.0 all-to-all-done
  47.8 0.6 %reduce_sum.9 = f32[128]{0:T(128)} reduce(f32[32,1,128]{2,1,0:T(1,128)S(1)} %all-to-all-done, f32[]{:T(128)} %constant.31.clone.1), dimensions={0,1}, to_apply=%region_0.1 | reduce | flops 3968 | bytes 16900 | tf_op jit(solution)/shard_map/reduce_sum | solution.py:349
  48.3 1.2 %shard_map.63 = f32[1,128]{1,0:T(1,128)} custom-call(f32[1,128]{1,0:T(1,128)} %bitcast.32), custom_call_target="tpu_custom_call" | custom-call | flops 99999997952 | bytes 1 | tf_op jit(solution)/shard_map/pallas_call | solution.py:252
  49.5 0.0 collective-permute-done.11
  49.5 2.1 %collective-permute-done.12 = f32[8,384]{1,0:T(8,128)S(1)} collective-permute-done((f32[8,384]{1,0:T(8,128)S(1)}, f32[8,384]{1,0:T(8,128)S(1)}, u32[]{:S(2)}, u32[]{:S(2)}) %collective-permute-start.12) | collective-permute-done | bytes 12320 | tf_op jit(solution)/shard_map/ppermute | solution.py:346
  51.5 0.0 collective-permute-done.10
  51.6 0.0 collective-permute-done.9
  51.6 0.8 %pad_maximum_fusion = f32[2,128,384]{2,1,0:T(8,128)} fusion(f32[1,128,384]{2,1,0:T(8,128)S(1)} %get-tuple-element.67, f32[1,128,384]{2,1,0:T(8,128)S(1)} %get-tuple-element.68), kind=kLoop, calls=%fused_computation | loop fusion | flops 98304 | bytes 786432 | tf_op jit(solution)/shard_map/stack | solution.py:354
  52.4 0.7 %select_select_fusion = f32[3,2,384]{2,1,0:T(2,128)} fusion(pred[2]{0:T(512)(128)(4,1)S(1)} %get-tuple-element.70, pred[2]{0:T(512)(128)(4,1)S(1)} %get-tuple-element.69, f32[3,384]{1,0:T(4,128)S(1)} %get-tuple-element.62, f32[3,384]{1,0:T(4,128)S(1)} %get-tuple-element.61), kind=kLoop, calls=%fused_computation.9 | loop fusion | flops 4608 | bytes 18436 | tf_op jit(solution)/shard_map/jit(_where)/select_n | solution.py:360
  (15 shorter events, 0.2 us)
Async XLA Ops:
  0.6 0.7 %copy-start = (s32[2,384]{1,0:T(2,128)S(1)}, s32[2,384]{1,0:T(2,128)}, u32[]{:S(2)}) copy-start(s32[2,384]{1,0:T(2,128)} %param.5) | copy-start | bytes 9220
  1.4 5.8 %collective-permute-start = (f32[4,384]{1,0:T(4,128)S(1)}, f32[4,384]{1,0:T(4,128)S(1)}, u32[]{:S(2)}, u32[]{:S(2)}) collective-permute-start(f32[4,384]{1,0:T(4,128)S(1)} %fusion), channel_id=1, source_target_pairs={{1,0},{2,1},{3,2},{5,4},{6,5},{7,6},{9,8},{10,9},{11,10},{13,12},{... | collective-permute-start | bytes 18440 | tf_op jit(solution)/shard_map/ppermute | solution.py:306
  7.4 9.8 %collective-permute-start.1 = (f32[136,384]{1,0:T(8,128)S(1)}, f32[136,384]{1,0:T(8,128)S(1)}, u32[]{:S(2)}, u32[]{:S(2)}) collective-permute-start(f32[136,384]{1,0:T(8,128)S(1)} %get-tuple-element.29), channel_id=1, source_target_pairs={{0,0},{1,8},{2,2},{3,10},{4,4},{5,12},{6,6},{7,14},{8,1},{9,9},{10... | collective-permute-start | bytes 626696 | tf_op jit(solution)/shard_map/ppermute | solution.py:325
  9.3 10.3 %collective-permute-start.2 = (f32[136,384]{1,0:T(8,128)S(1)}, f32[136,384]{1,0:T(8,128)S(1)}, u32[]{:S(2)}, u32[]{:S(2)}) collective-permute-start(f32[136,384]{1,0:T(8,128)S(1)} %get-tuple-element.30), channel_id=1, source_target_pairs={{0,4},{1,12},{2,6},{3,14},{4,0},{5,8},{6,2},{7,10},{8,5},{9,13},{1... | collective-permute-start | bytes 626696 | tf_op jit(solution)/shard_map/ppermute | solution.py:325
  12.0 14.7 %collective-permute-start.4 = (f32[136,384]{1,0:T(8,128)S(1)}, f32[136,384]{1,0:T(8,128)S(1)}, u32[]{:S(2)}, u32[]{:S(2)}) collective-permute-start(f32[136,384]{1,0:T(8,128)S(1)} %get-tuple-element.29), channel_id=1, source_target_pairs={{0,16},{1,24},{2,18},{3,26},{4,20},{5,28},{6,22},{7,30},{8,17},{9,... | collective-permute-start | bytes 626696 | tf_op jit(solution)/shard_map/ppermute | solution.py:325
  14.1 15.4 %collective-permute-start.3 = (f32[136,384]{1,0:T(8,128)S(1)}, f32[136,384]{1,0:T(8,128)S(1)}, u32[]{:S(2)}, u32[]{:S(2)}) collective-permute-start(f32[136,384]{1,0:T(8,128)S(1)} %get-tuple-element.30), channel_id=1, source_target_pairs={{0,20},{1,28},{2,22},{3,30},{4,16},{5,24},{6,18},{7,26},{8,21},{9,... | collective-permute-start | bytes 626696 | tf_op jit(solution)/shard_map/ppermute | solution.py:325
  17.1 6.1 %collective-permute-start.5 = (f32[136,384]{1,0:T(8,128)S(1)}, f32[136,384]{1,0:T(8,128)S(1)}, u32[]{:S(2)}, u32[]{:S(2)}) collective-permute-start(f32[136,384]{1,0:T(8,128)S(1)} %collective-permute-done.1.refs_0_.refs_2_), channel_id=1, source_target_pairs={{0,1},{1,0},{2,3},{3,2},{4,5},{5,4},{6,7},{7,6},{8,9},{9,8},{10,11... | collective-permute-start | bytes 626696 | tf_op jit(solution)/shard_map/ppermute | solution.py:330
  19.6 3.6 %collective-permute-start.6 = (f32[136,384]{1,0:T(8,128)S(1)}, f32[136,384]{1,0:T(8,128)S(1)}, u32[]{:S(2)}, u32[]{:S(2)}) collective-permute-start(f32[136,384]{1,0:T(8,128)S(1)} %collective-permute-done.2.refs_1_.refs_3_), channel_id=1, source_target_pairs={{0,1},{1,0},{2,3},{3,2},{4,5},{5,4},{6,7},{7,6},{8,9},{9,8},{10,11... | collective-permute-start | bytes 626696 | tf_op jit(solution)/shard_map/ppermute | solution.py:330
  26.8 2.7 %collective-permute-start.8 = (f32[136,384]{1,0:T(8,128)S(1)}, f32[136,384]{1,0:T(8,128)S(1)}, u32[]{:S(2)}, u32[]{:S(2)}) collective-permute-start(f32[136,384]{1,0:T(8,128)S(1)} %collective-permute-done.4.refs_2_), channel_id=1, source_target_pairs={{0,1},{1,0},{2,3},{3,2},{4,5},{5,4},{6,7},{7,6},{8,9},{9,8},{10,11... | collective-permute-start | bytes 626696 | tf_op jit(solution)/shard_map/ppermute | solution.py:330
  29.4 3.8 %collective-permute-start.7 = (f32[136,384]{1,0:T(8,128)S(1)}, f32[136,384]{1,0:T(8,128)S(1)}, u32[]{:S(2)}, u32[]{:S(2)}) collective-permute-start(f32[136,384]{1,0:T(8,128)S(1)} %collective-permute-done.3.refs_3_), channel_id=1, source_target_pairs={{0,1},{1,0},{2,3},{3,2},{4,5},{5,4},{6,7},{7,6},{8,9},{9,8},{10,11... | collective-permute-start | bytes 626696 | tf_op jit(solution)/shard_map/ppermute | solution.py:330
  35.6 12.2 %all-to-all-start = ((f32[32,1,128]{2,1,0:T(1,128)}), f32[32,1,128]{2,1,0:T(1,128)S(1)}, u32[]{:S(2)}, u32[]{:S(2)}) async-start(f32[32,1,128]{2,1,0:T(1,128)} %bitcast.8), calls=%async_computation | async-start | bytes 32768 | tf_op jit(solution)/shard_map/all_to_all | solution.py:347
  41.0 10.6 %collective-permute-start.9 = (f32[136,384]{1,0:T(8,128)S(1)}, f32[136,384]{1,0:T(8,128)S(1)}, u32[]{:S(2)}, u32[]{:S(2)}) collective-permute-start(f32[136,384]{1,0:T(8,128)S(1)} %get-tuple-element.47), channel_id=1, source_target_pairs={{0,0},{8,1},{2,2},{10,3},{4,4},{12,5},{6,6},{14,7},{1,8},{9,9},{3,... | collective-permute-start | bytes 626696 | tf_op jit(solution)/shard_map/ppermute | solution.py:345
  44.5 7.0 %collective-permute-start.10 = (f32[136,384]{1,0:T(8,128)S(1)}, f32[136,384]{1,0:T(8,128)S(1)}, u32[]{:S(2)}, u32[]{:S(2)}) collective-permute-start(f32[136,384]{1,0:T(8,128)S(1)} %get-tuple-element.48), channel_id=1, source_target_pairs={{4,0},{12,1},{6,2},{14,3},{0,4},{8,5},{2,6},{10,7},{5,8},{13,9},{7... | collective-permute-start | bytes 626696 | tf_op jit(solution)/shard_map/ppermute | solution.py:345
  45.8 3.7 %collective-permute-start.11 = (f32[8,384]{1,0:T(8,128)S(1)}, f32[8,384]{1,0:T(8,128)S(1)}, u32[]{:S(2)}, u32[]{:S(2)}) collective-permute-start(f32[8,384]{1,0:T(8,128)S(1)} %slice.70), channel_id=1, source_target_pairs={{4,5},{12,6},{6,7},{5,13},{13,14},{7,15},{20,21},{28,22},{22,23},{... | collective-permute-start | bytes 36872 | tf_op jit(solution)/shard_map/ppermute | solution.py:346
  46.5 5.1 %collective-permute-start.12 = (f32[8,384]{1,0:T(8,128)S(1)}, f32[8,384]{1,0:T(8,128)S(1)}, u32[]{:S(2)}, u32[]{:S(2)}) collective-permute-start(f32[8,384]{1,0:T(8,128)S(1)} %slice.71), channel_id=1, source_target_pairs={{4,1},{12,2},{6,3},{5,9},{13,10},{7,11},{20,17},{28,18},{22,19},{2... | collective-permute-start | bytes 36872 | tf_op jit(solution)/shard_map/ppermute | solution.py:346

commit v7 on v6

--- a/solution.py
+++ b/solution.py
@@ -57,7 +57,7 @@
     return start, end
 
 
-def pair_kernel(own_n, col_n, chunk, rows, first, home, lanes, energy, weight_scale, *refs):
+def pair_kernel(own_n, col_n, chunk, rows, first, home, lanes, weight_scale, *refs):
     refs = list(refs)
 
     def take(count):
@@ -68,7 +68,7 @@
     own_blocks, col_blocks = take(own_n), take(col_n)
     prev = take(0 if first else 2)
     kept = take(0 if first else 2)
-    outs = take(2 if home is None else len(home) + (energy is not None))
+    outs = take(2 if home is None else len(home) + 1)
     if first:
         kept = take(2)
     weights, geo_weights = kept
@@ -146,10 +146,7 @@
             pulls[k][0][at, :size], pulls[k][1][at, :size] = split(pull * inv0)
             pulls[k][2][at, :size], pulls[k][3][at, :size] = split(pull * inv1)
             total = total + value.reshape(rows // 8, 8, size).sum(0)
-        if energy is not None:
-            column = lax.broadcasted_iota(jnp.int32, (8, size), 1) + i[0]
-            factor = jnp.where(column >= energy, 2.0, 1.0) if energy < i[1] else 1.0
-            energies[:, mine] += total * factor
+        energies[:, mine] += total
 
     def gradients(n, i, k):
         cols, at, size = pl.ds(n * chunk, chunk), slice(*i), i[1] - i[0]
@@ -184,14 +181,13 @@
         out[emb : emb + 3, :] = (sums[0:3, at] - start * sums[6:7, at]) * seen
         out[emb + 3 : emb + 6, :] = (end * sums[14:15, at] - sums[11:14, at]) * seen
         out[emb + 6 : emb + 8, :] = jnp.zeros((2, width), f32)
-    if energy is not None:
-        loss = jnp.sum(energies[...] * own[6:7, :], axis=0, keepdims=True)
-        loss = jnp.sum(loss, axis=1, keepdims=True)
-        outs[len(home)][...] = jnp.broadcast_to(loss, outs[len(home)].shape)
+    loss = jnp.sum(energies[...] * own[6:7, :], axis=0, keepdims=True)
+    loss = jnp.sum(loss, axis=1, keepdims=True)
+    outs[len(home)][...] = jnp.broadcast_to(loss, outs[len(home)].shape)
 
 
 def pair_terms(
-    own_blocks, col_blocks, prev, weight_scale, peers, home=None, double=None, counted=True
+    own_blocks, col_blocks, prev, weight_scale, peers, home=None
 ):
     own_n, col_n = len(own_blocks), len(col_blocks)
     emb, width = own_blocks[0].shape[0] - TAIL, own_blocks[0].shape[1]
@@ -200,9 +196,6 @@
     low, high = (0, own_size) if home is None else (home[0] * width, (home[-1] + 1) * width)
     strip = 256 if (high - low) % 256 == 0 else 384 if (high - low) % 384 == 0 else 128
     lanes = [(i, i + strip) for i in range(low, high, strip)]
-    energy = None
-    if counted:
-        energy = own_size if double is None else double * width
     first = prev is None
     if home is None:
         out_shape = [
@@ -211,8 +204,7 @@
         ]
     else:
         out_shape = [jax.ShapeDtypeStruct((emb + TAIL, width), f32)] * len(home)
-        if counted:
-            out_shape.append(jax.ShapeDtypeStruct((peers, 128), f32))
+        out_shape.append(jax.ShapeDtypeStruct((peers, 128), f32))
     if first:
         out_shape.append(jax.ShapeDtypeStruct((3 * emb, own_size), bf16))
         out_shape.append(jax.ShapeDtypeStruct((GEO, 2 * own_size), bf16))
@@ -220,7 +212,7 @@
     tile = (chunk, strip)
     return pl.pallas_call(
         functools.partial(
-            pair_kernel, own_n, col_n, chunk, 32, first, home, lanes, energy, weight_scale
+            pair_kernel, own_n, col_n, chunk, 32, first, home, lanes, weight_scale
         ),
         out_shape=out_shape,
         scratch_shapes=[
@@ -334,8 +326,9 @@
     ready = across(own)
     made = terms(own, None)
     totals, kept = made[:2], made[2:]
-    totals = terms(ready, [*totals, *kept])
-    held = []
+    held = ready
+    if far:
+        totals, held = terms(ready, [*totals, *kept]), []
     for part in far:
         part, totals = lax.optimization_barrier((part, totals))
         following = across([part])
@@ -343,7 +336,7 @@
         held = following
     *done, loss = terms(held, [*totals, *kept], home=list(turns))
     back = [lax.ppermute(done[turn], AXES, inward(turn)) for turn in turns]
-    late = [lax.ppermute(done[turn][emb - 0:], AXES, inward_next(turn))[0:] for turn in turns]
+    late = [lax.ppermute(done[turn][emb:], AXES, inward_next(turn)) for turn in turns]
     shares = lax.all_to_all(loss, AXES, 0, 0, tiled=True)
     factor = 0.25 / (tracks * (tracks - 1) / 2.0 * (frames - 1))
     mean_loss = scaled(jnp.sum(shares, 0).reshape(1, 128), factor)
@@ -358,7 +351,6 @@
         moved = v[emb : emb + 3] + before
         before = v[emb + 3 : emb + 6]
         grad_pos = jnp.where(frame == k, moved[:, None, :], grad_pos)
-    shares, grad_emb = lax.optimization_barrier((shares, grad_emb))
     return (grad_pos, grad_emb, mean_loss[0, 0])
 
 

time: 53.4 us -> 53.4 us (level)
  no operation moved by 1% of the time
where the time goes in v7:
time: 53.4 us; the launch traced here: 53.1 us
  starting transfers between devices  22.9 us (43%)
  Pallas kernels  16.4 us (31%)
  waiting for transfers between devices  8.92 us (17%)
  other arithmetic  2.1 us (4%)
  local copies, waits for them, and re-layouts  1.89 us (4%)
  between operations  0.83 us (2%)
    pallas_call x5, Pallas kernels, pair_terms(): pl.pallas_call(functools.partial(pair_kernel, own_n, col_n, chunk, 32, fi...  15.3 us
    ppermute x4, starting transfers between devices, on_device(): lax.ppermute(sent[turn], AXES, outward(turn, shift))  8.16 us
    all_to_all x1, starting transfers between devices, on_device(): shares = lax.all_to_all(loss, AXES, 0, 0, tiled=True)  5.35 us
    ppermute x2, starting transfers between devices, on_device(): back = [lax.ppermute(done[turn], AXES, inward(turn)) for turn in turns]  4.82 us
    ppermute x4, waiting for transfers between devices, on_device(): lax.ppermute(sent[turn], AXES, outward(turn, shift))  4.07 us
    ppermute x1, waiting for transfers between devices, on_device(): lax.ppermute(rows[:, 0], 'tm', [(i, i - 1) for i in range(1, tm_n)])  2.78 us
    ppermute x2, waiting for transfers between devices, on_device(): lax.ppermute(done[turn][emb:], AXES, inward_next(turn))  2.05 us
    ppermute x1, starting transfers between devices, on_device(): lax.ppermute(rows[:, 0], 'tm', [(i, i - 1) for i in range(1, tm_n)])  1.97 us
  transfers between devices with their start and end apart: 14, of which 4 were waited for; matrix products, arithmetic and copies ran while one was open for 3% of the time, Pallas kernels for 26%

profile of v7, /device:TPU:1, one launch (start us, length us, event | category | flops | bytes accessed | tf_op | source)
XLA Modules:
  0.0 53.1 jit_solution(5820610077236647095)
XLA Ops:
  0.6 0.0 copy-start
  0.6 0.7 %copy.9 = f32[3,2,384]{2,0,1:T(4,128)S(1)} copy(f32[3,2,384]{2,1,0:T(2,128)} %param.3) | data formatting | bytes 18432 | tf_op args[0]
  1.3 0.0 copy-done
  1.4 2.0 %collective-permute-start = (f32[4,384]{1,0:T(4,128)S(1)}, f32[4,384]{1,0:T(4,128)S(1)}, u32[]{:S(2)}, u32[]{:S(2)}) collective-permute-start(f32[4,384]{1,0:T(4,128)S(1)} %fusion), channel_id=1, source_target_pairs={{1,0},{2,1},{3,2},{5,4},{6,5},{7,6},{9,8},{10,9},{11,10},{13,12},{... | collective-permute-start | bytes 18440 | tf_op jit(solution)/shard_map/ppermute | solution.py:298
  3.4 1.1 %slice_bitcast_fusion.2 = (f32[128,384]{1,0:T(8,128)S(1)}, f32[128,384]{1,0:T(8,128)S(1)}) fusion(f32[2,128,384]{2,1,0:T(8,128)} %param.4), kind=kLoop, calls=%fused_computation.3 | loop fusion | bytes 786432 | tf_op jit(solution)/shard_map/squeeze | solution.py:305
  4.5 2.8 %collective-permute-done = f32[4,384]{1,0:T(4,128)S(1)} collective-permute-done((f32[4,384]{1,0:T(4,128)S(1)}, f32[4,384]{1,0:T(4,128)S(1)}, u32[]{:S(2)}, u32[]{:S(2)}) %collective-permute-start) | collective-permute-done | bytes 6176 | tf_op jit(solution)/shard_map/ppermute | solution.py:298
  7.4 1.9 %collective-permute-start.1 = (f32[136,384]{1,0:T(8,128)S(1)}, f32[136,384]{1,0:T(8,128)S(1)}, u32[]{:S(2)}, u32[]{:S(2)}) collective-permute-start(f32[136,384]{1,0:T(8,128)S(1)} %get-tuple-element.29), channel_id=1, source_target_pairs={{0,0},{1,8},{2,2},{3,10},{4,4},{5,12},{6,6},{7,14},{8,1},{9,9},{10... | collective-permute-start | bytes 626696 | tf_op jit(solution)/shard_map/ppermute | solution.py:317
  9.3 2.7 %collective-permute-start.2 = (f32[136,384]{1,0:T(8,128)S(1)}, f32[136,384]{1,0:T(8,128)S(1)}, u32[]{:S(2)}, u32[]{:S(2)}) collective-permute-start(f32[136,384]{1,0:T(8,128)S(1)} %get-tuple-element.30), channel_id=1, source_target_pairs={{0,4},{1,12},{2,6},{3,14},{4,0},{5,8},{6,2},{7,10},{8,5},{9,13},{1... | collective-permute-start | bytes 626696 | tf_op jit(solution)/shard_map/ppermute | solution.py:317
  12.0 2.0 %collective-permute-start.4 = (f32[136,384]{1,0:T(8,128)S(1)}, f32[136,384]{1,0:T(8,128)S(1)}, u32[]{:S(2)}, u32[]{:S(2)}) collective-permute-start(f32[136,384]{1,0:T(8,128)S(1)} %get-tuple-element.29), channel_id=1, source_target_pairs={{0,16},{1,24},{2,18},{3,26},{4,20},{5,28},{6,22},{7,30},{8,17},{9,... | collective-permute-start | bytes 626696 | tf_op jit(solution)/shard_map/ppermute | solution.py:317
  14.1 1.5 %collective-permute-start.3 = (f32[136,384]{1,0:T(8,128)S(1)}, f32[136,384]{1,0:T(8,128)S(1)}, u32[]{:S(2)}, u32[]{:S(2)}) collective-permute-start(f32[136,384]{1,0:T(8,128)S(1)} %get-tuple-element.30), channel_id=1, source_target_pairs={{0,20},{1,28},{2,22},{3,30},{4,16},{5,24},{6,18},{7,26},{8,21},{9,... | collective-permute-start | bytes 626696 | tf_op jit(solution)/shard_map/ppermute | solution.py:317
  15.5 1.6 %collective-permute-done.1.refs_0_.refs_2_ = f32[136,384]{1,0:T(8,128)S(1)} collective-permute-done((f32[136,384]{1,0:T(8,128)S(1)}, f32[136,384]{1,0:T(8,128)S(1)}, u32[]{:S(2)}, u32[]{:S(2)}) %collective-permute-start.1) | collective-permute-done | bytes 208928 | tf_op jit(solution)/shard_map/ppermute | solution.py:317
  17.1 0.0 collective-permute-start.5
  17.1 2.5 %collective-permute-done.2.refs_1_.refs_3_ = f32[136,384]{1,0:T(8,128)S(1)} collective-permute-done((f32[136,384]{1,0:T(8,128)S(1)}, f32[136,384]{1,0:T(8,128)S(1)}, u32[]{:S(2)}, u32[]{:S(2)}) %collective-permute-start.2) | collective-permute-done | bytes 208928 | tf_op jit(solution)/shard_map/ppermute | solution.py:317
  19.6 0.0 collective-permute-start.6
  19.6 3.6 %shard_map.58 = (f32[128,768]{1,0:T(8,128)S(1)}, f32[24,768]{1,0:T(8,128)S(1)}, bf16[384,768]{1,0:T(8,128)(2,1)S(1)}, bf16[128,1536]{1,0:T(8,128)(2,1)S(1)}) custom-call(f32[136,384]{1,0:T(8,128)S(1)} %collective-permute-done.1.refs_0_.refs_2_, f32[136,384]{1,0:T(8,128)S(1)} %collective-permute-done.2.refs_1_.refs_3_, ...), custom_call_target="tpu_custom_call" | custom-call | flops 7549747200 | bytes 1 | tf_op jit(solution)/shard_map/pallas_call | solution.py:213
  23.2 0.0 collective-permute-done.5.refs_2_
  23.2 0.0 collective-permute-done.6.refs_3_
  23.2 3.5 %shard_map.59 = (f32[128,768]{1,0:T(8,128)S(1)}, f32[24,768]{1,0:T(8,128)S(1)}) custom-call(f32[136,384]{1,0:T(8,128)S(1)} %collective-permute-done.1.refs_0_.refs_2_, f32[136,384]{1,0:T(8,128)S(1)} %collective-permute-done.2.refs_1_.refs_3_, f32[136,384]{1,0:T(8,128)S(1)} %collective-permute-done.5.refs_2_, f32[136,384]{1,0:T(8,128)S(1)} %collective-permute-done.6.refs_3_, ...), custom_call_target="tpu_custom_call" | custom-call | flops 7549747200 | bytes 1 | tf_op jit(solution)/shard_map/pallas_call | solution.py:213
  26.8 0.0 collective-permute-done.4.refs_2_
  26.8 0.6 %collective-permute-start.8 = (f32[136,384]{1,0:T(8,128)S(1)}, f32[136,384]{1,0:T(8,128)S(1)}, u32[]{:S(2)}, u32[]{:S(2)}) collective-permute-start(f32[136,384]{1,0:T(8,128)S(1)} %collective-permute-done.4.refs_2_), channel_id=1, source_target_pairs={{0,1},{1,0},{2,3},{3,2},{4,5},{5,4},{6,7},{7,6},{8,9},{9,8},{10,11... | collective-permute-start | bytes 626696 | tf_op jit(solution)/shard_map/ppermute | solution.py:322
  27.3 2.1 %shard_map.60 = (f32[128,768]{1,0:T(8,128)S(1)}, f32[24,768]{1,0:T(8,128)S(1)}) custom-call(f32[136,384]{1,0:T(8,128)S(1)} %collective-permute-done.1.refs_0_.refs_2_, f32[136,384]{1,0:T(8,128)S(1)} %collective-permute-done.2.refs_1_.refs_3_, f32[136,384]{1,0:T(8,128)S(1)} %collective-permute-done.4.refs_2_, f32[128,768]{1,0:T(8,128)S(1)} %get-tuple-element.38.refs_3_, ...), custom_call_target="tpu_custom_call" | custom-call | flops 3774873600 | bytes 1 | tf_op jit(solution)/shard_map/pallas_call | solution.py:213
  29.4 0.0 collective-permute-done.3.refs_3_
  29.4 0.1 collective-permute-start.7
  29.5 0.0 collective-permute-done.8.refs_2_
  29.5 3.7 %shard_map.61 = (f32[128,768]{1,0:T(8,128)S(1)}, f32[24,768]{1,0:T(8,128)S(1)}) custom-call(f32[136,384]{1,0:T(8,128)S(1)} %collective-permute-done.1.refs_0_.refs_2_, f32[136,384]{1,0:T(8,128)S(1)} %collective-permute-done.2.refs_1_.refs_3_, f32[136,384]{1,0:T(8,128)S(1)} %collective-permute-done.8.refs_2_, f32[136,384]{1,0:T(8,128)S(1)} %collective-permute-done.3.refs_3_, ...), custom_call_target="tpu_custom_call" | custom-call | flops 7549747200 | bytes 1 | tf_op jit(solution)/shard_map/pallas_call | solution.py:213
  33.2 0.0 collective-permute-done.7.refs_2_
  33.2 2.4 %shard_map.62 = (f32[136,384]{1,0:T(8,128)S(1)}, f32[136,384]{1,0:T(8,128)S(1)}, f32[32,128]{1,0:T(8,128)}) custom-call(f32[136,384]{1,0:T(8,128)S(1)} %collective-permute-done.1.refs_0_.refs_2_, f32[136,384]{1,0:T(8,128)S(1)} %collective-permute-done.2.refs_1_.refs_3_, f32[136,384]{1,0:T(8,128)S(1)} %collective-permute-done.7.refs_2_, ...), custom_call_target="tpu_custom_call" | custom-call | flops 3774873600 | bytes 1 | tf_op jit(solution)/shard_map/pallas_call | solution.py:213
  35.6 5.4 %all-to-all-start = ((f32[32,1,128]{2,1,0:T(1,128)}), f32[32,1,128]{2,1,0:T(1,128)S(1)}, u32[]{:S(2)}, u32[]{:S(2)}) async-start(f32[32,1,128]{2,1,0:T(1,128)} %bitcast.8), calls=%async_computation | async-start | bytes 32768 | tf_op jit(solution)/shard_map/all_to_all | solution.py:340
  41.0 3.5 %collective-permute-start.9 = (f32[136,384]{1,0:T(8,128)S(1)}, f32[136,384]{1,0:T(8,128)S(1)}, u32[]{:S(2)}, u32[]{:S(2)}) collective-permute-start(f32[136,384]{1,0:T(8,128)S(1)} %get-tuple-element.47), channel_id=1, source_target_pairs={{0,0},{8,1},{2,2},{10,3},{4,4},{12,5},{6,6},{14,7},{1,8},{9,9},{3,... | collective-permute-start | bytes 626696 | tf_op jit(solution)/shard_map/ppermute | solution.py:338
  44.5 1.3 %collective-permute-start.10 = (f32[136,384]{1,0:T(8,128)S(1)}, f32[136,384]{1,0:T(8,128)S(1)}, u32[]{:S(2)}, u32[]{:S(2)}) collective-permute-start(f32[136,384]{1,0:T(8,128)S(1)} %get-tuple-element.48), channel_id=1, source_target_pairs={{4,0},{12,1},{6,2},{14,3},{0,4},{8,5},{2,6},{10,7},{5,8},{13,9},{7... | collective-permute-start | bytes 626696 | tf_op jit(solution)/shard_map/ppermute | solution.py:338
  45.8 0.7 %collective-permute-start.11 = (f32[8,384]{1,0:T(8,128)S(1)}, f32[8,384]{1,0:T(8,128)S(1)}, u32[]{:S(2)}, u32[]{:S(2)}) collective-permute-start(f32[8,384]{1,0:T(8,128)S(1)} %slice.70), channel_id=1, source_target_pairs={{4,5},{12,6},{6,7},{5,13},{13,14},{7,15},{20,21},{28,22},{22,23},{... | collective-permute-start | bytes 36872 | tf_op jit(solution)/shard_map/ppermute | solution.py:339
  46.5 1.3 %collective-permute-start.12 = (f32[8,384]{1,0:T(8,128)S(1)}, f32[8,384]{1,0:T(8,128)S(1)}, u32[]{:S(2)}, u32[]{:S(2)}) collective-permute-start(f32[8,384]{1,0:T(8,128)S(1)} %slice.71), channel_id=1, source_target_pairs={{4,1},{12,2},{6,3},{5,9},{13,10},{7,11},{20,17},{28,18},{22,19},{2... | collective-permute-start | bytes 36872 | tf_op jit(solution)/shard_map/ppermute | solution.py:339
  47.8 0.0 all-to-all-done
  47.8 0.6 %reduce_sum.9 = f32[128]{0:T(128)} reduce(f32[32,1,128]{2,1,0:T(1,128)S(1)} %all-to-all-done, f32[]{:T(128)} %constant.31.clone.1), dimensions={0,1}, to_apply=%region_0.1 | reduce | flops 3968 | bytes 16900 | tf_op jit(solution)/shard_map/reduce_sum | solution.py:342
  48.3 1.2 %shard_map.63 = f32[1,128]{1,0:T(1,128)} custom-call(f32[1,128]{1,0:T(1,128)} %bitcast.32), custom_call_target="tpu_custom_call" | custom-call | flops 99999997952 | bytes 1 | tf_op jit(solution)/shard_map/pallas_call | solution.py:244
  49.5 0.0 collective-permute-done.11
  49.5 2.1 %collective-permute-done.12 = f32[8,384]{1,0:T(8,128)S(1)} collective-permute-done((f32[8,384]{1,0:T(8,128)S(1)}, f32[8,384]{1,0:T(8,128)S(1)}, u32[]{:S(2)}, u32[]{:S(2)}) %collective-permute-start.12) | collective-permute-done | bytes 12320 | tf_op jit(solution)/shard_map/ppermute | solution.py:339
  51.5 0.0 collective-permute-done.10
  51.6 0.0 collective-permute-done.9
  51.6 0.8 %pad_maximum_fusion = f32[2,128,384]{2,1,0:T(8,128)} fusion(f32[1,128,384]{2,1,0:T(8,128)S(1)} %get-tuple-element.67, f32[1,128,384]{2,1,0:T(8,128)S(1)} %get-tuple-element.68), kind=kLoop, calls=%fused_computation | loop fusion | flops 98304 | bytes 786432 | tf_op jit(solution)/shard_map/stack | solution.py:347
  52.4 0.7 %select_select_fusion = f32[3,2,384]{2,1,0:T(2,128)} fusion(pred[2]{0:T(512)(128)(4,1)S(1)} %get-tuple-element.70, pred[2]{0:T(512)(128)(4,1)S(1)} %get-tuple-element.69, f32[3,384]{1,0:T(4,128)S(1)} %get-tuple-element.62, f32[3,384]{1,0:T(4,128)S(1)} %get-tuple-element.61), kind=kLoop, calls=%fused_computation.9 | loop fusion | flops 4608 | bytes 18436 | tf_op jit(solution)/shard_map/jit(_where)/select_n | solution.py:353
  (15 shorter events, 0.2 us)
Async XLA Ops:
  0.6 0.7 %copy-start = (s32[2,384]{1,0:T(2,128)S(1)}, s32[2,384]{1,0:T(2,128)}, u32[]{:S(2)}) copy-start(s32[2,384]{1,0:T(2,128)} %param.5) | copy-start | bytes 9220
  1.4 5.8 %collective-permute-start = (f32[4,384]{1,0:T(4,128)S(1)}, f32[4,384]{1,0:T(4,128)S(1)}, u32[]{:S(2)}, u32[]{:S(2)}) collective-permute-start(f32[4,384]{1,0:T(4,128)S(1)} %fusion), channel_id=1, source_target_pairs={{1,0},{2,1},{3,2},{5,4},{6,5},{7,6},{9,8},{10,9},{11,10},{13,12},{... | collective-permute-start | bytes 18440 | tf_op jit(solution)/shard_map/ppermute | solution.py:298
  7.4 9.8 %collective-permute-start.1 = (f32[136,384]{1,0:T(8,128)S(1)}, f32[136,384]{1,0:T(8,128)S(1)}, u32[]{:S(2)}, u32[]{:S(2)}) collective-permute-start(f32[136,384]{1,0:T(8,128)S(1)} %get-tuple-element.29), channel_id=1, source_target_pairs={{0,0},{1,8},{2,2},{3,10},{4,4},{5,12},{6,6},{7,14},{8,1},{9,9},{10... | collective-permute-start | bytes 626696 | tf_op jit(solution)/shard_map/ppermute | solution.py:317
  9.3 10.3 %collective-permute-start.2 = (f32[136,384]{1,0:T(8,128)S(1)}, f32[136,384]{1,0:T(8,128)S(1)}, u32[]{:S(2)}, u32[]{:S(2)}) collective-permute-start(f32[136,384]{1,0:T(8,128)S(1)} %get-tuple-element.30), channel_id=1, source_target_pairs={{0,4},{1,12},{2,6},{3,14},{4,0},{5,8},{6,2},{7,10},{8,5},{9,13},{1... | collective-permute-start | bytes 626696 | tf_op jit(solution)/shard_map/ppermute | solution.py:317
  12.0 14.7 %collective-permute-start.4 = (f32[136,384]{1,0:T(8,128)S(1)}, f32[136,384]{1,0:T(8,128)S(1)}, u32[]{:S(2)}, u32[]{:S(2)}) collective-permute-start(f32[136,384]{1,0:T(8,128)S(1)} %get-tuple-element.29), channel_id=1, source_target_pairs={{0,16},{1,24},{2,18},{3,26},{4,20},{5,28},{6,22},{7,30},{8,17},{9,... | collective-permute-start | bytes 626696 | tf_op jit(solution)/shard_map/ppermute | solution.py:317
  14.1 15.4 %collective-permute-start.3 = (f32[136,384]{1,0:T(8,128)S(1)}, f32[136,384]{1,0:T(8,128)S(1)}, u32[]{:S(2)}, u32[]{:S(2)}) collective-permute-start(f32[136,384]{1,0:T(8,128)S(1)} %get-tuple-element.30), channel_id=1, source_target_pairs={{0,20},{1,28},{2,22},{3,30},{4,16},{5,24},{6,18},{7,26},{8,21},{9,... | collective-permute-start | bytes 626696 | tf_op jit(solution)/shard_map/ppermute | solution.py:317
  17.1 6.1 %collective-permute-start.5 = (f32[136,384]{1,0:T(8,128)S(1)}, f32[136,384]{1,0:T(8,128)S(1)}, u32[]{:S(2)}, u32[]{:S(2)}) collective-permute-start(f32[136,384]{1,0:T(8,128)S(1)} %collective-permute-done.1.refs_0_.refs_2_), channel_id=1, source_target_pairs={{0,1},{1,0},{2,3},{3,2},{4,5},{5,4},{6,7},{7,6},{8,9},{9,8},{10,11... | collective-permute-start | bytes 626696 | tf_op jit(solution)/shard_map/ppermute | solution.py:322
  19.6 3.6 %collective-permute-start.6 = (f32[136,384]{1,0:T(8,128)S(1)}, f32[136,384]{1,0:T(8,128)S(1)}, u32[]{:S(2)}, u32[]{:S(2)}) collective-permute-start(f32[136,384]{1,0:T(8,128)S(1)} %collective-permute-done.2.refs_1_.refs_3_), channel_id=1, source_target_pairs={{0,1},{1,0},{2,3},{3,2},{4,5},{5,4},{6,7},{7,6},{8,9},{9,8},{10,11... | collective-permute-start | bytes 626696 | tf_op jit(solution)/shard_map/ppermute | solution.py:322
  26.8 2.7 %collective-permute-start.8 = (f32[136,384]{1,0:T(8,128)S(1)}, f32[136,384]{1,0:T(8,128)S(1)}, u32[]{:S(2)}, u32[]{:S(2)}) collective-permute-start(f32[136,384]{1,0:T(8,128)S(1)} %collective-permute-done.4.refs_2_), channel_id=1, source_target_pairs={{0,1},{1,0},{2,3},{3,2},{4,5},{5,4},{6,7},{7,6},{8,9},{9,8},{10,11... | collective-permute-start | bytes 626696 | tf_op jit(solution)/shard_map/ppermute | solution.py:322
  29.4 3.8 %collective-permute-start.7 = (f32[136,384]{1,0:T(8,128)S(1)}, f32[136,384]{1,0:T(8,128)S(1)}, u32[]{:S(2)}, u32[]{:S(2)}) collective-permute-start(f32[136,384]{1,0:T(8,128)S(1)} %collective-permute-done.3.refs_3_), channel_id=1, source_target_pairs={{0,1},{1,0},{2,3},{3,2},{4,5},{5,4},{6,7},{7,6},{8,9},{9,8},{10,11... | collective-permute-start | bytes 626696 | tf_op jit(solution)/shard_map/ppermute | solution.py:322
  35.6 12.2 %all-to-all-start = ((f32[32,1,128]{2,1,0:T(1,128)}), f32[32,1,128]{2,1,0:T(1,128)S(1)}, u32[]{:S(2)}, u32[]{:S(2)}) async-start(f32[32,1,128]{2,1,0:T(1,128)} %bitcast.8), calls=%async_computation | async-start | bytes 32768 | tf_op jit(solution)/shard_map/all_to_all | solution.py:340
  41.0 10.6 %collective-permute-start.9 = (f32[136,384]{1,0:T(8,128)S(1)}, f32[136,384]{1,0:T(8,128)S(1)}, u32[]{:S(2)}, u32[]{:S(2)}) collective-permute-start(f32[136,384]{1,0:T(8,128)S(1)} %get-tuple-element.47), channel_id=1, source_target_pairs={{0,0},{8,1},{2,2},{10,3},{4,4},{12,5},{6,6},{14,7},{1,8},{9,9},{3,... | collective-permute-start | bytes 626696 | tf_op jit(solution)/shard_map/ppermute | solution.py:338
  44.5 7.0 %collective-permute-start.10 = (f32[136,384]{1,0:T(8,128)S(1)}, f32[136,384]{1,0:T(8,128)S(1)}, u32[]{:S(2)}, u32[]{:S(2)}) collective-permute-start(f32[136,384]{1,0:T(8,128)S(1)} %get-tuple-element.48), channel_id=1, source_target_pairs={{4,0},{12,1},{6,2},{14,3},{0,4},{8,5},{2,6},{10,7},{5,8},{13,9},{7... | collective-permute-start | bytes 626696 | tf_op jit(solution)/shard_map/ppermute | solution.py:338
  45.8 3.7 %collective-permute-start.11 = (f32[8,384]{1,0:T(8,128)S(1)}, f32[8,384]{1,0:T(8,128)S(1)}, u32[]{:S(2)}, u32[]{:S(2)}) collective-permute-start(f32[8,384]{1,0:T(8,128)S(1)} %slice.70), channel_id=1, source_target_pairs={{4,5},{12,6},{6,7},{5,13},{13,14},{7,15},{20,21},{28,22},{22,23},{... | collective-permute-start | bytes 36872 | tf_op jit(solution)/shard_map/ppermute | solution.py:339
  46.5 5.1 %collective-permute-start.12 = (f32[8,384]{1,0:T(8,128)S(1)}, f32[8,384]{1,0:T(8,128)S(1)}, u32[]{:S(2)}, u32[]{:S(2)}) collective-permute-start(f32[8,384]{1,0:T(8,128)S(1)} %slice.71), channel_id=1, source_target_pairs={{4,1},{12,2},{6,3},{5,9},{13,10},{7,11},{20,17},{28,18},{22,19},{2... | collective-permute-start | bytes 36872 | tf_op jit(solution)/shard_map/ppermute | solution.py:339
